TPU v7x, 32 devices: a whole 2x2x4 slice. The times are simulated.
32 devices in a mesh: fsdp: 32 (over z, y, x, core).
Axes of the slice: x: 2, y: 2, z: 4, core: 2. Of those that a mesh axis runs over, the one named last changes fastest.
Arguments:
- tokens: bfloat16 [2048, 32, 128], P('fsdp'), may hold values from -6 to 6
- features: bfloat16 [2048, 2, 49, 128], P('fsdp'), may hold values from -6 to 6
- proprio: bfloat16 [2048, 2, 32], P('fsdp'), may hold values from -6 to 6
- embodiment: int32 [2048], P('fsdp'), may hold values from 0 to 31
- trunk_attn: bfloat16 [2, 512, 128], P(None, 'fsdp')
- feedforward_up_weight: bfloat16 [2, 512, 128], P(None, 'fsdp'), may hold values from -0.5 to 0.5
- mlp_down: bfloat16 [2, 512, 128], P(None, 'fsdp'), may hold values from -0.25 to 0.25
- stem_mats: bfloat16 [2, 4096, 512], P(None, 'fsdp')
- stem_queries: bfloat16 [2, 512, 128], P(None, 'fsdp'), may hold values from -6 to 6
- prop_in: bfloat16 [2, 1024, 128], P(None, 'fsdp'), may hold values from -1 to 1
- trunk_vectors: bfloat16 [2, 8, 128], replicated
- mlp_bias: bfloat16 [2, 512], replicated, may hold values from -2 to 2
- stem_bias: bfloat16 [2, 32, 2, 128], replicated, may hold values from -2 to 2
- cotangent: bfloat16 [2048, 32, 128], P('fsdp'), may hold values from -6 to 6
Outputs:
- out_tokens: bfloat16 [2048, 32, 128], P('fsdp')
- grad_tokens: float32 [2048, 32, 128], P('fsdp')
- grad_features: float32 [2048, 2, 49, 128], P('fsdp')
- grad_proprio: float32 [2048, 2, 32], P('fsdp')
- grad_trunk_attn: float32 [2, 512, 128], P(None, 'fsdp')
- grad_mlp_up: float32 [2, 512, 128], P(None, 'fsdp')
- grad_mlp_down: float32 [2, 512, 128], P(None, 'fsdp')
- grad_stem_mats: float32 [2, 4096, 512], P(None, 'fsdp')
- grad_stem_queries: float32 [2, 512, 128], P(None, 'fsdp')
- grad_prop_in: float32 [2, 1024, 128], P(None, 'fsdp')
- grad_trunk_vectors: float32 [2, 8, 128], replicated
- grad_mlp_bias: float32 [2, 512], replicated
- grad_stem_bias: float32 [2, 32, 2, 128], replicated
All inputs are finite; a program needn't handle non-finite values.
Results may differ from a plain program's by a relative error of at most 0.019.
Values may be sent and summed in bfloat16 or wider, within the bound.
A program may use at most 256 MiB of HBM per device.

v0:
```python
import math

import jax
import jax.numpy as jnp
from jax import lax
from jax.sharding import PartitionSpec as P

D = 128
HEADS = 8
HD = 16
SQ = 16
PROP = 32
STEMS = 32
STEPS = 2
LAYERS = 2


def layer_norm(values, gain_row, offset_row_vector):
    centred = values - jnp.mean(values, -1, keepdims=True)
    inverse = lax.rsqrt(jnp.mean(centred * centred, -1, keepdims=True) + 1e-05)
    return centred * inverse * gain_row + offset_row_vector


def gelu_exact(values):
    return jax.nn.gelu(values, approximate=False)


def stem_tables(weights, embodiment):
    stem_w = weights[3]
    query_w = weights[4]
    pin_w = weights[5]
    per_stem = jnp.take(stem_w.reshape(STEMS, D, 4 * D), embodiment, axis=0)
    queries = jnp.take(query_w.reshape(STEMS, SQ, D), embodiment, axis=0)
    per_input = jnp.take(pin_w.reshape(STEMS, PROP, D), embodiment, axis=0)
    return (per_stem, queries, per_input)


def layer_forward(hidden, features, proprio, embodiment, weights, vectors, mlp_b, stem_b):
    attn_w = weights[0]
    up_w = weights[1]
    down_w = weights[2]
    sample_count = embodiment.shape[0]
    tok_rows = hidden.shape[0] // sample_count
    context_rows = features.shape[2] + 1
    score_scale = 1.0 / math.sqrt(HD)
    per_stem, queries, per_input = stem_tables(weights, embodiment)
    per_bias = jnp.take(stem_b, embodiment, axis=0)
    prop_pre = (
        jnp.einsum("stp,spd->std", proprio, per_input, preferred_element_type=jnp.float32)
        + per_bias[:, 0][:, None, :]
    )
    prop_act = gelu_exact(prop_pre).astype(jnp.bfloat16)
    prop_row = (
        jnp.einsum(
            "std,sde->ste", prop_act, per_stem[:, :, 3 * D :], preferred_element_type=jnp.float32
        )
        + per_bias[:, 1][:, None, :]
    )
    context = jnp.concatenate([features, prop_row.astype(jnp.bfloat16)[:, :, None, :]], axis=2)
    stem_kv = jnp.einsum(
        "stcd,sde->stce", context, per_stem[:, :, : 2 * D], preferred_element_type=jnp.float32
    ).astype(jnp.bfloat16)
    key_heads = stem_kv[..., :D].reshape(sample_count, STEPS, context_rows, HEADS, HD)
    val_heads = stem_kv[..., D:].reshape(sample_count, STEPS, context_rows, HEADS, HD)
    query_heads = queries.reshape(sample_count, SQ, HEADS, HD)
    stem_score = (
        jnp.einsum("sqhe,stche->sthqc", query_heads, key_heads, preferred_element_type=jnp.float32)
        * score_scale
    )
    stem_prob = jax.nn.softmax(stem_score, axis=-1)
    stem_low = stem_prob.astype(jnp.bfloat16)
    stem_mix = (
        jnp.einsum("sthqc,stche->stqhe", stem_low, val_heads, preferred_element_type=jnp.float32)
        .reshape(sample_count, STEPS, SQ, D)
        .astype(jnp.bfloat16)
    )
    stem_out = jnp.einsum(
        "stqd,sde->stqe",
        stem_mix,
        per_stem[:, :, 2 * D : 3 * D],
        preferred_element_type=jnp.float32,
    )
    first_sum = hidden + stem_out.reshape(sample_count * tok_rows, D)
    normed = layer_norm(first_sum, vectors[0], vectors[1]).astype(jnp.bfloat16)
    qkv_raw = jnp.einsum(
        "rd,jde->jre", normed, attn_w[: 3 * D].reshape(3, D, D), preferred_element_type=jnp.float32
    )
    qkv_bias = jnp.stack([vectors[2], jnp.zeros_like(vectors[2]), vectors[3]])
    qkv_low = (qkv_raw + qkv_bias[:, None, :]).astype(jnp.bfloat16)
    head_shape = (sample_count, tok_rows, HEADS, HD)
    self_score = (
        jnp.einsum(
            "sqhe,skhe->shqk",
            qkv_low[0].reshape(head_shape),
            qkv_low[1].reshape(head_shape),
            preferred_element_type=jnp.float32,
        )
        * score_scale
    )
    self_prob = jax.nn.softmax(self_score, axis=-1)
    self_low = self_prob.astype(jnp.bfloat16)
    self_mix = (
        jnp.einsum(
            "shqk,skhe->sqhe",
            self_low,
            qkv_low[2].reshape(head_shape),
            preferred_element_type=jnp.float32,
        )
        .reshape(-1, D)
        .astype(jnp.bfloat16)
    )
    attn_out = jnp.dot(self_mix, attn_w[3 * D :], preferred_element_type=jnp.float32) + vectors[4]
    second_sum = first_sum + attn_out
    mlp_in = layer_norm(second_sum, vectors[5], vectors[6]).astype(jnp.bfloat16)
    mlp_pre = jnp.einsum("rd,fd->rf", mlp_in, up_w, preferred_element_type=jnp.float32) + mlp_b
    mlp_act = gelu_exact(mlp_pre).astype(jnp.bfloat16)
    result = second_sum + (
        jnp.dot(mlp_act, down_w, preferred_element_type=jnp.float32) + vectors[7]
    )
    saved_acts = (
        first_sum,
        second_sum,
        prop_pre,
        prop_act,
        context,
        stem_kv,
        stem_prob,
        stem_low,
        stem_mix,
        normed,
        qkv_low,
        self_prob,
        self_low,
        self_mix,
        mlp_in,
        mlp_pre,
        mlp_act,
    )
    return (result, saved_acts)


def layer_backward(grad_rows, proprio, embodiment, weights, vectors, saved_acts):
    attn_w = weights[0]
    up_w = weights[1]
    down_w = weights[2]
    (
        first_sum,
        second_sum,
        prop_pre,
        prop_act,
        context,
        stem_kv,
        stem_prob,
        stem_low,
        stem_mix,
        normed,
        qkv_low,
        self_prob,
        self_low,
        self_mix,
        mlp_in,
        mlp_pre,
        mlp_act,
    ) = saved_acts
    sample_count = embodiment.shape[0]
    tok_rows = grad_rows.shape[0] // sample_count
    context_rows = context.shape[2]
    score_scale = 1.0 / math.sqrt(HD)
    per_stem, queries, per_input = stem_tables(weights, embodiment)
    head_shape = (sample_count, tok_rows, HEADS, HD)
    out_low = grad_rows.astype(jnp.bfloat16)
    grad_b2 = jnp.sum(out_low.astype(jnp.float32), 0)
    grad_down = jnp.einsum("rf,rd->fd", mlp_act, out_low, preferred_element_type=jnp.float32)
    grad_act = jnp.einsum("rd,fd->rf", out_low, down_w, preferred_element_type=jnp.float32)
    gelu_back = jax.vjp(gelu_exact, mlp_pre)[1]
    grad_pre = gelu_back(grad_act)[0].astype(jnp.bfloat16)
    grad_mbias = jnp.sum(grad_pre.astype(jnp.float32), 0)
    grad_up = jnp.einsum("rf,rd->fd", grad_pre, mlp_in, preferred_element_type=jnp.float32)
    grad_in = jnp.einsum("rf,fd->rd", grad_pre, up_w, preferred_element_type=jnp.float32)
    norm_second = jax.vjp(layer_norm, second_sum, vectors[5], vectors[6])[1]
    grad_second, grad_gain2, grad_shift2 = norm_second(grad_in)
    grad_second = grad_rows + grad_second
    branch_low = grad_second.astype(jnp.bfloat16)
    grad_bout = jnp.sum(branch_low.astype(jnp.float32), 0)
    grad_wout = jnp.einsum("rd,re->de", self_mix, branch_low, preferred_element_type=jnp.float32)
    grad_mix = (
        jnp.einsum("re,de->rd", branch_low, attn_w[3 * D :], preferred_element_type=jnp.float32)
        .astype(jnp.bfloat16)
        .reshape(head_shape)
    )
    query_h = qkv_low[0].reshape(head_shape)
    key_h = qkv_low[1].reshape(head_shape)
    value_h = qkv_low[2].reshape(head_shape)
    grad_prob = jnp.einsum("sqhe,skhe->shqk", grad_mix, value_h, preferred_element_type=jnp.float32)
    grad_value = jnp.einsum(
        "shqk,sqhe->skhe", self_low, grad_mix, preferred_element_type=jnp.float32
    )
    grad_score = (
        self_prob * (grad_prob - jnp.sum(grad_prob * self_prob, -1, keepdims=True))
    ).astype(jnp.bfloat16)
    grad_query = (
        jnp.einsum("shqk,skhe->sqhe", grad_score, key_h, preferred_element_type=jnp.float32)
        * score_scale
    )
    grad_key = (
        jnp.einsum("shqk,sqhe->skhe", grad_score, query_h, preferred_element_type=jnp.float32)
        * score_scale
    )
    grad_qkv = jnp.stack([grad_query, grad_key, grad_value]).reshape(3, -1, D).astype(jnp.bfloat16)
    grad_wqkv = jnp.einsum(
        "rd,jre->jde", normed, grad_qkv, preferred_element_type=jnp.float32
    ).reshape(3 * D, D)
    grad_normed = jnp.einsum(
        "jre,jde->rd",
        grad_qkv,
        attn_w[: 3 * D].reshape(3, D, D),
        preferred_element_type=jnp.float32,
    )
    grad_bquery = jnp.sum(grad_qkv[0].astype(jnp.float32), 0)
    grad_bvalue = jnp.sum(grad_qkv[2].astype(jnp.float32), 0)
    norm_first = jax.vjp(layer_norm, first_sum, vectors[0], vectors[1])[1]
    grad_first, grad_gain1, grad_shift1 = norm_first(grad_normed)
    grad_first = grad_second + grad_first
    stem_grad = grad_first.reshape(sample_count, STEPS, SQ, D).astype(jnp.bfloat16)
    grad_wo_each = jnp.einsum(
        "stqd,stqe->sde", stem_mix, stem_grad, preferred_element_type=jnp.float32
    )
    grad_smix = (
        jnp.einsum(
            "stqe,sde->stqd",
            stem_grad,
            per_stem[:, :, 2 * D : 3 * D],
            preferred_element_type=jnp.float32,
        )
        .astype(jnp.bfloat16)
        .reshape(sample_count, STEPS, SQ, HEADS, HD)
    )
    key_heads = stem_kv[..., :D].reshape(sample_count, STEPS, context_rows, HEADS, HD)
    val_heads = stem_kv[..., D:].reshape(sample_count, STEPS, context_rows, HEADS, HD)
    query_heads = queries.reshape(sample_count, SQ, HEADS, HD)
    grad_sprob = jnp.einsum(
        "stqhe,stche->sthqc", grad_smix, val_heads, preferred_element_type=jnp.float32
    )
    stem_value_gradient = jnp.einsum(
        "sthqc,stqhe->stche", stem_low, grad_smix, preferred_element_type=jnp.float32
    )
    grad_sscore = (
        stem_prob * (grad_sprob - jnp.sum(grad_sprob * stem_prob, -1, keepdims=True))
    ).astype(jnp.bfloat16)
    grad_squery = (
        jnp.einsum("sthqc,stche->sqhe", grad_sscore, key_heads, preferred_element_type=jnp.float32)
        * score_scale
    )
    stem_key_gradient = (
        jnp.einsum(
            "sthqc,sqhe->stche", grad_sscore, query_heads, preferred_element_type=jnp.float32
        )
        * score_scale
    )
    key_value_shape = (sample_count, STEPS, context_rows, D)
    grad_kv = jnp.concatenate(
        [stem_key_gradient.reshape(key_value_shape), stem_value_gradient.reshape(key_value_shape)],
        -1,
    ).astype(jnp.bfloat16)
    grad_wkv_each = jnp.einsum(
        "stcd,stce->sde", context, grad_kv, preferred_element_type=jnp.float32
    )
    grad_context = jnp.einsum(
        "stce,sde->stcd", grad_kv, per_stem[:, :, : 2 * D], preferred_element_type=jnp.float32
    ).astype(jnp.bfloat16)
    grad_feat = grad_context[:, :, :-1].astype(jnp.float32)
    grad_prow = grad_context[:, :, -1]
    grad_wp_each = jnp.einsum(
        "std,ste->sde", prop_act, grad_prow, preferred_element_type=jnp.float32
    )
    grad_pact = jnp.einsum(
        "ste,sde->std", grad_prow, per_stem[:, :, 3 * D :], preferred_element_type=jnp.float32
    )
    prop_gelu_back = jax.vjp(gelu_exact, prop_pre)[1]
    grad_ppre = prop_gelu_back(grad_pact)[0].astype(jnp.bfloat16)
    grad_pin_each = jnp.einsum(
        "stp,std->spd", proprio, grad_ppre, preferred_element_type=jnp.float32
    )
    grad_prop = jnp.einsum("std,spd->stp", grad_ppre, per_input, preferred_element_type=jnp.float32)
    grad_each = jnp.concatenate([grad_wkv_each, grad_wo_each, grad_wp_each], -1)
    grad_stem = jax.ops.segment_sum(grad_each, embodiment, num_segments=STEMS).reshape(
        STEMS * D, 4 * D
    )
    grad_qw = jax.ops.segment_sum(
        grad_squery.reshape(sample_count, SQ, D), embodiment, num_segments=STEMS
    ).reshape(STEMS * SQ, D)
    grad_pin = jax.ops.segment_sum(grad_pin_each, embodiment, num_segments=STEMS).reshape(
        STEMS * PROP, D
    )
    bias_terms = jnp.stack(
        [jnp.sum(grad_ppre.astype(jnp.float32), 1), jnp.sum(grad_prow.astype(jnp.float32), 1)], 1
    )
    stem_bias_gradient = jax.ops.segment_sum(bias_terms, embodiment, num_segments=STEMS)
    matrices = (
        jnp.concatenate([grad_wqkv, grad_wout], 0),
        grad_up,
        grad_down,
        grad_stem,
        grad_qw,
        grad_pin,
    )
    vector_grad = jnp.stack(
        [
            grad_gain1,
            grad_shift1,
            grad_bquery,
            grad_bvalue,
            grad_bout,
            grad_gain2,
            grad_shift2,
            grad_b2,
        ]
    )
    return (grad_first, grad_feat, grad_prop, matrices, vector_grad, grad_mbias, stem_bias_gradient)


def body(
    tokens,
    features,
    proprio,
    embodiment,
    trunk_attn,
    feedforward_up_weight,
    mlp_down,
    stem_mats,
    stem_queries,
    prop_in,
    trunk_vectors,
    mlp_bias,
    stem_bias,
    cotangent,
):
    vectors_all = trunk_vectors.astype(jnp.float32)
    mbias_all = mlp_bias.astype(jnp.float32)
    sbias_all = stem_bias.astype(jnp.float32)
    hidden = tokens.astype(jnp.float32).reshape(-1, D)
    kept_weights = []
    saved_all = []
    for layer_index in range(LAYERS):
        shards = (
            trunk_attn[layer_index],
            feedforward_up_weight[layer_index],
            mlp_down[layer_index],
            stem_mats[layer_index],
            stem_queries[layer_index],
            prop_in[layer_index],
        )
        weights = (
            lax.all_gather(shards[0], "fsdp", axis=0, tiled=True),
            lax.all_gather(shards[1], "fsdp", axis=0, tiled=True),
            lax.all_gather(shards[2], "fsdp", axis=0, tiled=True),
            lax.all_gather(shards[3], "fsdp", axis=0, tiled=True),
            lax.all_gather(shards[4], "fsdp", axis=0, tiled=True),
            lax.all_gather(shards[5], "fsdp", axis=0, tiled=True),
        )
        hidden, saved_acts = layer_forward(
            hidden,
            features,
            proprio,
            embodiment,
            weights,
            vectors_all[layer_index],
            mbias_all[layer_index],
            sbias_all[layer_index],
        )
        kept_weights.append(weights)
        saved_all.append(saved_acts)
    out_tokens = hidden.reshape(tokens.shape).astype(jnp.bfloat16)
    grad_rows = cotangent.astype(jnp.float32).reshape(-1, D)
    grad_feat_total = jnp.zeros(features.shape, jnp.float32)
    grad_prop_total = jnp.zeros(proprio.shape, jnp.float32)
    local_grads = [None] * LAYERS
    shard_grads = [None] * LAYERS
    vector_list = [None] * LAYERS
    mbias_list = [None] * LAYERS
    sbias_list = [None] * LAYERS
    for layer_index in reversed(range(LAYERS)):
        shards = (
            trunk_attn[layer_index],
            feedforward_up_weight[layer_index],
            mlp_down[layer_index],
            stem_mats[layer_index],
            stem_queries[layer_index],
            prop_in[layer_index],
        )
        weights = (
            lax.all_gather(shards[0], "fsdp", axis=0, tiled=True),
            lax.all_gather(shards[1], "fsdp", axis=0, tiled=True),
            lax.all_gather(shards[2], "fsdp", axis=0, tiled=True),
            lax.all_gather(shards[3], "fsdp", axis=0, tiled=True),
            lax.all_gather(shards[4], "fsdp", axis=0, tiled=True),
            lax.all_gather(shards[5], "fsdp", axis=0, tiled=True),
        )
        grad_rows, grad_feat, grad_prop, matrices, vector_grad, grad_mbias, stem_bias_gradient = (
            layer_backward(
                grad_rows,
                proprio,
                embodiment,
                weights,
                vectors_all[layer_index],
                saved_all[layer_index],
            )
        )
        grad_feat_total = grad_feat_total + grad_feat
        grad_prop_total = grad_prop_total + grad_prop
        local_grads[layer_index] = matrices
        shard_grads[layer_index] = (
            lax.psum_scatter(matrices[0], "fsdp", scatter_dimension=0, tiled=True),
            lax.psum_scatter(matrices[1], "fsdp", scatter_dimension=0, tiled=True),
            lax.psum_scatter(matrices[2], "fsdp", scatter_dimension=0, tiled=True),
            lax.psum_scatter(matrices[3], "fsdp", scatter_dimension=0, tiled=True),
            lax.psum_scatter(matrices[4], "fsdp", scatter_dimension=0, tiled=True),
            lax.psum_scatter(matrices[5], "fsdp", scatter_dimension=0, tiled=True),
        )
        vector_list[layer_index] = vector_grad
        mbias_list[layer_index] = grad_mbias
        sbias_list[layer_index] = stem_bias_gradient
    summed_vectors, summed_mbias, summed_sbias = lax.psum(
        (jnp.stack(vector_list), jnp.stack(mbias_list), jnp.stack(sbias_list)), "fsdp"
    )
    stacked = [
        jnp.stack([shard_grads[layer_index][member] for layer_index in range(LAYERS)])
        for member in range(6)
    ]
    grad_tokens = grad_rows.reshape(tokens.shape)
    return (
        out_tokens,
        grad_tokens,
        grad_feat_total,
        grad_prop_total,
        stacked[0],
        stacked[1],
        stacked[2],
        stacked[3],
        stacked[4],
        stacked[5],
        summed_vectors,
        summed_mbias,
        summed_sbias,
    )


def solution(mesh):
    return jax.shard_map(
        body,
        mesh=mesh,
        in_specs=(
            P("fsdp", None, None),
            P("fsdp", None, None, None),
            P("fsdp", None, None),
            P("fsdp"),
            P(None, "fsdp", None),
            P(None, "fsdp", None),
            P(None, "fsdp", None),
            P(None, "fsdp", None),
            P(None, "fsdp", None),
            P(None, "fsdp", None),
            P(),
            P(),
            P(),
            P("fsdp", None, None),
        ),
        out_specs=(
            P("fsdp", None, None),
            P("fsdp", None, None),
            P("fsdp", None, None, None),
            P("fsdp", None, None),
            P(None, "fsdp", None),
            P(None, "fsdp", None),
            P(None, "fsdp", None),
            P(None, "fsdp", None),
            P(None, "fsdp", None),
            P(None, "fsdp", None),
            P(),
            P(),
            P(),
        ),
        check_vma=False,
    )
```

profile of v0, /device:TPU:0, one launch (start us, length us, event | category | flops | bytes accessed | tf_op | source)
XLA Modules:
  0.0 2711.9 jit_solution(17822703056896190177)
XLA Ops:
  15.9 44.3 %all-gather.6 = bf16[1,1024,128]{2,1,0:T(8,128)(2,1)S(1)} all-gather(bf16[1,32,128]{2,1,0:T(8,128)(2,1)S(1)} %get-tuple-element.124), channel_id=8, replica_groups=mesh['fsdp'=32] {'fsdp'}, dimensions={1}, use_global_device_ids=true | all-gather | bytes 270336 | tf_op jit(solution)/shard_map/all_gather | solution.py:359
  62.8 37.5 %all-gather.2 = bf16[1,512,128]{2,1,0:T(8,128)(2,1)S(1)} all-gather(bf16[1,16,128]{2,1,0:T(8,128)(2,1)S(1)} %get-tuple-element.147), channel_id=4, replica_groups=mesh['fsdp'=32] {'fsdp'}, dimensions={1}, use_global_device_ids=true | all-gather | bytes 135168 | tf_op jit(solution)/shard_map/all_gather | solution.py:358
  101.0 38.2 %all-gather.8 = bf16[1,512,128]{2,1,0:T(8,128)(2,1)S(1)} all-gather(bf16[1,16,128]{2,1,0:T(8,128)(2,1)S(1)} %get-tuple-element.148), channel_id=10, replica_groups=mesh['fsdp'=32] {'fsdp'}, dimensions={1}, use_global_device_ids=true | all-gather | bytes 135168 | tf_op jit(solution)/shard_map/all_gather | solution.py:358
  141.7 37.9 %all-gather = bf16[1,1024,128]{2,1,0:T(8,128)(2,1)S(1)} all-gather(bf16[1,32,128]{2,1,0:T(8,128)(2,1)S(1)} %get-tuple-element.123), channel_id=2, replica_groups=mesh['fsdp'=32] {'fsdp'}, dimensions={1}, use_global_device_ids=true | all-gather | bytes 270336 | tf_op jit(solution)/shard_map/all_gather | solution.py:359
  182.8 37.8 %all-gather.3 = bf16[1,512,128]{2,1,0:T(8,128)(2,1)S(1)} all-gather(bf16[1,16,128]{2,1,0:T(8,128)(2,1)S(1)} %get-tuple-element.146), channel_id=5, replica_groups=mesh['fsdp'=32] {'fsdp'}, dimensions={1}, use_global_device_ids=true | all-gather | bytes 135168 | tf_op jit(solution)/shard_map/all_gather | solution.py:354
  221.3 37.5 %all-gather.9 = bf16[1,512,128]{2,1,0:T(8,128)(2,1)S(1)} all-gather(bf16[1,16,128]{2,1,0:T(8,128)(2,1)S(1)} %get-tuple-element.145), channel_id=11, replica_groups=mesh['fsdp'=32] {'fsdp'}, dimensions={1}, use_global_device_ids=true | all-gather | bytes 135168 | tf_op jit(solution)/shard_map/all_gather | solution.py:354
  259.6 40.5 %all-gather.4 = bf16[1,512,128]{2,1,0:T(8,128)(2,1)} all-gather(bf16[1,16,128]{2,1,0:T(8,128)(2,1)S(1)} %get-tuple-element.144), channel_id=6, replica_groups=mesh['fsdp'=32] {'fsdp'}, dimensions={1}, use_global_device_ids=true | all-gather | bytes 135168 | tf_op jit(solution)/shard_map/all_gather | solution.py:355
  300.7 40.1 %all-gather.5 = bf16[1,512,128]{2,1,0:T(8,128)(2,1)} all-gather(bf16[1,16,128]{2,1,0:T(8,128)(2,1)S(1)} %get-tuple-element.126), channel_id=7, replica_groups=mesh['fsdp'=32] {'fsdp'}, dimensions={1}, use_global_device_ids=true | all-gather | bytes 135168 | tf_op jit(solution)/shard_map/all_gather | solution.py:356
  340.9 40.5 %all-gather.10 = bf16[1,512,128]{2,1,0:T(8,128)(2,1)} all-gather(bf16[1,16,128]{2,1,0:T(8,128)(2,1)S(1)} %get-tuple-element.143), channel_id=12, replica_groups=mesh['fsdp'=32] {'fsdp'}, dimensions={1}, use_global_device_ids=true | all-gather | bytes 135168 | tf_op jit(solution)/shard_map/all_gather | solution.py:355
  381.3 40.3 %all-gather.11 = bf16[1,512,128]{2,1,0:T(8,128)(2,1)} all-gather(bf16[1,16,128]{2,1,0:T(8,128)(2,1)S(1)} %get-tuple-element.125), channel_id=13, replica_groups=mesh['fsdp'=32] {'fsdp'}, dimensions={1}, use_global_device_ids=true | all-gather | bytes 135168 | tf_op jit(solution)/shard_map/all_gather | solution.py:356
  535.8 10.2 fusion.299
  575.7 18.8 fusion.301
  607.7 13.1 multiply_convert_fusion.11
  643.2 18.8 fusion.304
  677.5 12.9 multiply_convert_fusion.10
  713.4 14.1 multiply_reduce_fusion.3
  799.8 14.6 multiply_reduce_fusion.2
  911.9 10.8 multiply_reduce_fusion
  1094.3 36.1 %scatter_fusion.1 = f32[32,128,512]{2,1,0:T(8,128)} fusion(f32[32,128,512]{2,1,0:T(8,128)} %broadcast.509.clone, s32[64]{0:T(128)S(1)} %copy-done.134, f32[64,128,512]{2,1,0:T(8,128)} %pad_maximum_fusion.1), kind=kCustom, calls=%fused_computation.9 | custom fusion | flops 4194304 | bytes 50331904 | tf_op jit(solution)/shard_map/scatter-add | solution.py:286
  1148.1 36.0 %scatter_fusion = f32[32,128,512]{2,1,0:T(8,128)} fusion(f32[32,128,512]{2,1,0:T(8,128)} %broadcast.509.clone.1, s32[64]{0:T(128)S(1)} %copy-done.134, f32[64,128,512]{2,1,0:T(8,128)} %pad_maximum_fusion), kind=kCustom, calls=%fused_computation.8 | custom fusion | flops 4194304 | bytes 50331904 | tf_op jit(solution)/shard_map/scatter-add | solution.py:286
  1205.5 37.2 %all-reduce = (f32[2,8,128]{2,1,0:T(8,128)}, f32[2,512]{1,0:T(2,128)}) all-reduce(f32[2,8,128]{2,1,0:T(8,128)S(1)} %pad_maximum_fusion.35, f32[2,512]{1,0:T(2,128)S(1)} %pad_maximum_fusion.36), channel_id=1, replica_groups=mesh['fsdp'=32] {'fsdp'}, use_global_device_ids=true, to_apply=%region_62.67 | all-reduce | flops 3072 | bytes 24576 | tf_op jit(solution)/shard_map/psum | solution.py:423
  1246.3 121.7 %reduce-scatter.19.cloned.1.call-done = f32[16,128]{1,0:T(8,128)} async-done(((f32[512,128]{1,0:T(8,128)}), f32[16,128]{1,0:T(8,128)}) %reduce-scatter.19.cloned.1.call-update) | async-done | bytes 8208 | tf_op jit(solution)/shard_map/reduce_scatter | solution.py:414
  1368.0 131.5 %reduce-scatter.17.cloned.1.call-done = f32[16,128]{1,0:T(8,128)} async-done(((f32[512,128]{1,0:T(8,128)}), f32[16,128]{1,0:T(8,128)}) %reduce-scatter.17.cloned.1.call-update) | async-done | bytes 8208 | tf_op jit(solution)/shard_map/reduce_scatter | solution.py:414
  1500.8 130.3 %reduce-scatter.23.cloned.1.call-done = f32[16,128]{1,0:T(8,128)} async-done(((f32[512,128]{1,0:T(8,128)}), f32[16,128]{1,0:T(8,128)}) %reduce-scatter.23.cloned.1.call-update) | async-done | bytes 8208 | tf_op jit(solution)/shard_map/reduce_scatter | solution.py:415
  1631.1 131.7 %reduce-scatter.21.cloned.1.call-done = f32[16,128]{1,0:T(8,128)} async-done(((f32[512,128]{1,0:T(8,128)}), f32[16,128]{1,0:T(8,128)}) %reduce-scatter.21.cloned.1.call-update) | async-done | bytes 8208 | tf_op jit(solution)/shard_map/reduce_scatter | solution.py:415
  1764.1 130.3 %reduce-scatter.31.cloned.1.call-done = f32[16,128]{1,0:T(8,128)} async-done(((f32[512,128]{1,0:T(8,128)}), f32[16,128]{1,0:T(8,128)}) %reduce-scatter.31.cloned.1.call-update) | async-done | bytes 8208 | tf_op jit(solution)/shard_map/reduce_scatter | solution.py:417
  1894.4 131.5 %reduce-scatter.29.cloned.1.call-done = f32[16,128]{1,0:T(8,128)} async-done(((f32[512,128]{1,0:T(8,128)}), f32[16,128]{1,0:T(8,128)}) %reduce-scatter.29.cloned.1.call-update) | async-done | bytes 8208 | tf_op jit(solution)/shard_map/reduce_scatter | solution.py:417
  2027.2 131.5 %reduce-scatter.35.cloned.1.call-done = f32[32,128]{1,0:T(8,128)} async-done(((f32[1024,128]{1,0:T(8,128)}), f32[32,128]{1,0:T(8,128)}) %reduce-scatter.35.cloned.1.call-update) | async-done | bytes 16400 | tf_op jit(solution)/shard_map/reduce_scatter | solution.py:418
  2158.7 131.9 %reduce-scatter.33.cloned.1.call-done = f32[32,128]{1,0:T(8,128)} async-done(((f32[1024,128]{1,0:T(8,128)}), f32[32,128]{1,0:T(8,128)}) %reduce-scatter.33.cloned.1.call-update) | async-done | bytes 16400 | tf_op jit(solution)/shard_map/reduce_scatter | solution.py:418
  2291.9 145.6 %reduce-scatter.27.cloned.1.call-done = f32[128,512]{1,0:T(8,128)} async-done(((f32[4096,512]{1,0:T(8,128)}), f32[128,512]{1,0:T(8,128)}) %reduce-scatter.27.cloned.1.call-update) | async-done | bytes 262160 | tf_op jit(solution)/shard_map/reduce_scatter | solution.py:416
  2437.5 146.6 %reduce-scatter.25.cloned.1.call-done = f32[128,512]{1,0:T(8,128)} async-done(((f32[4096,512]{1,0:T(8,128)}), f32[128,512]{1,0:T(8,128)}) %reduce-scatter.25.cloned.1.call-update) | async-done | bytes 262160 | tf_op jit(solution)/shard_map/reduce_scatter | solution.py:416
  2586.1 117.6 %all-reduce.3.cloned.1.call-done = f32[2,32,2,128]{3,2,1,0:T(2,128)} async-done(((f32[2,32,2,128]{3,2,1,0:T(2,128)}), f32[2,32,2,128]{3,2,1,0:T(2,128)}) %all-reduce.3.cloned.1.call-update) | async-done | bytes 65552 | tf_op jit(solution)/shard_map/psum | solution.py:423
  (639 shorter events, 627.8 us)
Async XLA Ops:
  7.2 132.6 %copy-start.133 = (s32[64]{0:T(128)S(1)}, s32[64]{0:T(128)}, u32[]{:S(2)}) copy-start(s32[64]{0:T(128)} %param.25) | copy-start | bytes 772
  7.2 55.6 %copy-start.136 = (bf16[2,16,128]{2,1,0:T(8,128)(2,1)S(1)}, bf16[2,16,128]{2,1,0:T(8,128)(2,1)}, u32[]{:S(2)}) copy-start(bf16[2,16,128]{2,1,0:T(8,128)(2,1)} %param.30) | copy-start | bytes 24580
  7.2 423.6 %all-gather.15.cloned.1.call-start = ((), (), s32[]{:S(2)}) async-start(), calls=%async_computation.25 | async-start | bytes 4325376 | tf_op jit(solution)/shard_map/all_gather | solution.py:357
  9.0 429.6 %all-gather.17.cloned.1.call-start = ((), (), s32[]{:S(2)}) async-start(), calls=%async_computation.26 | async-start | bytes 4325376 | tf_op jit(solution)/shard_map/all_gather | solution.py:357
  9.7 1235.2 %reduce-scatter.15.cloned.1.call-start = ((), (), s32[]{:S(2)}) async-start(), calls=%async_computation.13 | async-start | bytes 270336 | tf_op jit(solution)/shard_map/reduce_scatter | solution.py:413
  60.9 364.3 %copy-start.90 = (bf16[64,32,128]{2,1,0:T(8,128)(2,1)}, bf16[64,32,128]{2,1,0:T(8,128)(2,1)S(1)}, u32[]{:S(2)}) copy-start(bf16[64,32,128]{2,1,0:T(8,128)(2,1)S(1)} %gather_fusion.4) | copy-start | bytes 1572868
  62.8 449.9 %copy-start.2 = (bf16[64,2,49,128]{3,2,1,0:T(8,128)(2,1)}, bf16[64,2,49,128]{3,2,1,0:T(8,128)(2,1)S(1)}, u32[]{:S(2)}) copy-start(bf16[64,2,49,128]{3,2,1,0:T(8,128)(2,1)S(1)} %copy.210) | copy-start | bytes 4816900
  62.8 120.0 %copy-start.154 = (bf16[2,8,128]{2,1,0:T(8,128)(2,1)S(1)}, bf16[2,8,128]{2,1,0:T(8,128)(2,1)}, u32[]{:S(2)}) copy-start(bf16[2,8,128]{2,1,0:T(8,128)(2,1)} %param.32) | copy-start | bytes 12292
  62.8 120.0 %copy-start.137 = (bf16[2,16,128]{2,1,0:T(8,128)(2,1)S(1)}, bf16[2,16,128]{2,1,0:T(8,128)(2,1)}, u32[]{:S(2)}) copy-start(bf16[2,16,128]{2,1,0:T(8,128)(2,1)} %param.26) | copy-start | bytes 24580
  139.2 120.4 %copy-start.138 = (bf16[2,16,128]{2,1,0:T(8,128)(2,1)S(1)}, bf16[2,16,128]{2,1,0:T(8,128)(2,1)}, u32[]{:S(2)}) copy-start(bf16[2,16,128]{2,1,0:T(8,128)(2,1)} %param.27) | copy-start | bytes 24580
  139.8 43.0 %copy-start.141 = (pred[64]{0:T(512)(128)(4,1)}, pred[64]{0:T(512)(128)(4,1)S(1)}, u32[]{:S(2)}) copy-start(pred[64]{0:T(512)(128)(4,1)S(1)} %compare_and_fusion) | copy-start | bytes 196
  139.8 283.1 %copy-start.139 = (bf16[2,512]{1,0:T(2,128)(2,1)S(1)}, bf16[2,512]{1,0:T(2,128)(2,1)}, u32[]{:S(2)}) copy-start(bf16[2,512]{1,0:T(2,128)(2,1)} %param.33) | copy-start | bytes 6148
  141.7 288.2 %copy-start.38 = (bf16[64,32,128]{2,1,0:T(8,128)(2,1)S(1)}, bf16[64,32,128]{2,1,0:T(8,128)(2,1)}, u32[]{:S(2)}) copy-start(bf16[64,32,128]{2,1,0:T(8,128)(2,1)} %param.35) | copy-start | bytes 1572868
  258.8 179.8 %copy-start.74 = (bf16[1,512,128]{2,1,0:T(8,128)(2,1)}, bf16[1,512,128]{2,1,0:T(8,128)(2,1)S(1)}, u32[]{:S(2)}) copy-start(bf16[1,512,128]{2,1,0:T(8,128)(2,1)S(1)} %all-gather.9) | copy-start | bytes 393220
  422.3 185.4 %copy-start.144 = (f32[128]{0:T(128)}, f32[128]{0:T(128)S(1)}, u32[]{:S(2)}) copy-start(f32[128]{0:T(128)S(1)} %get-tuple-element.137) | copy-start | bytes 1540
  676.7 218.5 %copy-start.15 = (f32[2048,128]{1,0:T(8,128)}, f32[2048,128]{1,0:T(8,128)S(1)}, u32[]{:S(2)}) copy-start(f32[2048,128]{1,0:T(8,128)S(1)} %get-tuple-element.173) | copy-start | bytes 3145732
  974.4 270.5 %reduce-scatter.13.cloned.1.call-start = ((), (), s32[]{:S(2)}) async-start(), calls=%async_computation.12 | async-start | bytes 270336 | tf_op jit(solution)/shard_map/reduce_scatter | solution.py:413
  992.6 375.4 %reduce-scatter.19.cloned.1.call-start = ((), (), s32[]{:S(2)}) async-start(), calls=%async_computation.15 | async-start | bytes 270336 | tf_op jit(solution)/shard_map/reduce_scatter | solution.py:414
  998.1 501.4 %reduce-scatter.17.cloned.1.call-start = ((), (), s32[]{:S(2)}) async-start(), calls=%async_computation.14 | async-start | bytes 270336 | tf_op jit(solution)/shard_map/reduce_scatter | solution.py:414
  1007.9 623.2 %reduce-scatter.23.cloned.1.call-start = ((), (), s32[]{:S(2)}) async-start(), calls=%async_computation.17 | async-start | bytes 270336 | tf_op jit(solution)/shard_map/reduce_scatter | solution.py:415
  1014.8 748.0 %reduce-scatter.21.cloned.1.call-start = ((), (), s32[]{:S(2)}) async-start(), calls=%async_computation.16 | async-start | bytes 270336 | tf_op jit(solution)/shard_map/reduce_scatter | solution.py:415
  1021.6 872.8 %reduce-scatter.31.cloned.1.call-start = ((), (), s32[]{:S(2)}) async-start(), calls=%async_computation.21 | async-start | bytes 270336 | tf_op jit(solution)/shard_map/reduce_scatter | solution.py:417
  1051.3 974.6 %reduce-scatter.29.cloned.1.call-start = ((), (), s32[]{:S(2)}) async-start(), calls=%async_computation.20 | async-start | bytes 270336 | tf_op jit(solution)/shard_map/reduce_scatter | solution.py:417
  1059.9 1098.8 %reduce-scatter.35.cloned.1.call-start = ((), (), s32[]{:S(2)}) async-start(), calls=%async_computation.23 | async-start | bytes 540672 | tf_op jit(solution)/shard_map/reduce_scatter | solution.py:418
  1068.2 1222.4 %reduce-scatter.33.cloned.1.call-start = ((), (), s32[]{:S(2)}) async-start(), calls=%async_computation.22 | async-start | bytes 540672 | tf_op jit(solution)/shard_map/reduce_scatter | solution.py:418
  1079.0 1358.6 %reduce-scatter.27.cloned.1.call-start = ((), (), s32[]{:S(2)}) async-start(), calls=%async_computation.19 | async-start | bytes 8650752 | tf_op jit(solution)/shard_map/reduce_scatter | solution.py:416
  1130.4 1453.8 %reduce-scatter.25.cloned.1.call-start = ((), (), s32[]{:S(2)}) async-start(), calls=%async_computation.18 | async-start | bytes 8650752 | tf_op jit(solution)/shard_map/reduce_scatter | solution.py:416
  1184.1 1519.6 %all-reduce.3.cloned.1.call-start = ((), (), s32[]{:S(2)}) async-start(), calls=%async_computation.24 | async-start | bytes 131072 | tf_op jit(solution)/shard_map/psum | solution.py:423
  1191.1 52.2 %copy-start.16 = (f32[2048,128]{1,0:T(8,128)S(1)}, f32[2048,128]{1,0:T(8,128)}, u32[]{:S(2)}) copy-start(f32[2048,128]{1,0:T(8,128)} %copy-done.15) | copy-start | bytes 3145732
  1191.1 52.2 %copy-start.42 = (bf16[2048,512]{1,0:T(8,128)(2,1)S(1)}, bf16[2048,512]{1,0:T(8,128)(2,1)}, u32[]{:S(2)}) copy-start(bf16[2048,512]{1,0:T(8,128)(2,1)} %get-tuple-element.95) | copy-start | bytes 6291460
  1191.1 52.2 %copy-start.82 = (bf16[1,512,128]{2,1,0:T(8,128)(2,1)S(1)}, bf16[1,512,128]{2,1,0:T(8,128)(2,1)}, u32[]{:S(2)}) copy-start(bf16[1,512,128]{2,1,0:T(8,128)(2,1)} %all-gather.11) | copy-start | bytes 393220
  1191.2 52.2 %copy-start.155 = (f32[128]{0:T(128)S(1)}, f32[128]{0:T(128)}, u32[]{:S(2)}) copy-start(f32[128]{0:T(128)} %get-tuple-element.127) | copy-start | bytes 1540
  (158 other events, 974.5 us)
Sparse Core Ops, SparseCore 0:
  11.5 65.5 all-gather.14
  80.5 60.6 all-gather.16
  974.5 130.3 reduce-scatter.14
  1107.1 129.3 reduce-scatter.12
  1238.6 129.3 reduce-scatter.18
  1370.2 129.3 reduce-scatter.16
  1501.8 129.3 reduce-scatter.22
  1633.4 129.3 reduce-scatter.20
  1765.0 129.3 reduce-scatter.30
  1896.6 129.3 reduce-scatter.28
  2028.7 129.9 reduce-scatter.34
  2160.9 129.6 reduce-scatter.32
  2292.9 144.6 reduce-scatter.26
  2439.7 144.4 reduce-scatter.24
  2590.2 113.3 all-reduce.2
where the time goes:
time: 2720 us; the launch traced here: 2710 us
  waiting for transfers between devices  1450 us (53%)
  blocking collectives  432 us (16%)
  matrix products  298 us (11%)
  local copies, waits for them, and re-layouts  283 us (10%)
  other arithmetic  230 us (8%)
    reduce_scatter x2, waiting for transfers between devices, body(): lax.psum_scatter(matrices[3], 'fsdp', scatter_dimension=0, tiled=True)  292 us
    reduce_scatter x2, waiting for transfers between devices, body(): lax.psum_scatter(matrices[5], 'fsdp', scatter_dimension=0, tiled=True)  263 us
    reduce_scatter x2, waiting for transfers between devices, body(): lax.psum_scatter(matrices[2], 'fsdp', scatter_dimension=0, tiled=True)  262 us
    reduce_scatter x2, waiting for transfers between devices, body(): lax.psum_scatter(matrices[4], 'fsdp', scatter_dimension=0, tiled=True)  262 us
    reduce_scatter x2, waiting for transfers between devices, body(): lax.psum_scatter(matrices[1], 'fsdp', scatter_dimension=0, tiled=True)  253 us
    psum x1, waiting for transfers between devices, body(): lax.psum((jnp.stack(vector_list), jnp.stack(mbias_list), jnp.stack(sbias_...  118 us
    all_gather x2, blocking collectives, body(): lax.all_gather(shards[5], 'fsdp', axis=0, tiled=True)  82.3 us
    all_gather x2, blocking collectives, body(): lax.all_gather(shards[1], 'fsdp', axis=0, tiled=True)  80.9 us
  transfers between devices with their start and end apart: 15, of which 11 were waited for; matrix products, arithmetic and copies ran while one was open for 10% of the time, Pallas kernels for 0%

commit v1 on v0

v1 whole, which is shorter than its diff:
```python
import functools
import math

import jax
import jax.numpy as jnp
from jax import lax
from jax.experimental import pallas as pl
from jax.experimental.pallas import tpu as pltpu
from jax.sharding import PartitionSpec as P

D = 128
HEADS = 8
HD = 16
FF = 512
SQ = 16
FR = 49
CR = 64
PROP = 32
PR = 16
STEMS = 32
STEPS = 2
LAYERS = 2
TOK = 32
SB = 8

R_Q = 4 * D
R_PIN = R_Q + SQ
R_ATT = R_PIN + PROP
R_UP = R_ATT + 16
R_DOWN = R_UP + 16
ROWS = R_DOWN + 16
STEM_ROWS = R_ATT

F32 = jnp.float32
BF16 = jnp.bfloat16
VMEM_LIMIT = 60 * 1024 * 1024


def dot(a, b):
    return lax.dot_general(a, b, (((1,), (0,)), ((), ())), preferred_element_type=F32)


def dot_nt(a, b):
    return lax.dot_general(a, b, (((1,), (1,)), ((), ())), preferred_element_type=F32)


def dot_tn(a, b):
    return lax.dot_general(a, b, (((0,), (0,)), ((), ())), preferred_element_type=F32)


def gelu_parts(x):
    cdf = 0.5 + 0.5 * lax.erf(x * math.sqrt(0.5))
    slope = cdf + x * (jnp.exp(-0.5 * x * x) * (1.0 / math.sqrt(2.0 * math.pi)))
    return x * cdf, slope


def norm_parts(x):
    centred = x - jnp.mean(x, -1, keepdims=True)
    inverse = lax.rsqrt(jnp.mean(centred * centred, -1, keepdims=True) + 1e-05)
    return centred * inverse, inverse


def norm_back(grad, gain, hat, inverse):
    g = grad * gain
    return inverse * (
        g - jnp.mean(g, -1, keepdims=True) - hat * jnp.mean(g * hat, -1, keepdims=True)
    )


def head_mask(rows, value):
    row = lax.broadcasted_iota(jnp.int32, (HEADS * rows, D), 0) // rows
    lane = lax.broadcasted_iota(jnp.int32, (HEADS * rows, D), 1) // HD
    return jnp.where(row == lane, value, 0.0).astype(BF16)


def expand(rows, mask):
    return jnp.concatenate([rows] * HEADS, 0) * mask


def contract(wide, rows):
    lane = lax.broadcasted_iota(jnp.int32, (rows, D), 1) // HD
    out = wide[:rows]
    for head in range(1, HEADS):
        out = jnp.where(lane == head, wide[head * rows : (head + 1) * rows], out)
    return out


def fold(x):
    return jnp.sum(x.reshape(x.shape[0] // 8, 8, x.shape[1]), 0)


def trunk_weights(w_ref):
    attn = w_ref[:, R_ATT:R_UP, :].reshape(4 * D, D)
    up = w_ref[:, R_UP:R_DOWN, :].reshape(FF, D)
    down = w_ref[:, R_DOWN:ROWS, :].reshape(FF, D)
    wqkv = jnp.concatenate([attn[:D], attn[D : 2 * D], attn[2 * D : 3 * D]], 1)
    return wqkv, attn[3 * D :], up, down


def stem_kv_weight(w_ref, e):
    return jnp.concatenate([w_ref[e, 0:D, :], w_ref[e, D : 2 * D, :]], 1)


def softmax_rows(score):
    top = jnp.max(score, 0, keepdims=True)
    weight = jnp.exp(score - top)
    return weight * (1.0 / jnp.sum(weight, 0, keepdims=True))


def forward_block(es, hidden, feat_ref, prop_ref, w_ref, vec, mb, sb_ref):
    kept = {}
    pre = [
        dot(prop_ref[j].astype(BF16), w_ref[e, R_PIN:R_ATT, :]) + sb_ref[e, 0:1, :]
        for j, e in enumerate(es)
    ]
    pact, pslope = gelu_parts(jnp.concatenate(pre, 0))
    pact = pact.astype(BF16)
    kept["pact"], kept["pslope"] = pact, pslope
    row16 = lax.broadcasted_iota(jnp.int32, (16, D), 0)
    contexts = []
    for j, e in enumerate(es):
        prow = dot(pact[j * PR : (j + 1) * PR], w_ref[e, 3 * D : 4 * D, :]) + sb_ref[e, 1:2, :]
        parts = []
        for t in range(STEPS):
            last = feat_ref[j, t, 48:49, :].astype(F32)
            tail = jnp.where(row16 == 0, last, jnp.where(row16 == 1, prow[t : t + 1], 0.0))
            parts += [feat_ref[j, t, 0:48, :], tail.astype(BF16)]
        contexts.append(jnp.concatenate(parts, 0))
    kept["ctx"] = contexts
    kvs = [dot(contexts[j], stem_kv_weight(w_ref, e)).astype(BF16) for j, e in enumerate(es)]
    kept["kv"] = kvs
    mask16 = head_mask(SQ, 0.25)
    scores = [
        dot_nt(kvs[j][:, :D], expand(w_ref[e, R_Q:R_PIN, :], mask16)) for j, e in enumerate(es)
    ]
    row8 = lax.broadcasted_iota(jnp.int32, (56, D), 0)
    pad = jnp.zeros((8, D), F32)
    probs = []
    for j in range(SB):
        parts = []
        for t in range(STEPS):
            s = scores[j][t * CR : t * CR + 56]
            parts += [softmax_rows(jnp.where(row8 < FR + 1, s, -1e30)), pad]
        probs.append(jnp.concatenate(parts, 0))
    kept["prob"] = probs
    mixes = []
    for j in range(SB):
        low = probs[j].astype(BF16)
        mixes += [
            contract(
                dot_tn(low[t * CR : (t + 1) * CR], kvs[j][t * CR : (t + 1) * CR, D:]), SQ
            ).astype(BF16)
            for t in range(STEPS)
        ]
    mix = jnp.concatenate(mixes, 0)
    kept["mix"] = mix
    outs = [
        dot(mix[j * TOK : (j + 1) * TOK], w_ref[e, 2 * D : 3 * D, :]) for j, e in enumerate(es)
    ]
    first = hidden + jnp.concatenate(outs, 0)
    kept["first"] = first
    wqkv, wout, up, down = trunk_weights(w_ref)
    normed = (norm_parts(first)[0] * vec[0:1] + vec[1:2]).astype(BF16)
    bias = jnp.concatenate([vec[2:3], jnp.zeros((1, D), F32), vec[3:4]], 1)
    qkv = (dot(normed, wqkv) + bias).astype(BF16)
    kept["qkv"] = qkv
    mask32 = head_mask(TOK, 0.25)
    sprobs = []
    smixes = []
    for j in range(SB):
        rows = qkv[j * TOK : (j + 1) * TOK]
        p = softmax_rows(dot_nt(rows[:, D : 2 * D], expand(rows[:, :D], mask32)))
        sprobs.append(p)
        smixes.append(contract(dot_tn(p.astype(BF16), rows[:, 2 * D :]), TOK).astype(BF16))
    kept["sprob"] = sprobs
    smix = jnp.concatenate(smixes, 0)
    kept["smix"] = smix
    second = first + (dot(smix, wout) + vec[4:5])
    kept["second"] = second
    mlp_in = (norm_parts(second)[0] * vec[5:6] + vec[6:7]).astype(BF16)
    act, slope = gelu_parts(dot_nt(mlp_in, up) + mb)
    act = act.astype(BF16)
    kept["act"], kept["slope"] = act, slope
    return second + (dot(act, down) + vec[7:8]), kept


def backward_block(es, grad, kept, prop_ref, w_ref, vec, acc):
    wqkv, wout, up, down = trunk_weights(w_ref)
    out_low = grad.astype(BF16)
    acc["vec"][7] += fold(out_low.astype(F32))
    acc["down"][...] += dot_tn(out_low, kept["act"])
    grad_act = dot_nt(out_low, down)
    grad_pre = (grad_act * kept["slope"].astype(F32)).astype(BF16)
    acc["mb"][...] += fold(grad_pre.astype(F32))
    hat, inverse = norm_parts(kept["second"])
    mlp_in = (hat * vec[5:6] + vec[6:7]).astype(BF16)
    acc["up"][...] += dot_tn(mlp_in, grad_pre)
    grad_in = dot(grad_pre, up)
    acc["vec"][5] += fold(grad_in * hat)
    acc["vec"][6] += fold(grad_in)
    grad_second = grad + norm_back(grad_in, vec[5:6], hat, inverse)
    branch = grad_second.astype(BF16)
    acc["vec"][4] += fold(branch.astype(F32))
    acc["wout"][...] += dot_tn(kept["smix"], branch)
    grad_mix = dot_nt(branch, wout).astype(BF16)
    mask32 = head_mask(TOK, 0.25)
    mask32_one = head_mask(TOK, 1.0)
    grads_q, grads_k, grads_v = [], [], []
    for j in range(SB):
        rows = kept["qkv"][j * TOK : (j + 1) * TOK]
        p = kept["sprob"][j]
        wide = expand(grad_mix[j * TOK : (j + 1) * TOK], mask32_one)
        grad_p = dot_nt(rows[:, 2 * D :], wide)
        grads_v.append(dot(p.astype(BF16), wide))
        p = p.astype(F32)
        gs = (p * (grad_p - jnp.sum(grad_p * p, 0, keepdims=True))).astype(BF16)
        grads_q.append(contract(dot_tn(gs, rows[:, D : 2 * D]), TOK) * 0.25)
        grads_k.append(dot(gs, expand(rows[:, :D], mask32)))
    grad_qkv = jnp.concatenate(
        [jnp.concatenate(g, 0).astype(BF16) for g in (grads_q, grads_k, grads_v)], 1
    )
    acc["vec"][2] += fold(grad_qkv[:, :D].astype(F32))
    acc["vec"][3] += fold(grad_qkv[:, 2 * D :].astype(F32))
    hat, inverse = norm_parts(kept["first"])
    normed = (hat * vec[0:1] + vec[1:2]).astype(BF16)
    acc["wqkv"][...] += dot_tn(normed, grad_qkv)
    grad_normed = dot_nt(grad_qkv, wqkv)
    acc["vec"][0] += fold(grad_normed * hat)
    acc["vec"][1] += fold(grad_normed)
    grad_first = grad_second + norm_back(grad_normed, vec[0:1], hat, inverse)
    stem_grad = grad_first.astype(BF16)
    mask16 = head_mask(SQ, 0.25)
    mask16_one = head_mask(SQ, 1.0)
    row16 = lax.broadcasted_iota(jnp.int32, (PR, D), 0)
    grad_contexts, grad_props = [], []
    for j, e in enumerate(es):
        g = stem_grad[j * TOK : (j + 1) * TOK]
        grad_wo = dot_tn(kept["mix"][j * TOK : (j + 1) * TOK], g)
        gmix = dot_nt(g, w_ref[e, 2 * D : 3 * D, :]).astype(BF16)
        kv = kept["kv"][j]
        p = kept["prob"][j]
        p_low = p.astype(BF16)
        p = p.astype(F32)
        gss, gvs = [], []
        for t in range(STEPS):
            wide = expand(gmix[t * SQ : (t + 1) * SQ], mask16_one)
            grad_p = dot_nt(kv[t * CR : (t + 1) * CR, D:], wide)
            gvs.append(dot(p_low[t * CR : (t + 1) * CR], wide))
            pt = p[t * CR : (t + 1) * CR]
            gss.append(pt * (grad_p - jnp.sum(grad_p * pt, 0, keepdims=True)))
        gs = jnp.concatenate(gss, 0).astype(BF16)
        grad_q = contract(dot_tn(gs, kv[:, :D]), SQ) * 0.25
        gk = dot(gs, expand(w_ref[e, R_Q:R_PIN, :], mask16))
        gkv = jnp.concatenate([gk, jnp.concatenate(gvs, 0)], 1).astype(BF16)
        grad_wkv = dot_tn(kept["ctx"][j], gkv)
        grad_ctx = dot_nt(gkv, stem_kv_weight(w_ref, e)).astype(BF16)
        grad_contexts.append(grad_ctx)
        wide_ctx = grad_ctx.astype(F32)
        prow = jnp.where(
            row16 == 0,
            wide_ctx[FR : FR + 1],
            jnp.where(row16 == 1, wide_ctx[CR + FR : CR + FR + 1], 0.0),
        )
        prow_low = prow.astype(BF16)
        pact = kept["pact"][j * PR : (j + 1) * PR]
        grad_wp = dot_tn(pact, prow_low)
        gpact = dot_nt(prow_low, w_ref[e, 3 * D : 4 * D, :])
        gppre = (gpact * kept["pslope"][j * PR : (j + 1) * PR]).astype(BF16)
        grad_pin = dot_tn(prop_ref[j].astype(BF16), gppre)
        grad_props.append(dot_nt(gppre, w_ref[e, R_PIN:R_ATT, :]))
        stem = acc["stem"]
        stem[e, 0:D, :] += grad_wkv[:, :D]
        stem[e, D : 2 * D, :] += grad_wkv[:, D:]
        stem[e, 2 * D : 3 * D, :] += grad_wo
        stem[e, 3 * D : 4 * D, :] += grad_wp
        stem[e, R_Q:R_PIN, :] += grad_q
        stem[e, R_PIN:R_ATT, :] += grad_pin
        acc["sb"][e, 0:1, :] += jnp.sum(gppre.astype(F32), 0, keepdims=True)
        acc["sb"][e, 1:2, :] += jnp.sum(prow, 0, keepdims=True)
    return grad_first, grad_contexts, grad_props


ACC = ("stem", "sb", "wqkv", "wout", "up", "down", "vec", "mb")


def acc_shapes():
    return [
        pltpu.VMEM((STEMS, STEM_ROWS, D), F32),
        pltpu.VMEM((STEMS, 2, D), F32),
        pltpu.VMEM((D, 3 * D), F32),
        pltpu.VMEM((D, D), F32),
        pltpu.VMEM((D, FF), F32),
        pltpu.VMEM((D, FF), F32),
        pltpu.VMEM((8, 8, D), F32),
        pltpu.VMEM((8, FF), F32),
    ]


def clear(acc):
    for ref in acc.values():
        ref[...] = jnp.zeros(ref.shape, ref.dtype)


def finish(acc, grad_ref, vec_ref, mb_ref, sb_ref):
    def stem_out(e, carry):
        grad_ref[e, 0:STEM_ROWS, :] = acc["stem"][e].astype(grad_ref.dtype)
        return carry

    lax.fori_loop(0, STEMS, stem_out, 0)
    wqkv = acc["wqkv"][...]
    attn = [wqkv[:, :D], wqkv[:, D : 2 * D], wqkv[:, 2 * D :], acc["wout"][...]]
    for block in range(4):
        grad_ref[block * 8 : block * 8 + 8, R_ATT:R_UP, :] = (
            attn[block].astype(grad_ref.dtype).reshape(8, 16, D)
        )
    grad_ref[:, R_UP:R_DOWN, :] = acc["up"][...].T.astype(grad_ref.dtype).reshape(STEMS, 16, D)
    grad_ref[:, R_DOWN:ROWS, :] = acc["down"][...].T.astype(grad_ref.dtype).reshape(STEMS, 16, D)
    vec_ref[...] = jnp.sum(acc["vec"][...], 1)
    mb_ref[...] = jnp.sum(acc["mb"][...], 0, keepdims=True)
    sb_ref[...] = acc["sb"][...]


SAVED = ("ctx", "kv", "prob", "mix", "first", "qkv", "sprob", "smix", "second", "act", "slope", "pact", "pslope")
PER_SAMPLE = ("ctx", "kv", "prob", "sprob")


def saved_shapes(samples):
    rows = samples * TOK
    return dict(
        ctx=((samples, STEPS * CR, D), BF16),
        kv=((samples, STEPS * CR, 2 * D), BF16),
        prob=((samples, STEPS * CR, D), BF16),
        mix=((rows, D), BF16),
        first=((rows, D), F32),
        qkv=((rows, 3 * D), BF16),
        sprob=((samples, TOK, HEADS * TOK), BF16),
        smix=((rows, D), BF16),
        second=((rows, D), F32),
        act=((rows, FF), BF16),
        slope=((rows, FF), BF16),
        pact=((samples * PR, D), BF16),
        pslope=((samples * PR, D), F32),
    )


def forward_kernel(emb_ref, tok_ref, feat_ref, prop_ref, w_ref, vec_ref, mb_ref, sb_ref, out_ref, *saved):
    step = pl.program_id(0)
    es = [emb_ref[step * SB + j] for j in range(SB)]
    out, kept = forward_block(
        es, tok_ref[...].astype(F32), feat_ref, prop_ref, w_ref, vec_ref[...], mb_ref[...], sb_ref
    )
    out_ref[...] = out
    for name, ref in zip(SAVED, saved):
        if name in PER_SAMPLE:
            for j in range(SB):
                ref[j] = kept[name][j].astype(ref.dtype)
        else:
            ref[...] = kept[name].astype(ref.dtype)


def middle_kernel(
    emb_ref, hid_ref, feat_ref, prop_ref, w_ref, vec_ref, mb_ref, sb_ref, cot_ref,
    out_ref, ghid_ref, gfeat_ref, gprop_ref, gw_ref, gvec_ref, gmb_ref, gsb_ref, *accs
):
    step = pl.program_id(0)
    acc = dict(zip(ACC, accs))
    pl.when(step == 0)(lambda: clear(acc))
    es = [emb_ref[step * SB + j] for j in range(SB)]
    vec = vec_ref[...]
    out, kept = forward_block(es, hid_ref[...], feat_ref, prop_ref, w_ref, vec, mb_ref[...], sb_ref)
    out_ref[...] = out.astype(BF16)
    ghid, gctx, gprop = backward_block(
        es, cot_ref[...].astype(F32), kept, prop_ref, w_ref, vec, acc
    )
    ghid_ref[...] = ghid
    for j in range(SB):
        gfeat_ref[j] = gctx[j]
        gprop_ref[j] = gprop[j]
    pl.when(step == pl.num_programs(0) - 1)(lambda: finish(acc, gw_ref, gvec_ref, gmb_ref, gsb_ref))


def backward_kernel(emb_ref, grad_ref, prop_ref, w_ref, vec_ref, gfeat1_ref, gprop1_ref, *rest):
    saved = rest[: len(SAVED)]
    gtok_ref, gfeat_ref, gprop_ref, gw_ref, gvec_ref, gmb_ref, gsb_ref = rest[len(SAVED) : len(SAVED) + 7]
    acc = dict(zip(ACC, rest[len(SAVED) + 7 :]))
    step = pl.program_id(0)
    pl.when(step == 0)(lambda: clear(acc))
    es = [emb_ref[step * SB + j] for j in range(SB)]
    kept = {name: ref if name in PER_SAMPLE else ref[...] for name, ref in zip(SAVED, saved)}
    ghid, gctx, gprop = backward_block(es, grad_ref[...], kept, prop_ref, w_ref, vec_ref[...], acc)
    gtok_ref[...] = ghid
    for j in range(SB):
        total = gctx[j].astype(F32) + gfeat1_ref[j].astype(F32)
        for t in range(STEPS):
            gfeat_ref[j, t] = total[t * CR : t * CR + FR]
        gprop_ref[j] = (gprop[j] + gprop1_ref[j])[:STEPS]
    pl.when(step == pl.num_programs(0) - 1)(lambda: finish(acc, gw_ref, gvec_ref, gmb_ref, gsb_ref))


def blocked(shape, per_step):
    block = (per_step,) + tuple(shape[1:])
    zeros = (0,) * (len(shape) - 1)
    return pl.BlockSpec(block, lambda i, *_: (i,) + zeros)


def whole(shape):
    zeros = (0,) * len(shape)
    return pl.BlockSpec(tuple(shape), lambda i, *_: zeros, pipeline_mode=pl.Buffered(1))


def call(kernel, steps, emb, ins, outs, scratch):
    return pl.pallas_call(
        kernel,
        grid_spec=pltpu.PrefetchScalarGridSpec(
            num_scalar_prefetch=1,
            grid=(steps,),
            in_specs=[blocked(a.shape, n) if n else whole(a.shape) for a, n in ins],
            out_specs=[blocked(s, n) if n else whole(s) for s, _, n in outs],
            scratch_shapes=scratch,
        ),
        out_shape=[jax.ShapeDtypeStruct(s, d) for s, d, _ in outs],
        compiler_params=pltpu.CompilerParams(
            dimension_semantics=("arbitrary",), vmem_limit_bytes=VMEM_LIMIT
        ),
    )(emb, *[a for a, _ in ins])


def compute(tokens, features, proprio, emb, w0, w1, vecs, mbs, sbs, cot, wire):
    samples = emb.shape[0]
    steps = samples // SB
    rows = samples * TOK
    rb = SB * TOK
    tok = tokens.reshape(rows, D)
    prop = jnp.pad(proprio.astype(F32), ((0, 0), (0, PR - STEPS), (0, 0)))
    shapes = saved_shapes(samples)
    per = lambda s: s[0] // steps
    saved_outs = [(shapes[n][0], shapes[n][1], per(shapes[n][0])) for n in SAVED]
    res = call(
        forward_kernel, steps, emb,
        [(tok, rb), (features, SB), (prop, SB), (w0, 0), (vecs[0], 0), (mbs[0], 0), (sbs[0], 0)],
        [((rows, D), F32, rb)] + saved_outs, [],
    )
    hidden, saved = res[0], res[1:]
    grad_outs = [
        ((STEMS, ROWS, D), wire, 0), ((8, D), F32, 0), ((1, FF), F32, 0), ((STEMS, 2, D), F32, 0)
    ]
    out, ghid, gfeat1, gprop1, *grads1 = call(
        middle_kernel, steps, emb,
        [(hidden, rb), (features, SB), (prop, SB), (w1, 0), (vecs[1], 0), (mbs[1], 0), (sbs[1], 0),
         (cot.reshape(rows, D), rb)],
        [((rows, D), BF16, rb), ((rows, D), F32, rb), ((samples, STEPS * CR, D), BF16, SB),
         ((samples, PR, PROP), F32, SB)] + grad_outs,
        acc_shapes(),
    )
    gtok, gfeat, gprop, *grads0 = call(
        backward_kernel, steps, emb,
        [(ghid, rb), (prop, SB), (w0, 0), (vecs[0], 0), (gfeat1, SB), (gprop1, SB)]
        + [(a, per(a.shape)) for a in saved],
        [((rows, D), F32, rb), ((samples, STEPS, FR, D), F32, SB), ((samples, STEPS, PROP), F32, SB)]
        + grad_outs,
        acc_shapes(),
    )
    return (
        out.reshape(tokens.shape), gtok.reshape(tokens.shape), gfeat, gprop, grads0, grads1
    )


def pack(attn, up, down, stem, queries, pin, n):
    gathered = [lax.all_gather(a, "fsdp", axis=1, tiled=True) for a in (attn, up, down, stem, queries, pin)]
    attn, up, down, stem, queries, pin = gathered
    stem = stem.reshape(LAYERS, STEMS, D, 4, D).transpose(0, 1, 3, 2, 4).reshape(LAYERS, STEMS, 4 * D, D)
    parts = [stem] + [a.reshape(LAYERS, STEMS, -1, D) for a in (queries, pin, attn, up, down)]
    return jnp.concatenate(parts, 2)


def unpack_blocks(grad):
    lead = grad.shape[:-2]
    stem = grad[..., : 4 * D, :].reshape(lead + (4, D, D))
    stem = jnp.swapaxes(stem, -3, -2).reshape(lead + (D, 4 * D))
    return (
        grad[..., R_ATT:R_UP, :], grad[..., R_UP:R_DOWN, :], grad[..., R_DOWN:ROWS, :],
        stem, grad[..., R_Q:R_PIN, :], grad[..., R_PIN:R_ATT, :],
    )


def body(n, tokens, features, proprio, embodiment, trunk_attn, feedforward_up_weight, mlp_down,
         stem_mats, stem_queries, prop_in, trunk_vectors, mlp_bias, stem_bias, cotangent):
    if n == STEMS:
        stem = stem_mats.reshape(LAYERS, D, 4, D).transpose(0, 2, 1, 3).reshape(LAYERS, 4 * D, D)
        packed = jnp.concatenate(
            [stem, stem_queries, prop_in, trunk_attn, feedforward_up_weight, mlp_down], 1
        )
        w = lax.all_gather(packed, "fsdp", axis=1)
    else:
        w = pack(trunk_attn, feedforward_up_weight, mlp_down, stem_mats, stem_queries, prop_in, n)
    vecs = trunk_vectors.astype(F32)
    mbs = mlp_bias.astype(F32).reshape(LAYERS, 1, FF)
    sbs = stem_bias.astype(F32)
    out, gtok, gfeat, gprop, g0, g1 = compute(
        tokens, features, proprio, embodiment, w[0], w[1], vecs, mbs, sbs, cotangent, F32
    )
    grads = jnp.stack([g0[0], g1[0]])
    if n == STEMS:
        mine = lax.psum_scatter(grads, "fsdp", scatter_dimension=1, tiled=True)
        mats = [a[:, 0] for a in unpack_blocks(mine)]
    else:
        mats = [
            lax.psum_scatter(a.reshape(LAYERS, -1, a.shape[-1]), "fsdp", scatter_dimension=1, tiled=True)
            for a in unpack_blocks(grads)
        ]
    small = lax.psum(tuple(jnp.stack([a, b]) for a, b in zip(g0[1:], g1[1:])), "fsdp")
    return (out, gtok, gfeat, gprop, *mats, small[0], small[1].reshape(LAYERS, FF), small[2])


def solution(mesh):
    n = mesh.shape["fsdp"]
    return jax.shard_map(
        functools.partial(body, n),
        mesh=mesh,
        in_specs=(
            P("fsdp"), P("fsdp"), P("fsdp"), P("fsdp"),
            P(None, "fsdp"), P(None, "fsdp"), P(None, "fsdp"), P(None, "fsdp"), P(None, "fsdp"),
            P(None, "fsdp"), P(), P(), P(), P("fsdp"),
        ),
        out_specs=(
            P("fsdp"), P("fsdp"), P("fsdp"), P("fsdp"),
            P(None, "fsdp"), P(None, "fsdp"), P(None, "fsdp"), P(None, "fsdp"), P(None, "fsdp"),
            P(None, "fsdp"), P(), P(), P(),
        ),
        check_vma=False,
    )
```

time: 2720 us -> 661 us (0.24)
  waiting for transfers between devices: 1450 us -> 352 us
  blocking collectives: 432 us -> 41.4 us
  matrix products: 298 us -> 0 us
  local copies, waits for them, and re-layouts: 283 us -> 32.5 us
  other arithmetic: 230 us -> 18.1 us
  Pallas kernels: 0 us -> 201 us
    reduce_scatter x12 -> x0, waiting for transfers between devices: 1330 us -> none  [the longest x2 292 us: body(): lax.psum_scatter(matrices[3], 'fsdp', scatter_dimension=0, tiled=True)]
    all_gather x10 -> x0, blocking collectives: 395 us -> none  [the longest x2 82.3 us: body(): lax.all_gather(shards[5], 'fsdp', axis=0, tiled=True)]
    dot_general x70 -> x0, matrix products: 278 us -> none  [the longest x2 28.7 us: layer_backward(): jnp.einsum('sqhe,skhe->shqk', grad_mix, value_h, preferred_element_type=j...]
    unnamed x15 -> x3, waiting for transfers between devices: 0.96 us -> 272 us
    pallas_call x0 -> x3, Pallas kernels: none -> 201 us  [call(): pl.pallas_call(kernel, grid_spec=pltpu.PrefetchScalarGridSpec(num_scalar_...]
    psum x1 -> x0, waiting for transfers between devices: 118 us -> none  [body(): lax.psum((jnp.stack(vector_list), jnp.stack(mbias_list), jnp.stack(sbias_...]
    scatter-add x8 -> x0, other arithmetic: 89.9 us -> none  [the longest x2 72.1 us: layer_backward(): jax.ops.segment_sum(grad_each, embodiment, num_segments=STEMS)]
    reshape x16 -> x1, local copies, waits for them, and re-layouts: 83.2 us -> 1.02 us  [body(): stem_mats.reshape(LAYERS, D, 4, D).transpose(0, 2, 1, 3)]
  transfers between devices with their start and end apart: 15 -> 2, of which waited for: 11 -> 2; matrix products, arithmetic and copies ran while one was open for 10% -> 2% of each run, Pallas kernels for 0% -> 0%
where the time goes in v1:
time: 661 us; the launch traced here: 660 us
  waiting for transfers between devices  352 us (53%)
  Pallas kernels  201 us (30%)
  blocking collectives  41.4 us (6%)
  local copies, waits for them, and re-layouts  32.5 us (5%)
  other arithmetic  18.1 us (3%)
  between operations  14.2 us (2%)
    unnamed x3, waiting for transfers between devices  272 us
    pallas_call x3, Pallas kernels, call(): pl.pallas_call(kernel, grid_spec=pltpu.PrefetchScalarGridSpec(num_scalar_...  201 us
    all_gather x1, waiting for transfers between devices, body(): w = lax.all_gather(packed, 'fsdp', axis=1)  80.1 us
    psum x1, blocking collectives, body(): lax.psum(tuple((jnp.stack([a, b]) for a, b in zip(g0[1:], g1[1:]))), 'fsdp')  41.4 us
    unnamed x28, local copies, waits for them, and re-layouts  15.2 us
    another operation x1, other arithmetic, body(): grads = jnp.stack([g0[0], g1[0]])  15.1 us
  transfers between devices with their start and end apart: 2, of which 2 were waited for; matrix products, arithmetic and copies ran while one was open for 2% of the time, Pallas kernels for 0%

profile of v1, /device:TPU:0, one launch (start us, length us, event | category | flops | bytes accessed | tf_op | source)
XLA Modules:
  0.0 659.7 jit_solution(16232352046812155441)
XLA Ops:
  7.2 1.0 reshape.56
  8.3 0.7 constant_dynamic-update-slice_fusion.4
  9.0 0.7 constant_dynamic-update-slice_fusion.3
  9.8 0.7 constant_dynamic-update-slice_fusion.2
  10.5 0.7 constant_dynamic-update-slice_fusion.1
  11.2 0.7 constant_dynamic-update-slice_fusion
  11.9 0.7 copy-done
  12.6 0.0 all-reduce.6.cloned.1.call-start
  12.7 0.8 copy.34
  13.5 0.7 convert_element_type.12
  14.2 2.9 copy.36.feat_ref
  17.1 0.8 pad_convert_fusion.prop_ref
  18.0 0.6 fusion.1
  18.6 0.6 slice_bitcast_fusion.2
  19.2 0.6 slice_bitcast_fusion
  19.8 80.1 %all-gather.3.cloned.1.call-done = bf16[2,19456,128]{2,1,0:T(8,128)(2,1)} async-done(((bf16[2,608,128]{2,1,0:T(8,128)(2,1)}), bf16[2,19456,128]{2,1,0:T(8,128)(2,1)}) %all-gather.3.cloned.1.call-update) | async-done | bytes 9961488 | tf_op jit(solution)/shard_map/all_gather | solution.py:493
  99.9 8.5 %fusion = (bf16[1,19456,128]{2,1,0:T(8,128)(2,1)}, bf16[1,19456,128]{2,1,0:T(8,128)(2,1)}) fusion(bf16[2,19456,128]{2,1,0:T(8,128)(2,1)} %all-gather.3.cloned.1.call-done), kind=kLoop, calls=%fused_computation.21 | loop fusion | bytes 19922944 | tf_op jit(solution)/shard_map/slice | solution.py:500
  108.5 29.7 %shard_map.237 = (f32[2048,128]{1,0:T(8,128)}, bf16[64,128,128]{2,1,0:T(8,128)(2,1)}, bf16[64,128,256]{2,1,0:T(8,128)(2,1)}, bf16[64,128,128]{2,1,0:T(8,128)(2,1...) custom-call(s32[64]{0:T(128)} %emb_ref.5, ...), custom_call_target="tpu_custom_call" | custom-call | tf_op jit(solution)/shard_map/pallas_call | solution.py:412
  138.2 96.9 %shard_map.238 = (bf16[2048,128]{1,0:T(8,128)(2,1)}, f32[2048,128]{1,0:T(8,128)}, bf16[64,128,128]{2,1,0:T(8,128)(2,1)}, f32[64,16,32]{2,1,0:T(8,128)}, f32[32,6...) custom-call(s32[64]{0:T(128)} %emb_ref.5, ...), custom_call_target="tpu_custom_call" | custom-call | tf_op jit(solution)/shard_map/pallas_call | solution.py:412
  235.1 74.7 %shard_map.239 = (f32[2048,128]{1,0:T(8,128)}, f32[64,2,49,128]{3,2,1,0:T(8,128)}, f32[64,2,32]{2,1,0:T(2,128)}, f32[32,608,128]{2,1,0:T(8,128)}, f32[8,128]{1,0...) custom-call(s32[64]{0:T(128)} %emb_ref.5, f32[2048,128]{1,0:T(8,128)} %get-tuple-element.44.grad_ref, ...), custom_call_target="tpu_custom_call" | custom-call | tf_op jit(solution)/shard_map/pallas_call | solution.py:412
  309.9 1.4 pad_maximum_fusion.1
  311.3 15.1 %pad_maximum_fusion = f32[2,32,608,128]{3,2,1,0:T(8,128)} fusion(f32[1,32,608,128]{3,2,1,0:T(8,128)} %bitcast.50, f32[1,32,608,128]{3,2,1,0:T(8,128)} %bitcast.51), kind=kLoop, calls=%fused_computation | loop fusion | flops 4980736 | bytes 39845888 | tf_op jit(solution)/shard_map/stack | solution.py:502
  326.5 5.7 copy.39
  332.2 0.7 copy.40
  332.9 41.4 %all-reduce.2 = (f32[2,8,128]{2,1,0:T(8,128)}, f32[2,512]{1,0:T(2,128)}) all-reduce(f32[2,8,128]{2,1,0:T(8,128)S(1)} %pad_maximum_fusion.2, f32[2,512]{1,0:T(2,128)S(1)} %maximum_bitcast_fusion), channel_id=1, replica_groups=mesh['fsdp'=32] {'fsdp'}, use_global_device_ids=true, to_apply=%region_1.2 | all-reduce | flops 3072 | bytes 24576 | tf_op jit(solution)/shard_map/psum | solution.py:511
  374.3 271.8 %all-reduce.6.cloned.1.call-done = (f32[2,32,608,128]{3,2,1,0:T(8,128)}, f32[2,32,2,128]{3,2,1,0:T(2,128)}) async-done(((f32[2,32,608,128]{3,2,1,0:T(8,128)}, f32[2,32,2,128]{3,2,1,0:T(2,128)}), (f32[2,32,608,128]{3,2,1,0:T(8,128)}, f32[2,32,2,128]{3,2,1,0:T(2,128)})) %all-reduce.6.cloned.1.call-update) | async-done | bytes 19988496
  646.1 1.1 constant_dynamic-slice_fusion
  647.2 0.3 copy.38
  647.5 1.0 squeeze_reshape.3
  648.6 1.4 dynamic-slice_bitcast_fusion
  650.0 1.4 dynamic-slice_bitcast_fusion.1
  651.4 1.5 copy.50
  (25 shorter events, 0.2 us)
Async XLA Ops:
  7.2 9.9 %copy-start.2 = (bf16[2,32,2,128]{3,2,1,0:T(2,128)(2,1)S(1)}, bf16[2,32,2,128]{3,2,1,0:T(2,128)(2,1)}, u32[]{:S(2)}) copy-start(bf16[2,32,2,128]{3,2,1,0:T(2,128)(2,1)} %param.26) | copy-start | bytes 98308
  7.2 10.8 %copy-start.4 = (bf16[2,512]{1,0:T(2,128)(2,1)S(1)}, bf16[2,512]{1,0:T(2,128)(2,1)}, u32[]{:S(2)}) copy-start(bf16[2,512]{1,0:T(2,128)(2,1)} %param.25) | copy-start | bytes 6148
  7.2 92.7 %all-gather.3.cloned.1.call-start = ((), (), s32[]{:S(2)}) async-start(), calls=%async_computation | async-start | bytes 10272768 | tf_op jit(solution)/shard_map/all_gather | solution.py:493
  11.9 0.7 copy-start
  12.6 633.5 %all-reduce.6.cloned.1.call-start = ((), (), s32[]{:S(2)}) async-start(), calls=%async_computation.1 | async-start | bytes 39976960
  235.1 74.7 %copy-start.3 = (f32[32,2,128]{2,1,0:T(2,128)S(1)}, f32[32,2,128]{2,1,0:T(2,128)}, u32[]{:S(2)}) copy-start(f32[32,2,128]{2,1,0:T(2,128)} %get-tuple-element.70) | copy-start | bytes 98308
  326.4 5.7 copy-start.1
  326.4 6.4 copy-start.7
  326.5 6.4 copy-start.8
  326.5 6.4 copy-start.5
  326.5 6.4 copy-start.6
Sparse Core Ops, SparseCore 0:
  12.7 87.1 all-gather.2
  326.6 319.5 all-reduce.5

commit v2 on v1

--- a/solution.py
+++ b/solution.py
@@ -30,6 +30,7 @@
 R_DOWN = R_UP + 16
 ROWS = R_DOWN + 16
 STEM_ROWS = R_ATT
+SMALL = 16 + 2 * STEMS
 
 F32 = jnp.float32
 BF16 = jnp.bfloat16
@@ -275,8 +276,8 @@
         stem[e, 3 * D : 4 * D, :] += grad_wp
         stem[e, R_Q:R_PIN, :] += grad_q
         stem[e, R_PIN:R_ATT, :] += grad_pin
-        acc["sb"][e, 0:1, :] += jnp.sum(gppre.astype(F32), 0, keepdims=True)
-        acc["sb"][e, 1:2, :] += jnp.sum(prow, 0, keepdims=True)
+        acc["sb"][0, pl.ds(e, 1), :] += jnp.sum(gppre.astype(F32), 0, keepdims=True)
+        acc["sb"][1, pl.ds(e, 1), :] += jnp.sum(prow, 0, keepdims=True)
     return grad_first, grad_contexts, grad_props
 
 
@@ -286,7 +287,7 @@
 def acc_shapes():
     return [
         pltpu.VMEM((STEMS, STEM_ROWS, D), F32),
-        pltpu.VMEM((STEMS, 2, D), F32),
+        pltpu.VMEM((2, STEMS, D), F32),
         pltpu.VMEM((D, 3 * D), F32),
         pltpu.VMEM((D, D), F32),
         pltpu.VMEM((D, FF), F32),
@@ -301,7 +302,7 @@
         ref[...] = jnp.zeros(ref.shape, ref.dtype)
 
 
-def finish(acc, grad_ref, vec_ref, mb_ref, sb_ref):
+def finish(acc, grad_ref, small_ref):
     def stem_out(e, carry):
         grad_ref[e, 0:STEM_ROWS, :] = acc["stem"][e].astype(grad_ref.dtype)
         return carry
@@ -315,9 +316,13 @@
         )
     grad_ref[:, R_UP:R_DOWN, :] = acc["up"][...].T.astype(grad_ref.dtype).reshape(STEMS, 16, D)
     grad_ref[:, R_DOWN:ROWS, :] = acc["down"][...].T.astype(grad_ref.dtype).reshape(STEMS, 16, D)
-    vec_ref[...] = jnp.sum(acc["vec"][...], 1)
-    mb_ref[...] = jnp.sum(acc["mb"][...], 0, keepdims=True)
-    sb_ref[...] = acc["sb"][...]
+    small_ref[0:8, :] = jnp.sum(acc["vec"][...], 1)
+    mb = jnp.sum(acc["mb"][...], 0, keepdims=True)
+    small_ref[8:16, :] = jnp.concatenate(
+        [mb[:, i * D : (i + 1) * D] for i in range(4)] + [jnp.zeros((4, D), F32)], 0
+    )
+    for i in range(2):
+        small_ref[16 + i * STEMS : 16 + (i + 1) * STEMS, :] = acc["sb"][i]
 
 
 SAVED = ("ctx", "kv", "prob", "mix", "first", "qkv", "sprob", "smix", "second", "act", "slope", "pact", "pslope")
@@ -360,7 +365,7 @@
 
 def middle_kernel(
     emb_ref, hid_ref, feat_ref, prop_ref, w_ref, vec_ref, mb_ref, sb_ref, cot_ref,
-    out_ref, ghid_ref, gfeat_ref, gprop_ref, gw_ref, gvec_ref, gmb_ref, gsb_ref, *accs
+    out_ref, ghid_ref, gfeat_ref, gprop_ref, gw_ref, gsmall_ref, *accs
 ):
     step = pl.program_id(0)
     acc = dict(zip(ACC, accs))
@@ -376,13 +381,13 @@
     for j in range(SB):
         gfeat_ref[j] = gctx[j]
         gprop_ref[j] = gprop[j]
-    pl.when(step == pl.num_programs(0) - 1)(lambda: finish(acc, gw_ref, gvec_ref, gmb_ref, gsb_ref))
+    pl.when(step == pl.num_programs(0) - 1)(lambda: finish(acc, gw_ref, gsmall_ref))
 
 
 def backward_kernel(emb_ref, grad_ref, prop_ref, w_ref, vec_ref, gfeat1_ref, gprop1_ref, *rest):
     saved = rest[: len(SAVED)]
-    gtok_ref, gfeat_ref, gprop_ref, gw_ref, gvec_ref, gmb_ref, gsb_ref = rest[len(SAVED) : len(SAVED) + 7]
-    acc = dict(zip(ACC, rest[len(SAVED) + 7 :]))
+    gtok_ref, gfeat_ref, gprop_ref, gw_ref, gsmall_ref = rest[len(SAVED) : len(SAVED) + 5]
+    acc = dict(zip(ACC, rest[len(SAVED) + 5 :]))
     step = pl.program_id(0)
     pl.when(step == 0)(lambda: clear(acc))
     es = [emb_ref[step * SB + j] for j in range(SB)]
@@ -394,7 +399,7 @@
         for t in range(STEPS):
             gfeat_ref[j, t] = total[t * CR : t * CR + FR]
         gprop_ref[j] = (gprop[j] + gprop1_ref[j])[:STEPS]
-    pl.when(step == pl.num_programs(0) - 1)(lambda: finish(acc, gw_ref, gvec_ref, gmb_ref, gsb_ref))
+    pl.when(step == pl.num_programs(0) - 1)(lambda: finish(acc, gw_ref, gsmall_ref))
 
 
 def blocked(shape, per_step):
@@ -441,9 +446,7 @@
         [((rows, D), F32, rb)] + saved_outs, [],
     )
     hidden, saved = res[0], res[1:]
-    grad_outs = [
-        ((STEMS, ROWS, D), wire, 0), ((8, D), F32, 0), ((1, FF), F32, 0), ((STEMS, 2, D), F32, 0)
-    ]
+    grad_outs = [((STEMS, ROWS, D), wire, 0), ((SMALL, D), F32, 0)]
     out, ghid, gfeat1, gprop1, *grads1 = call(
         middle_kernel, steps, emb,
         [(hidden, rb), (features, SB), (prop, SB), (w1, 0), (vecs[1], 0), (mbs[1], 0), (sbs[1], 0),
@@ -465,7 +468,304 @@
     )
 
 
-def pack(attn, up, down, stem, queries, pin, n):
+STREAMS = (
+    (0, 256, ("z", "x", "y")),
+    (256, 256, ("z", "y", "x")),
+    (512, 48, ("x", "y", "z")),
+    (560, 48, ("y", "x", "z")),
+)
+SIZES = {"z": 4, "y": 2, "x": 2, "c": 2}
+AXES = ("z", "y", "x", "c")
+MESH = pl.DeviceIdType.MESH
+
+
+def place():
+    me = lax.axis_index("fsdp")
+    return {"z": me // 8, "y": (me // 4) % 2, "x": (me // 2) % 2, "c": me % 2}
+
+
+def number(at):
+    return ((at["z"] * 2 + at["y"]) * 2 + at["x"]) * 2 + at["c"]
+
+
+def moved(at, axis, by):
+    out = dict(at)
+    out[axis] = (at[axis] + by) % SIZES[axis]
+    return out
+
+
+def greet(at):
+    barrier = pltpu.get_barrier_semaphore()
+    count = 0
+    for axis in AXES:
+        for by in range(1, SIZES[axis]):
+            pl.semaphore_signal(
+                barrier, inc=1, device_id=(number(moved(at, axis, by)),), device_id_type=MESH
+            )
+            count += 1
+    pl.semaphore_wait(barrier, count)
+
+
+def block(ref, at, done, row, count):
+    index = tuple(pl.ds(0, SIZES[a]) if a in done else pl.ds(at[a], 1) for a in AXES)
+    return ref.at[index + (pl.ds(row, count), slice(None))]
+
+
+def gather_kernel(att, up, down, stem, q, pin, g0, g1, local_sem, send_sem, recv_sem):
+    at = place()
+    outs = (g0, g1)
+    locals_ = []
+    for layer in range(LAYERS):
+        slot = outs[layer].at[at["z"], at["y"], at["x"], at["c"]]
+        pieces = [
+            (stem.at[layer, :, pl.ds(j * D, D)], j * D, D) for j in range(4)
+        ] + [
+            (q.at[layer], R_Q, SQ), (pin.at[layer], R_PIN, PROP), (att.at[layer], R_ATT, 16),
+            (up.at[layer], R_UP, 16), (down.at[layer], R_DOWN, 16),
+        ]
+        for i, (piece, row, count) in enumerate(pieces):
+            copy = pltpu.make_async_copy(piece, slot.at[pl.ds(row, count), :], local_sem.at[layer, i])
+            copy.start()
+            locals_.append(copy)
+    greet(at)
+    for copy in locals_:
+        copy.wait()
+    chains = [(layer, s) for layer in range(LAYERS) for s in range(len(STREAMS))]
+    pending = {}
+    sent = []
+    for phase in range(4):
+        for chain in chains:
+            layer, s = chain
+            row, count, order = STREAMS[s]
+            order = order + ("c",)
+            for copy in pending.pop(chain, ()):
+                copy.wait_recv()
+            axis, done = order[phase], order[:phase]
+            got = []
+            for by in range(1, SIZES[axis]):
+                to = moved(at, axis, by)
+                sem = (layer * 4 + s, AXES.index(axis), by - 1)
+                mine = block(outs[layer], at, done, row, count)
+                copy = pltpu.make_async_remote_copy(
+                    mine, mine, send_sem.at[sem], recv_sem.at[sem],
+                    device_id=(number(to),), device_id_type=MESH,
+                )
+                copy.start()
+                sent.append(copy)
+                theirs = block(outs[layer], moved(at, axis, -by), done, row, count)
+                got.append(
+                    pltpu.make_async_remote_copy(
+                        theirs, theirs, send_sem.at[sem], recv_sem.at[sem],
+                        device_id=(number(to),), device_id_type=MESH,
+                    )
+                )
+            pending[chain] = got
+    for chain in chains:
+        for copy in pending.pop(chain):
+            copy.wait_recv()
+    for copy in sent:
+        copy.wait_send()
+
+
+def gather(att, up, down, stem, q, pin):
+    shape = jax.ShapeDtypeStruct((4, 2, 2, 2, ROWS, D), BF16)
+    any_spec = pl.BlockSpec(memory_space=pl.ANY)
+    return pl.pallas_call(
+        gather_kernel,
+        out_shape=[shape, shape],
+        in_specs=[any_spec] * 6,
+        out_specs=[any_spec] * 2,
+        scratch_shapes=[
+            pltpu.SemaphoreType.DMA((LAYERS, 9)),
+            pltpu.SemaphoreType.DMA((8, 4, 3)),
+            pltpu.SemaphoreType.DMA((8, 4, 3)),
+        ],
+        compiler_params=pltpu.CompilerParams(collective_id=0, has_side_effects=True),
+    )(att, up, down, stem, q, pin)
+
+
+def scatter_kernel(
+    g0, g1, s0, s1, att, up, down, stem, q, pin, small,
+    acc0, acc1, rc0, rc1, rx0, rx1, ry0, ry1, rz0, rz1, sm, smr, smz,
+    send_sem, recv_sem, ssend, srecv,
+):
+    at = place()
+    grads = (g0, g1)
+    accs = (acc0, acc1)
+    lands = {"c": (rc0, rc1), "x": (rx0, rx1), "y": (ry0, ry1), "z": (rz0, rz1)}
+    greet(at)
+    chains = [(layer, s) for layer in (1, 0) for s in range(len(STREAMS))]
+    sent = []
+
+    def start(chain, phase):
+        layer, s = chain
+        row, count, order = STREAMS[s]
+        order = ("c",) + order[::-1]
+        axis = order[phase]
+        left = [a for a in AXES if a not in order[: phase + 1]]
+        source = grads[layer] if phase == 0 else accs[layer]
+        got = []
+        for by in range(1, SIZES[axis]):
+            to = moved(at, axis, by)
+            index = []
+            for a in AXES:
+                if a == "c" and phase > 0:
+                    continue
+                if a == axis:
+                    index.append(to[a])
+                else:
+                    index.append(pl.ds(0, SIZES[a]) if a in left else at[a])
+            src = source.at[tuple(index) + (pl.ds(row, count), slice(None))]
+            index = [] if axis != "z" else [by - 1]
+            for a in AXES:
+                if a != axis and a != "c":
+                    index.append(pl.ds(0, SIZES[a]) if a in left else 0)
+            dst = lands[axis][layer].at[tuple(index) + (pl.ds(row, count), slice(None))]
+            sem = (layer * 4 + s, AXES.index(axis), by - 1)
+            copy = pltpu.make_async_remote_copy(
+                src, dst, send_sem.at[sem], recv_sem.at[sem],
+                device_id=(number(to),), device_id_type=MESH,
+            )
+            copy.start()
+            sent.append(copy)
+            got.append(copy)
+        return got
+
+    def add(chain, phase):
+        layer, s = chain
+        row, count, order = STREAMS[s]
+        order = ("c",) + order[::-1]
+        axis = order[phase]
+        left = [a for a in AXES if a not in order[: phase + 1]]
+        source = grads[layer] if phase == 0 else accs[layer]
+        acc, land = accs[layer], lands[axis][layer]
+        rows = pl.ds(row, count)
+        total = 1
+        for a in left:
+            total *= SIZES[a]
+
+        def one(i, carry):
+            spot = dict(at)
+            lspot = {"z": 0, "y": 0, "x": 0}
+            rest = i
+            for a in left[::-1]:
+                spot[a] = rest % SIZES[a]
+                lspot[a] = spot[a]
+                rest = rest // SIZES[a]
+            keep = (spot["z"], spot["y"], spot["x"])
+            mine = source[keep + ((at["c"],) if phase == 0 else ()) + (rows, slice(None))]
+            value = mine.astype(F32)
+            for by in range(1, SIZES[axis]):
+                index = () if axis != "z" else (by - 1,)
+                index += tuple(lspot[a] for a in AXES if a != axis and a != "c")
+                value = value + land[index + (rows, slice(None))].astype(F32)
+            if phase < 3:
+                acc[keep + (rows, slice(None))] = value.astype(BF16)
+            else:
+                finish_rows(layer, s, value)
+            return carry
+
+        if total == 1:
+            one(0, 0)
+        else:
+            lax.fori_loop(0, total, one, 0)
+
+    def finish_rows(layer, s, value):
+        if s < 2:
+            for j in range(2):
+                col = (2 * s + j) * D
+                stem[layer, :, col : col + D] = value[j * D : (j + 1) * D]
+        elif s == 2:
+            q[layer] = value[:SQ]
+            pin[layer] = value[SQ:]
+        else:
+            att[layer] = value[0:16]
+            up[layer] = value[16:32]
+            down[layer] = value[32:48]
+
+    smalls = ("c", "x", "y", "z")
+
+    def small_start(phase):
+        axis = smalls[phase]
+        for by in range(1, SIZES[axis]):
+            to = moved(at, axis, by)
+            dst = smr.at[phase] if axis != "z" else smz.at[at["z"]]
+            sem = (phase, by - 1)
+            copy = pltpu.make_async_remote_copy(
+                sm.at[phase], dst, ssend.at[sem], srecv.at[sem],
+                device_id=(number(to),), device_id_type=MESH,
+            )
+            copy.start()
+            sent.append(copy)
+
+    def small_land(phase):
+        axis = smalls[phase]
+        for by in range(1, SIZES[axis]):
+            src = moved(at, axis, -by)
+            dst = smr.at[phase] if axis != "z" else smz.at[src["z"]]
+            sem = (phase, by - 1)
+            pltpu.make_async_remote_copy(
+                sm.at[phase], dst, ssend.at[sem], srecv.at[sem],
+                device_id=(number(moved(at, axis, by)),), device_id_type=MESH,
+            ).wait_recv()
+        if axis != "z":
+            sm[phase + 1] = sm[phase] + smr[phase]
+        else:
+            smz[at["z"]] = sm[phase]
+            small[...] = (smz[0] + smz[1]) + (smz[2] + smz[3])
+
+    pending = {chain: start(chain, 0) for chain in chains}
+    sm[0, 0] = s0[...]
+    sm[0, 1] = s1[...]
+    small_start(0)
+    for phase in range(4):
+        for chain in chains:
+            for copy in pending.pop(chain):
+                copy.wait_recv()
+            add(chain, phase)
+            if phase < 3:
+                pending[chain] = start(chain, phase + 1)
+        small_land(phase)
+        if phase < 3:
+            small_start(phase + 1)
+    for copy in sent:
+        copy.wait_send()
+
+
+def scatter(g0, g1, s0, s1):
+    def out(*shape):
+        return jax.ShapeDtypeStruct(shape, F32)
+
+    vmem = pl.BlockSpec(memory_space=pltpu.VMEM)
+    lead = (4, 2, 2, 2, ROWS, D)
+    scratch = []
+    for shape in ((4, 2, 2), (4, 2, 2), (4, 2), (4, 2), (3, 2, 2)):
+        scratch += [pltpu.VMEM(shape + (ROWS, D), BF16)] * 2
+    return pl.pallas_call(
+        scatter_kernel,
+        out_shape=[
+            out(LAYERS, 16, D), out(LAYERS, 16, D), out(LAYERS, 16, D), out(LAYERS, D, 4 * D),
+            out(LAYERS, SQ, D), out(LAYERS, PROP, D), out(LAYERS, SMALL, D),
+        ],
+        in_specs=[vmem] * 4,
+        out_specs=[vmem] * 7,
+        scratch_shapes=scratch
+        + [
+            pltpu.VMEM((4, LAYERS, SMALL, D), F32),
+            pltpu.VMEM((3, LAYERS, SMALL, D), F32),
+            pltpu.VMEM((4, LAYERS, SMALL, D), F32),
+            pltpu.SemaphoreType.DMA((8, 4, 3)),
+            pltpu.SemaphoreType.DMA((8, 4, 3)),
+            pltpu.SemaphoreType.DMA((4, 3)),
+            pltpu.SemaphoreType.DMA((4, 3)),
+        ],
+        compiler_params=pltpu.CompilerParams(
+            collective_id=1, has_side_effects=True, vmem_limit_bytes=VMEM_LIMIT
+        ),
+    )(g0.reshape(lead), g1.reshape(lead), s0, s1)
+
+
+def pack(attn, up, down, stem, queries, pin):
     gathered = [lax.all_gather(a, "fsdp", axis=1, tiled=True) for a in (attn, up, down, stem, queries, pin)]
     attn, up, down, stem, queries, pin = gathered
     stem = stem.reshape(LAYERS, STEMS, D, 4, D).transpose(0, 1, 3, 2, 4).reshape(LAYERS, STEMS, 4 * D, D)
@@ -485,31 +785,29 @@
 
 def body(n, tokens, features, proprio, embodiment, trunk_attn, feedforward_up_weight, mlp_down,
          stem_mats, stem_queries, prop_in, trunk_vectors, mlp_bias, stem_bias, cotangent):
-    if n == STEMS:
-        stem = stem_mats.reshape(LAYERS, D, 4, D).transpose(0, 2, 1, 3).reshape(LAYERS, 4 * D, D)
-        packed = jnp.concatenate(
-            [stem, stem_queries, prop_in, trunk_attn, feedforward_up_weight, mlp_down], 1
-        )
-        w = lax.all_gather(packed, "fsdp", axis=1)
-    else:
-        w = pack(trunk_attn, feedforward_up_weight, mlp_down, stem_mats, stem_queries, prop_in, n)
+    shards = (trunk_attn, feedforward_up_weight, mlp_down, stem_mats, stem_queries, prop_in)
     vecs = trunk_vectors.astype(F32)
     mbs = mlp_bias.astype(F32).reshape(LAYERS, 1, FF)
     sbs = stem_bias.astype(F32)
+    if n == 32:
+        w0, w1 = (w.reshape(STEMS, ROWS, D) for w in gather(*shards))
+    else:
+        w0, w1 = pack(*shards)
     out, gtok, gfeat, gprop, g0, g1 = compute(
-        tokens, features, proprio, embodiment, w[0], w[1], vecs, mbs, sbs, cotangent, F32
-    )
-    grads = jnp.stack([g0[0], g1[0]])
-    if n == STEMS:
-        mine = lax.psum_scatter(grads, "fsdp", scatter_dimension=1, tiled=True)
-        mats = [a[:, 0] for a in unpack_blocks(mine)]
+        tokens, features, proprio, embodiment, w0, w1, vecs, mbs, sbs, cotangent, BF16
+    )
+    if n == 32:
+        *mats, small = scatter(g0[0], g1[0], g0[1], g1[1])
     else:
         mats = [
             lax.psum_scatter(a.reshape(LAYERS, -1, a.shape[-1]), "fsdp", scatter_dimension=1, tiled=True)
-            for a in unpack_blocks(grads)
+            for a in unpack_blocks(jnp.stack([g0[0], g1[0]]).astype(F32))
         ]
-    small = lax.psum(tuple(jnp.stack([a, b]) for a, b in zip(g0[1:], g1[1:])), "fsdp")
-    return (out, gtok, gfeat, gprop, *mats, small[0], small[1].reshape(LAYERS, FF), small[2])
+        small = lax.psum(jnp.stack([g0[1], g1[1]]), "fsdp")
+    gvec = small[:, :8]
+    gmb = small[:, 8:12].reshape(LAYERS, FF)
+    gsb = jnp.swapaxes(small[:, 16:].reshape(LAYERS, 2, STEMS, D), 1, 2)
+    return (out, gtok, gfeat, gprop, *mats, gvec, gmb, gsb)
 
 
 def solution(mesh):

time: 661 us -> 372 us (0.56)
  waiting for transfers between devices: 352 us -> 0 us
  Pallas kernels: 201 us -> 348 us
  blocking collectives: 41.4 us -> 0 us
  other arithmetic: 18.1 us -> 2.31 us
  between operations: 14.2 us -> 0.73 us
  local copies, waits for them, and re-layouts: 32.5 us -> 20.4 us
    unnamed x3 -> x0, waiting for transfers between devices: 272 us -> none
    pallas_call x0 -> x2, Pallas kernels: none -> 150 us  [the longest x1 76.9 us: scatter(): pl.pallas_call(scatter_kernel, out_shape=[out(LAYERS, 16, D), out(LAYERS,...]
    all_gather x1 -> x0, waiting for transfers between devices: 80.1 us -> none  [body(): w = lax.all_gather(packed, 'fsdp', axis=1)]
    psum x1 -> x0, blocking collectives: 41.4 us -> none  [body(): lax.psum(tuple((jnp.stack([a, b]) for a, b in zip(g0[1:], g1[1:]))), 'fsdp')]
    another operation x3 -> x0, other arithmetic: 16.6 us -> none  [the longest x1 15.1 us: body(): grads = jnp.stack([g0[0], g1[0]])]
    slice x2, local copies, waits for them, and re-layouts: 9.61 us -> 2.14 us  [the longest x1 1.29 us: body(): gvec = small[:, :8]]
    unnamed x28 -> x26, local copies, waits for them, and re-layouts: 15.2 us -> 15 us
  transfers between devices with their start and end apart: 2 -> 0, of which waited for: 2 -> 0; matrix products, arithmetic and copies ran while one was open for 2% -> 0% of each run, Pallas kernels for 0% -> 0%
where the time goes in v2:
time: 372 us
  Pallas kernels  348 us (94%)
  local copies, waits for them, and re-layouts  20.4 us (5%)
    pallas_call x3, Pallas kernels, call(): pl.pallas_call(kernel, grid_spec=pltpu.PrefetchScalarGridSpec(num_scalar_...  198 us
    pallas_call x1, Pallas kernels, scatter(): pl.pallas_call(scatter_kernel, out_shape=[out(LAYERS, 16, D), out(LAYERS,...  76.9 us
    pallas_call x1, Pallas kernels, gather(): pl.pallas_call(gather_kernel, out_shape=[shape, shape], in_specs=[any_spe...  73.5 us
    unnamed x26, local copies, waits for them, and re-layouts  15 us

profile of v2, /device:TPU:0, one launch (start us, length us, event | category | flops | bytes accessed | tf_op | source)
XLA Modules:
  0.0 371.6 jit_solution(7841901616559072227)
XLA Ops:
  0.6 1.3 fusion
  2.0 0.7 convert_element_type.12
  2.7 0.6 slice_bitcast_fusion.2
  3.3 0.8 copy.27
  4.1 0.8 convert_element_type.14
  4.9 0.6 slice_bitcast_fusion
  5.5 0.8 pad_convert_fusion.prop_ref
  6.3 2.9 copy.28.feat_ref
  9.3 73.5 %shard_map.237 = (bf16[4,2,2,2,608,128]{5,4,3,2,1,0:T(8,128)(2,1)}, bf16[4,2,2,2,608,128]{5,4,3,2,1,0:T(8,128)(2,1)}) custom-call(bf16[2,16,128]{2,1,0:T(8,128)(2,1)} %att.1, bf16[2,16,128]{2,1,0:T(8,128)(2,1)} %up.1, bf16[2,16,128]{2,1,0:T(8,128)(2,1)} %down.1, bf16[2,128,512]{2,1,0:T(8,128)(2,1)} %stem.1, bf16[2,16,128]{2,1,0:T(8,128)(2,1)} %q.1, ...), custom_call_target="tpu_custom_call" | custom-call | tf_op jit(solution)/shard_map/pallas_call | solution.py:573
  82.8 29.8 %shard_map.238 = (f32[2048,128]{1,0:T(8,128)}, bf16[64,128,128]{2,1,0:T(8,128)(2,1)}, bf16[64,128,256]{2,1,0:T(8,128)(2,1)}, bf16[64,128,128]{2,1,0:T(8,128)(2,1...) custom-call(s32[64]{0:T(128)} %emb_ref.5, ...), custom_call_target="tpu_custom_call" | custom-call | tf_op jit(solution)/shard_map/pallas_call | solution.py:417
  112.6 95.1 %shard_map.239 = (bf16[2048,128]{1,0:T(8,128)(2,1)}, f32[2048,128]{1,0:T(8,128)}, bf16[64,128,128]{2,1,0:T(8,128)(2,1)}, f32[64,16,32]{2,1,0:T(8,128)}, bf16[32,...) custom-call(s32[64]{0:T(128)} %emb_ref.5, f32[2048,128]{1,0:T(8,128)} %get-tuple-element.48.hid_ref, ...), custom_call_target="tpu_custom_call" | custom-call | tf_op jit(solution)/shard_map/pallas_call | solution.py:417
  207.7 72.9 %shard_map.240 = (f32[2048,128]{1,0:T(8,128)}, f32[64,2,49,128]{3,2,1,0:T(8,128)}, f32[64,2,32]{2,1,0:T(2,128)}, bf16[32,608,128]{2,1,0:T(8,128)(2,1)}, f32[80,128]{1,0:T(8,128)}) custom-call(s32[64]{0:T(128)} %emb_ref.5, f32[2048,128]{1,0:T(8,128)} %get-tuple-element.51.grad_ref, f32[64,16,32]{2,1,0:T(8,128)} %pad_convert_fusion.prop_ref, ...), custom_call_target="tpu_custom_call" | custom-call | tf_op jit(solution)/shard_map/pallas_call | solution.py:417
  280.6 0.0 copy-start.1
  280.6 76.9 %shard_map.241 = (f32[2,16,128]{2,1,0:T(8,128)}, f32[2,16,128]{2,1,0:T(8,128)}, f32[2,16,128]{2,1,0:T(8,128)}, f32[2,128,512]{2,1,0:T(8,128)}, f32[2,16,128]{2,1...) custom-call(bf16[4,2,2,2,608,128]{5,4,3,2,1,0:T(8,128)(2,1)} %bitcast.28, ...), custom_call_target="tpu_custom_call" | custom-call | tf_op jit(solution)/shard_map/pallas_call | solution.py:744
  357.4 0.7 slice_bitcast_fusion.4
  358.1 0.6 copy.37
  358.7 1.3 slice.36
  360.0 0.8 slice.38
  360.9 0.7 copy.36
  361.6 0.0 copy-done.1
  361.6 0.7 copy.32
  362.3 0.0 copy-start.3
  362.3 0.0 copy-start.2
  362.3 5.4 %copy.31 = f32[64,2,49,128]{3,1,2,0:T(2,128)} copy(f32[64,2,49,128]{3,2,1,0:T(8,128)} %get-tuple-element.83) | data formatting | bytes 6422528
  367.7 0.0 copy-done.6
  367.7 0.6 copy.44
  368.3 0.0 copy-done.5
  368.3 0.6 copy.45
  368.9 0.6 copy.46
  369.5 0.8 copy.47
  370.3 0.6 copy.48
  370.9 0.6 copy.49
  (8 shorter events, 0.0 us)
Async XLA Ops:
  280.6 81.0 %copy-start.1 = (f32[64,2,32]{2,1,0:T(2,128)S(1)}, f32[64,2,32]{2,1,0:T(2,128)}, u32[]{:S(2)}) copy-start(f32[64,2,32]{2,1,0:T(2,128)} %get-tuple-element.84) | copy-start | bytes 49156
  362.3 5.5 %copy-start.6 = (f32[2,16,128]{2,1,0:T(8,128)S(1)}, f32[2,16,128]{2,1,0:T(8,128)}, u32[]{:S(2)}) copy-start(f32[2,16,128]{2,1,0:T(8,128)} %get-tuple-element.117) | copy-start | bytes 49156
  362.3 6.1 %copy-start.5 = (f32[2,16,128]{2,1,0:T(8,128)S(1)}, f32[2,16,128]{2,1,0:T(8,128)}, u32[]{:S(2)}) copy-start(f32[2,16,128]{2,1,0:T(8,128)} %get-tuple-element.118) | copy-start | bytes 49156
  362.3 6.7 %copy-start.4 = (f32[2,16,128]{2,1,0:T(8,128)S(1)}, f32[2,16,128]{2,1,0:T(8,128)}, u32[]{:S(2)}) copy-start(f32[2,16,128]{2,1,0:T(8,128)} %get-tuple-element.119) | copy-start | bytes 49156
  362.3 7.3 %copy-start = (f32[2,128,512]{2,1,0:T(8,128)S(1)}, f32[2,128,512]{2,1,0:T(8,128)}, u32[]{:S(2)}) copy-start(f32[2,128,512]{2,1,0:T(8,128)} %get-tuple-element.120) | copy-start | bytes 1572868
  362.3 8.1 %copy-start.3 = (f32[2,16,128]{2,1,0:T(8,128)S(1)}, f32[2,16,128]{2,1,0:T(8,128)}, u32[]{:S(2)}) copy-start(f32[2,16,128]{2,1,0:T(8,128)} %get-tuple-element.121) | copy-start | bytes 49156
  362.3 8.7 %copy-start.2 = (f32[2,32,128]{2,1,0:T(8,128)S(1)}, f32[2,32,128]{2,1,0:T(8,128)}, u32[]{:S(2)}) copy-start(f32[2,32,128]{2,1,0:T(8,128)} %get-tuple-element.122) | copy-start | bytes 98308

commit v3 on v2

--- a/solution.py
+++ b/solution.py
@@ -14,14 +14,14 @@
 FF = 512
 SQ = 16
 FR = 49
-CR = 64
+CR = 112
 PROP = 32
 PR = 16
 STEMS = 32
 STEPS = 2
 LAYERS = 2
 TOK = 32
-SB = 8
+SB = 16
 
 R_Q = 4 * D
 R_PIN = R_Q + SQ
@@ -90,16 +90,49 @@
     return jnp.sum(x.reshape(x.shape[0] // 8, 8, x.shape[1]), 0)
 
 
+def slot(w_ref, e, start, stop):
+    if len(w_ref.shape) == 3:
+        return w_ref[e, start:stop, :]
+    return w_ref[e // 8, (e // 4) % 2, (e // 2) % 2, e % 2, start:stop, :]
+
+
+def all_slots(w_ref, start, stop):
+    index = (slice(None),) * (len(w_ref.shape) - 2)
+    return w_ref[index + (slice(start, stop), slice(None))].reshape(STEMS * (stop - start), D)
+
+
 def trunk_weights(w_ref):
-    attn = w_ref[:, R_ATT:R_UP, :].reshape(4 * D, D)
-    up = w_ref[:, R_UP:R_DOWN, :].reshape(FF, D)
-    down = w_ref[:, R_DOWN:ROWS, :].reshape(FF, D)
+    attn = all_slots(w_ref, R_ATT, R_UP)
+    up = all_slots(w_ref, R_UP, R_DOWN)
+    down = all_slots(w_ref, R_DOWN, ROWS)
     wqkv = jnp.concatenate([attn[:D], attn[D : 2 * D], attn[2 * D : 3 * D]], 1)
     return wqkv, attn[3 * D :], up, down
 
 
 def stem_kv_weight(w_ref, e):
-    return jnp.concatenate([w_ref[e, 0:D, :], w_ref[e, D : 2 * D, :]], 1)
+    return jnp.concatenate([slot(w_ref, e, 0, D), slot(w_ref, e, D, 2 * D)], 1)
+
+
+def step_reduce(x, op):
+    x = x.reshape(x.shape[0] // 8, 8, x.shape[1])
+    out = x[0]
+    for i in range(1, x.shape[0]):
+        out = op(out, x[i])
+    out = op(out, pltpu.roll(out, 4, 0))
+    return op(out, pltpu.roll(out, 2, 0))
+
+
+def step_apply(x, y, op):
+    return op(x.reshape(x.shape[0] // 8, 8, x.shape[1]), y[None]).reshape(x.shape)
+
+
+def step_masks():
+    odd = lax.broadcasted_iota(jnp.int32, (CR, D), 0) % 2
+    return (odd == 0).astype(BF16), odd.astype(BF16)
+
+
+def split_steps(p, masks):
+    return jnp.concatenate([p * masks[0], p * masks[1]], 1)
 
 
 def softmax_rows(score):
@@ -108,55 +141,52 @@
     return weight * (1.0 / jnp.sum(weight, 0, keepdims=True))
 
 
-def forward_block(es, hidden, feat_ref, prop_ref, w_ref, vec, mb, sb_ref):
+def forward_block(es, hidden, feat_ref, props, w_ref, vec, mb, sb):
     kept = {}
     pre = [
-        dot(prop_ref[j].astype(BF16), w_ref[e, R_PIN:R_ATT, :]) + sb_ref[e, 0:1, :]
+        dot(props[j * PR : (j + 1) * PR], slot(w_ref, e, R_PIN, R_ATT))
+        + sb(e)[0:1, :]
         for j, e in enumerate(es)
     ]
     pact, pslope = gelu_parts(jnp.concatenate(pre, 0))
     pact = pact.astype(BF16)
     kept["pact"], kept["pslope"] = pact, pslope
-    row16 = lax.broadcasted_iota(jnp.int32, (16, D), 0)
+    row16 = lax.broadcasted_iota(jnp.int32, (PR, D), 0)
+    prows = [
+        dot(pact[j * PR : (j + 1) * PR], slot(w_ref, e, 3 * D, 4 * D)) + sb(e)[1:2, :]
+        for j, e in enumerate(es)
+    ]
     contexts = []
-    for j, e in enumerate(es):
-        prow = dot(pact[j * PR : (j + 1) * PR], w_ref[e, 3 * D : 4 * D, :]) + sb_ref[e, 1:2, :]
-        parts = []
-        for t in range(STEPS):
-            last = feat_ref[j, t, 48:49, :].astype(F32)
-            tail = jnp.where(row16 == 0, last, jnp.where(row16 == 1, prow[t : t + 1], 0.0))
-            parts += [feat_ref[j, t, 0:48, :], tail.astype(BF16)]
-        contexts.append(jnp.concatenate(parts, 0))
+    for j in range(SB):
+        rows = feat_ref[j * STEPS * FR : (j + 1) * STEPS * FR, :]
+        last = jnp.concatenate([rows[96:98], jnp.zeros((14, D), BF16)], 0).astype(F32)
+        tail = jnp.where(row16 < 2, last, jnp.where(row16 < 4, prows[j], 0.0))
+        contexts.append(jnp.concatenate([rows[:96], tail.astype(BF16)], 0))
     kept["ctx"] = contexts
     kvs = [dot(contexts[j], stem_kv_weight(w_ref, e)).astype(BF16) for j, e in enumerate(es)]
     kept["kv"] = kvs
     mask16 = head_mask(SQ, 0.25)
     scores = [
-        dot_nt(kvs[j][:, :D], expand(w_ref[e, R_Q:R_PIN, :], mask16)) for j, e in enumerate(es)
-    ]
-    row8 = lax.broadcasted_iota(jnp.int32, (56, D), 0)
+        dot_nt(kvs[j][:, :D], expand(slot(w_ref, e, R_Q, R_PIN), mask16)) for j, e in enumerate(es)
+    ]
+    valid = lax.broadcasted_iota(jnp.int32, (104, D), 0) < STEPS * (FR + 1)
     pad = jnp.zeros((8, D), F32)
     probs = []
     for j in range(SB):
-        parts = []
-        for t in range(STEPS):
-            s = scores[j][t * CR : t * CR + 56]
-            parts += [softmax_rows(jnp.where(row8 < FR + 1, s, -1e30)), pad]
-        probs.append(jnp.concatenate(parts, 0))
+        s = jnp.where(valid, scores[j][:104], -1e30)
+        weight = jnp.exp(step_apply(s, step_reduce(s, jnp.maximum), jnp.subtract))
+        scale = 1.0 / step_reduce(weight, jnp.add)
+        probs.append(jnp.concatenate([step_apply(weight, scale, jnp.multiply), pad], 0))
     kept["prob"] = probs
+    masks = step_masks()
     mixes = []
     for j in range(SB):
-        low = probs[j].astype(BF16)
-        mixes += [
-            contract(
-                dot_tn(low[t * CR : (t + 1) * CR], kvs[j][t * CR : (t + 1) * CR, D:]), SQ
-            ).astype(BF16)
-            for t in range(STEPS)
-        ]
+        wide = dot_tn(split_steps(probs[j].astype(BF16), masks), kvs[j][:, D:])
+        mixes += [contract(wide[t * D : (t + 1) * D], SQ).astype(BF16) for t in range(STEPS)]
     mix = jnp.concatenate(mixes, 0)
     kept["mix"] = mix
     outs = [
-        dot(mix[j * TOK : (j + 1) * TOK], w_ref[e, 2 * D : 3 * D, :]) for j, e in enumerate(es)
+        dot(mix[j * TOK : (j + 1) * TOK], slot(w_ref, e, 2 * D, 3 * D)) for j, e in enumerate(es)
     ]
     first = hidden + jnp.concatenate(outs, 0)
     kept["first"] = first
@@ -166,13 +196,13 @@
     qkv = (dot(normed, wqkv) + bias).astype(BF16)
     kept["qkv"] = qkv
     mask32 = head_mask(TOK, 0.25)
-    sprobs = []
-    smixes = []
-    for j in range(SB):
-        rows = qkv[j * TOK : (j + 1) * TOK]
-        p = softmax_rows(dot_nt(rows[:, D : 2 * D], expand(rows[:, :D], mask32)))
-        sprobs.append(p)
-        smixes.append(contract(dot_tn(p.astype(BF16), rows[:, 2 * D :]), TOK).astype(BF16))
+    rows = [qkv[j * TOK : (j + 1) * TOK] for j in range(SB)]
+    scores = [dot_nt(rows[j][:, D : 2 * D], expand(rows[j][:, :D], mask32)) for j in range(SB)]
+    sprobs = [softmax_rows(s) for s in scores]
+    smixes = [
+        contract(dot_tn(sprobs[j].astype(BF16), rows[j][:, 2 * D :]), TOK).astype(BF16)
+        for j in range(SB)
+    ]
     kept["sprob"] = sprobs
     smix = jnp.concatenate(smixes, 0)
     kept["smix"] = smix
@@ -185,7 +215,7 @@
     return second + (dot(act, down) + vec[7:8]), kept
 
 
-def backward_block(es, grad, kept, prop_ref, w_ref, vec, acc):
+def backward_block(es, grad, kept, props, w_ref, vec, acc):
     wqkv, wout, up, down = trunk_weights(w_ref)
     out_low = grad.astype(BF16)
     acc["vec"][7] += fold(out_low.astype(F32))
@@ -206,17 +236,16 @@
     grad_mix = dot_nt(branch, wout).astype(BF16)
     mask32 = head_mask(TOK, 0.25)
     mask32_one = head_mask(TOK, 1.0)
-    grads_q, grads_k, grads_v = [], [], []
+    rows = [kept["qkv"][j * TOK : (j + 1) * TOK] for j in range(SB)]
+    wides = [expand(grad_mix[j * TOK : (j + 1) * TOK], mask32_one) for j in range(SB)]
+    grad_ps = [dot_nt(rows[j][:, 2 * D :], wides[j]) for j in range(SB)]
+    grads_v = [dot(kept["sprob"][j].astype(BF16), wides[j]) for j in range(SB)]
+    gss = []
     for j in range(SB):
-        rows = kept["qkv"][j * TOK : (j + 1) * TOK]
-        p = kept["sprob"][j]
-        wide = expand(grad_mix[j * TOK : (j + 1) * TOK], mask32_one)
-        grad_p = dot_nt(rows[:, 2 * D :], wide)
-        grads_v.append(dot(p.astype(BF16), wide))
-        p = p.astype(F32)
-        gs = (p * (grad_p - jnp.sum(grad_p * p, 0, keepdims=True))).astype(BF16)
-        grads_q.append(contract(dot_tn(gs, rows[:, D : 2 * D]), TOK) * 0.25)
-        grads_k.append(dot(gs, expand(rows[:, :D], mask32)))
+        p = kept["sprob"][j].astype(F32)
+        gss.append((p * (grad_ps[j] - jnp.sum(grad_ps[j] * p, 0, keepdims=True))).astype(BF16))
+    grads_q = [contract(dot_tn(gss[j], rows[j][:, D : 2 * D]), TOK) * 0.25 for j in range(SB)]
+    grads_k = [dot(gss[j], expand(rows[j][:, :D], mask32)) for j in range(SB)]
     grad_qkv = jnp.concatenate(
         [jnp.concatenate(g, 0).astype(BF16) for g in (grads_q, grads_k, grads_v)], 1
     )
@@ -233,51 +262,59 @@
     mask16 = head_mask(SQ, 0.25)
     mask16_one = head_mask(SQ, 1.0)
     row16 = lax.broadcasted_iota(jnp.int32, (PR, D), 0)
-    grad_contexts, grad_props = [], []
+    gs_in = [stem_grad[j * TOK : (j + 1) * TOK] for j in range(SB)]
+    gmixes = [dot_nt(gs_in[j], slot(w_ref, e, 2 * D, 3 * D)).astype(BF16) for j, e in enumerate(es)]
+    grad_wo = [dot_tn(kept["mix"][j * TOK : (j + 1) * TOK], gs_in[j]) for j in range(SB)]
+    kvs = [kept["kv"][j] for j in range(SB)]
+    probs = [kept["prob"][j] for j in range(SB)]
+    wides = [
+        jnp.concatenate(
+            [expand(gmixes[j][t * SQ : (t + 1) * SQ], mask16_one) for t in range(STEPS)], 0
+        )
+        for j in range(SB)
+    ]
+    grad_ps = [dot_nt(kvs[j][:, D:], wides[j]) for j in range(SB)]
+    masks = step_masks()
+    gvs = [dot(split_steps(probs[j].astype(BF16), masks), wides[j]) for j in range(SB)]
+    even = lax.broadcasted_iota(jnp.int32, (104, D), 0) % 2 == 0
+    pad = jnp.zeros((8, D), F32)
+    gss = []
+    for j in range(SB):
+        p = probs[j][:104].astype(F32)
+        gp = jnp.where(even, grad_ps[j][:104, :D], grad_ps[j][:104, D:])
+        gs = p * step_apply(gp, step_reduce(gp * p, jnp.add), jnp.subtract)
+        gss.append(jnp.concatenate([gs, pad], 0).astype(BF16))
+    gks = [dot(gss[j], expand(slot(w_ref, e, R_Q, R_PIN), mask16)) for j, e in enumerate(es)]
+    gkvs = [
+        jnp.concatenate([gks[j], gvs[j]], 1).astype(BF16) for j in range(SB)
+    ]
+    grad_contexts = [
+        dot_nt(gkvs[j], stem_kv_weight(w_ref, e)).astype(BF16) for j, e in enumerate(es)
+    ]
+    prows = [
+        jnp.where((row16 == 2) | (row16 == 3), grad_contexts[j][96:112].astype(F32), 0.0)
+        for j in range(SB)
+    ]
+    prow_low = [p.astype(BF16) for p in prows]
+    gpacts = [dot_nt(prow_low[j], slot(w_ref, e, 3 * D, 4 * D)) for j, e in enumerate(es)]
+    gppres = [
+        (gpacts[j] * kept["pslope"][j * PR : (j + 1) * PR]).astype(BF16) for j in range(SB)
+    ]
+    grad_props = [dot_nt(gppres[j], slot(w_ref, e, R_PIN, R_ATT)) for j, e in enumerate(es)]
+    grad_q = [contract(dot_tn(gss[j], kvs[j][:, :D]), SQ) * 0.25 for j in range(SB)]
+    grad_wkv = [dot_tn(kept["ctx"][j], gkvs[j]) for j in range(SB)]
+    grad_wp = [dot_tn(kept["pact"][j * PR : (j + 1) * PR], prow_low[j]) for j in range(SB)]
+    grad_pin = [dot_tn(props[j * PR : (j + 1) * PR], gppres[j]) for j in range(SB)]
+    stem = acc["stem"]
     for j, e in enumerate(es):
-        g = stem_grad[j * TOK : (j + 1) * TOK]
-        grad_wo = dot_tn(kept["mix"][j * TOK : (j + 1) * TOK], g)
-        gmix = dot_nt(g, w_ref[e, 2 * D : 3 * D, :]).astype(BF16)
-        kv = kept["kv"][j]
-        p = kept["prob"][j]
-        p_low = p.astype(BF16)
-        p = p.astype(F32)
-        gss, gvs = [], []
-        for t in range(STEPS):
-            wide = expand(gmix[t * SQ : (t + 1) * SQ], mask16_one)
-            grad_p = dot_nt(kv[t * CR : (t + 1) * CR, D:], wide)
-            gvs.append(dot(p_low[t * CR : (t + 1) * CR], wide))
-            pt = p[t * CR : (t + 1) * CR]
-            gss.append(pt * (grad_p - jnp.sum(grad_p * pt, 0, keepdims=True)))
-        gs = jnp.concatenate(gss, 0).astype(BF16)
-        grad_q = contract(dot_tn(gs, kv[:, :D]), SQ) * 0.25
-        gk = dot(gs, expand(w_ref[e, R_Q:R_PIN, :], mask16))
-        gkv = jnp.concatenate([gk, jnp.concatenate(gvs, 0)], 1).astype(BF16)
-        grad_wkv = dot_tn(kept["ctx"][j], gkv)
-        grad_ctx = dot_nt(gkv, stem_kv_weight(w_ref, e)).astype(BF16)
-        grad_contexts.append(grad_ctx)
-        wide_ctx = grad_ctx.astype(F32)
-        prow = jnp.where(
-            row16 == 0,
-            wide_ctx[FR : FR + 1],
-            jnp.where(row16 == 1, wide_ctx[CR + FR : CR + FR + 1], 0.0),
-        )
-        prow_low = prow.astype(BF16)
-        pact = kept["pact"][j * PR : (j + 1) * PR]
-        grad_wp = dot_tn(pact, prow_low)
-        gpact = dot_nt(prow_low, w_ref[e, 3 * D : 4 * D, :])
-        gppre = (gpact * kept["pslope"][j * PR : (j + 1) * PR]).astype(BF16)
-        grad_pin = dot_tn(prop_ref[j].astype(BF16), gppre)
-        grad_props.append(dot_nt(gppre, w_ref[e, R_PIN:R_ATT, :]))
-        stem = acc["stem"]
-        stem[e, 0:D, :] += grad_wkv[:, :D]
-        stem[e, D : 2 * D, :] += grad_wkv[:, D:]
-        stem[e, 2 * D : 3 * D, :] += grad_wo
-        stem[e, 3 * D : 4 * D, :] += grad_wp
-        stem[e, R_Q:R_PIN, :] += grad_q
-        stem[e, R_PIN:R_ATT, :] += grad_pin
-        acc["sb"][0, pl.ds(e, 1), :] += jnp.sum(gppre.astype(F32), 0, keepdims=True)
-        acc["sb"][1, pl.ds(e, 1), :] += jnp.sum(prow, 0, keepdims=True)
+        stem[e, 0:D, :] += grad_wkv[j][:, :D]
+        stem[e, D : 2 * D, :] += grad_wkv[j][:, D:]
+        stem[e, 2 * D : 3 * D, :] += grad_wo[j]
+        stem[e, 3 * D : 4 * D, :] += grad_wp[j]
+        stem[e, R_Q:R_PIN, :] += grad_q[j]
+        stem[e, R_PIN:R_ATT, :] += grad_pin[j]
+        acc["sb"][pl.ds(2 * e, 1), :] += jnp.sum(gppres[j].astype(F32), 0, keepdims=True)
+        acc["sb"][pl.ds(2 * e + 1, 1), :] += jnp.sum(prows[j], 0, keepdims=True)
     return grad_first, grad_contexts, grad_props
 
 
@@ -287,7 +324,7 @@
 def acc_shapes():
     return [
         pltpu.VMEM((STEMS, STEM_ROWS, D), F32),
-        pltpu.VMEM((2, STEMS, D), F32),
+        pltpu.VMEM((2 * STEMS, D), F32),
         pltpu.VMEM((D, 3 * D), F32),
         pltpu.VMEM((D, D), F32),
         pltpu.VMEM((D, FF), F32),
@@ -321,8 +358,7 @@
     small_ref[8:16, :] = jnp.concatenate(
         [mb[:, i * D : (i + 1) * D] for i in range(4)] + [jnp.zeros((4, D), F32)], 0
     )
-    for i in range(2):
-        small_ref[16 + i * STEMS : 16 + (i + 1) * STEMS, :] = acc["sb"][i]
+    small_ref[16:SMALL, :] = acc["sb"][...]
 
 
 SAVED = ("ctx", "kv", "prob", "mix", "first", "qkv", "sprob", "smix", "second", "act", "slope", "pact", "pslope")
@@ -332,9 +368,9 @@
 def saved_shapes(samples):
     rows = samples * TOK
     return dict(
-        ctx=((samples, STEPS * CR, D), BF16),
-        kv=((samples, STEPS * CR, 2 * D), BF16),
-        prob=((samples, STEPS * CR, D), BF16),
+        ctx=((samples, CR, D), BF16),
+        kv=((samples, CR, 2 * D), BF16),
+        prob=((samples, CR, D), BF16),
         mix=((rows, D), BF16),
         first=((rows, D), F32),
         qkv=((rows, 3 * D), BF16),
@@ -348,11 +384,33 @@
     )
 
 
-def forward_kernel(emb_ref, tok_ref, feat_ref, prop_ref, w_ref, vec_ref, mb_ref, sb_ref, out_ref, *saved):
+def step_rows(step, samples):
+    shape = (SB * PR, STEPS * samples)
+    row = lax.broadcasted_iota(jnp.int32, shape, 0)
+    column = (row % PR - 2) * samples + step * SB + row // PR
+    held = (row % PR == 2) | (row % PR == 3)
+    return jnp.where(held & (lax.broadcasted_iota(jnp.int32, shape, 1) == column), 1.0, 0.0).astype(BF16)
+
+
+def prop_block(prop_ref, step):
+    both = jnp.concatenate([prop_ref[t] for t in range(STEPS)], 1)
+    return dot_nt(step_rows(step, prop_ref.shape[2]), both).astype(BF16)
+
+
+def layer_inputs(layer, vec_ref, mb_ref, sb_ref):
+    return (
+        vec_ref[layer].astype(F32), mb_ref[layer : layer + 1, :].astype(F32),
+        lambda e: sb_ref[layer, e].astype(F32),
+    )
+
+
+def forward_kernel(emb_ref, tok_ref, feat_ref, prop_ref, w_ref, vec_ref, mb_ref, sb_ref, out_ref, *rest):
+    saved = rest
     step = pl.program_id(0)
     es = [emb_ref[step * SB + j] for j in range(SB)]
     out, kept = forward_block(
-        es, tok_ref[...].astype(F32), feat_ref, prop_ref, w_ref, vec_ref[...], mb_ref[...], sb_ref
+        es, tok_ref[...].astype(F32), feat_ref, prop_block(prop_ref, step), w_ref,
+        *layer_inputs(0, vec_ref, mb_ref, sb_ref)
     )
     out_ref[...] = out
     for name, ref in zip(SAVED, saved):
@@ -369,37 +427,64 @@
 ):
     step = pl.program_id(0)
     acc = dict(zip(ACC, accs))
+
     pl.when(step == 0)(lambda: clear(acc))
+
     es = [emb_ref[step * SB + j] for j in range(SB)]
-    vec = vec_ref[...]
-    out, kept = forward_block(es, hid_ref[...], feat_ref, prop_ref, w_ref, vec, mb_ref[...], sb_ref)
+    vec, mb, sb = layer_inputs(1, vec_ref, mb_ref, sb_ref)
+    props = prop_block(prop_ref, step)
+    out, kept = forward_block(es, hid_ref[...], feat_ref, props, w_ref, vec, mb, sb)
     out_ref[...] = out.astype(BF16)
-    ghid, gctx, gprop = backward_block(
-        es, cot_ref[...].astype(F32), kept, prop_ref, w_ref, vec, acc
-    )
+    ghid, gctx, gprop = backward_block(es, cot_ref[...].astype(F32), kept, props, w_ref, vec, acc)
     ghid_ref[...] = ghid
     for j in range(SB):
         gfeat_ref[j] = gctx[j]
-        gprop_ref[j] = gprop[j]
+        gprop_ref[j * PR : (j + 1) * PR, :] = gprop[j]
     pl.when(step == pl.num_programs(0) - 1)(lambda: finish(acc, gw_ref, gsmall_ref))
 
 
 def backward_kernel(emb_ref, grad_ref, prop_ref, w_ref, vec_ref, gfeat1_ref, gprop1_ref, *rest):
-    saved = rest[: len(SAVED)]
-    gtok_ref, gfeat_ref, gprop_ref, gw_ref, gsmall_ref = rest[len(SAVED) : len(SAVED) + 5]
-    acc = dict(zip(ACC, rest[len(SAVED) + 5 :]))
+    n = len(SAVED)
+    saved = rest[:n]
+    gtok_ref, gfeat_ref, gprop_ref, gw_ref, gsmall_ref, gprops = rest[n : n + 6]
+    acc = dict(zip(ACC, rest[n + 6 :]))
     step = pl.program_id(0)
+
     pl.when(step == 0)(lambda: clear(acc))
+
     es = [emb_ref[step * SB + j] for j in range(SB)]
-    kept = {name: ref if name in PER_SAMPLE else ref[...] for name, ref in zip(SAVED, saved)}
-    ghid, gctx, gprop = backward_block(es, grad_ref[...], kept, prop_ref, w_ref, vec_ref[...], acc)
+    kept = {name: [ref[j] for j in range(SB)] if name in PER_SAMPLE else ref[...] for name, ref in zip(SAVED, saved)}
+    props = prop_block(prop_ref, step)
+    vec = vec_ref[0].astype(F32)
+    ghid, gctx, gprop = backward_block(es, grad_ref[...], kept, props, w_ref, vec, acc)
     gtok_ref[...] = ghid
-    for j in range(SB):
-        total = gctx[j].astype(F32) + gfeat1_ref[j].astype(F32)
-        for t in range(STEPS):
-            gfeat_ref[j, t] = total[t * CR : t * CR + FR]
-        gprop_ref[j] = (gprop[j] + gprop1_ref[j])[:STEPS]
-    pl.when(step == pl.num_programs(0) - 1)(lambda: finish(acc, gw_ref, gsmall_ref))
+    for j in range(0, SB, 4):
+        totals = [gctx[i].astype(F32) + gfeat1_ref[i].astype(F32) for i in range(j, j + 4)]
+        gfeat_ref[j * STEPS * FR : (j + 4) * STEPS * FR, :] = jnp.concatenate(
+            [total[: STEPS * FR] for total in totals], 0
+        )
+    add_proprio(jnp.concatenate(gprop, 0) + gprop1_ref[...], gprops, step)
+
+    @pl.when(step == pl.num_programs(0) - 1)
+    def _():
+        finish(acc, gw_ref, gsmall_ref)
+        write_proprio(gprops, gprop_ref)
+
+
+def add_proprio(rows, gprops, step):
+    place_ = step_rows(step, gprops.shape[1] // STEPS)
+    high = rows.astype(BF16)
+    rest = rows - high.astype(F32)
+    middle = rest.astype(BF16)
+    low = (rest - middle.astype(F32)).astype(BF16)
+    part = dot_tn(high, place_) + (dot_tn(middle, place_) + dot_tn(low, place_))
+    gprops[...] = jnp.where(step == 0, part, gprops[...] + part)
+
+
+def write_proprio(gprops, gprop_ref):
+    samples = gprop_ref.shape[2]
+    for t in range(STEPS):
+        gprop_ref[t] = gprops[:, t * samples : (t + 1) * samples]
 
 
 def blocked(shape, per_step):
@@ -430,50 +515,62 @@
     )(emb, *[a for a, _ in ins])
 
 
-def compute(tokens, features, proprio, emb, w0, w1, vecs, mbs, sbs, cot, wire):
+def compute(tokens, features, proprio, emb, shards, vecs, mbs, sbs, cot, weights=None):
     samples = emb.shape[0]
     steps = samples // SB
     rows = samples * TOK
     rb = SB * TOK
     tok = tokens.reshape(rows, D)
-    prop = jnp.pad(proprio.astype(F32), ((0, 0), (0, PR - STEPS), (0, 0)))
+    feat = jnp.swapaxes(features, 1, 2).reshape(samples * FR * STEPS, D)
+    prop = proprio.transpose(1, 2, 0)
+    fb = SB * FR * STEPS
     shapes = saved_shapes(samples)
     per = lambda s: s[0] // steps
-    saved_outs = [(shapes[n][0], shapes[n][1], per(shapes[n][0])) for n in SAVED]
-    res = call(
-        forward_kernel, steps, emb,
-        [(tok, rb), (features, SB), (prop, SB), (w0, 0), (vecs[0], 0), (mbs[0], 0), (sbs[0], 0)],
-        [((rows, D), F32, rb)] + saved_outs, [],
-    )
-    hidden, saved = res[0], res[1:]
-    grad_outs = [((STEMS, ROWS, D), wire, 0), ((SMALL, D), F32, 0)]
+    if weights is None:
+        hidden, saved, w0, w1 = gather_forward(tok, feat, prop, emb, vecs, mbs, sbs, shards)
+    else:
+        w0, w1 = weights
+        saved_outs = [(shapes[n][0], shapes[n][1], per(shapes[n][0])) for n in SAVED]
+        res = call(
+            forward_kernel, steps, emb,
+            [(tok, rb), (feat, fb), (prop, 0), (w0, 0), (vecs, 0), (mbs, 0), (sbs, 0)],
+            [((rows, D), F32, rb)] + saved_outs, [],
+        )
+        hidden, saved = res[0], res[1:]
+    grad_outs = [((STEMS, ROWS, D), BF16, 0), ((SMALL, D), F32, 0)]
     out, ghid, gfeat1, gprop1, *grads1 = call(
         middle_kernel, steps, emb,
-        [(hidden, rb), (features, SB), (prop, SB), (w1, 0), (vecs[1], 0), (mbs[1], 0), (sbs[1], 0),
+        [(hidden, rb), (feat, fb), (prop, 0), (w1, 0), (vecs, 0), (mbs, 0), (sbs, 0),
          (cot.reshape(rows, D), rb)],
-        [((rows, D), BF16, rb), ((rows, D), F32, rb), ((samples, STEPS * CR, D), BF16, SB),
-         ((samples, PR, PROP), F32, SB)] + grad_outs,
+        [((rows, D), BF16, rb), ((rows, D), F32, rb), ((samples, CR, D), BF16, SB),
+         ((samples * PR, PROP), F32, SB * PR)] + grad_outs,
         acc_shapes(),
     )
     gtok, gfeat, gprop, *grads0 = call(
         backward_kernel, steps, emb,
-        [(ghid, rb), (prop, SB), (w0, 0), (vecs[0], 0), (gfeat1, SB), (gprop1, SB)]
+        [(ghid, rb), (prop, 0), (w0, 0), (vecs, 0), (gfeat1, SB), (gprop1, SB * PR)]
         + [(a, per(a.shape)) for a in saved],
-        [((rows, D), F32, rb), ((samples, STEPS, FR, D), F32, SB), ((samples, STEPS, PROP), F32, SB)]
+        [((rows, D), F32, rb), ((samples * FR * STEPS, D), F32, fb), ((STEPS, PROP, samples), F32, 0)]
         + grad_outs,
-        acc_shapes(),
-    )
+        [pltpu.VMEM((PROP, STEPS * samples), F32)] + acc_shapes(),
+    )
+    gfeat = jnp.swapaxes(gfeat.reshape(samples, FR, STEPS, D), 1, 2)
     return (
-        out.reshape(tokens.shape), gtok.reshape(tokens.shape), gfeat, gprop, grads0, grads1
-    )
-
-
-STREAMS = (
-    (0, 256, ("z", "x", "y")),
-    (256, 256, ("z", "y", "x")),
-    (512, 48, ("x", "y", "z")),
-    (560, 48, ("y", "x", "z")),
-)
+        out.reshape(tokens.shape), gtok.reshape(tokens.shape), gfeat, gprop.transpose(2, 0, 1),
+        grads0, grads1
+    )
+
+
+def chunks_of(layer, bounds):
+    groups = []
+    for start, stop in zip(bounds[:-1], bounds[1:]):
+        half = (stop - start) // 32 * 16
+        groups.append(
+            [(layer, start, half, ("z", "x", "y")), (layer, start + half, stop - start - half, ("z", "y", "x"))]
+        )
+    return groups
+
+
 SIZES = {"z": 4, "y": 2, "x": 2, "c": 2}
 AXES = ("z", "y", "x", "c")
 MESH = pl.DeviceIdType.MESH
@@ -511,12 +608,66 @@
     return ref.at[index + (pl.ds(row, count), slice(None))]
 
 
-def gather_kernel(att, up, down, stem, q, pin, g0, g1, local_sem, send_sem, recv_sem):
-    at = place()
-    outs = (g0, g1)
-    locals_ = []
+class Gather:
+    def __init__(self, at, outs, groups, send_sem, recv_sem):
+        self.at, self.outs, self.groups = at, outs, groups
+        self.send_sem, self.recv_sem = send_sem, recv_sem
+
+    def copies(self, g, phase, arriving):
+        for i, (layer, row, count, order) in enumerate(self.groups[g]):
+            order = order + ("c",)
+            axis, done = order[phase], order[:phase]
+            for by in range(1, SIZES[axis]):
+                whose = moved(self.at, axis, -by) if arriving else self.at
+                ref = block(self.outs[layer], whose, done, row, count)
+                sem = (2 * g + i, AXES.index(axis), by - 1)
+                yield pltpu.make_async_remote_copy(
+                    ref, ref, self.send_sem.at[sem], self.recv_sem.at[sem],
+                    device_id=(number(moved(self.at, axis, by)),), device_id_type=MESH,
+                )
+
+    def start(self, g, phase):
+        for copy in self.copies(g, phase, False):
+            copy.start()
+
+    def land(self, g, phase):
+        for copy in self.copies(g, phase, True):
+            copy.wait_recv()
+
+    def run(self, moves):
+        for g, phase in moves:
+            if phase > 0:
+                self.land(g, phase - 1)
+            if phase < 4:
+                self.start(g, phase)
+
+    def close(self):
+        for g in range(len(self.groups)):
+            for phase in range(4):
+                for copy in self.copies(g, phase, False):
+                    copy.wait_send()
+
+
+BOUNDS = (0, 160, 320, 480, ROWS)
+GATHER_GROUPS = chunks_of(0, BOUNDS) + chunks_of(1, BOUNDS)
+GATHER_FIRST = (
+    (0, 0), (1, 0), (0, 1), (2, 0), (1, 1), (0, 2), (3, 0), (2, 1), (1, 2), (0, 3), (4, 0), (3, 1), (2, 2),
+    (1, 3), (5, 0), (0, 4), (3, 2), (2, 3), (1, 4), (6, 0), (3, 3), (7, 0), (2, 4), (3, 4),
+)
+GATHER_LATER = (
+    ((4, 1), (5, 1), (6, 1), (7, 1)),
+    ((4, 2), (5, 2)),
+    ((6, 2), (7, 2)),
+    ((4, 3), (5, 3)),
+    ((6, 3), (7, 3), (4, 4), (5, 4), (6, 4), (7, 4)),
+)
+
+
+def place_own(at, shards, outs, local_sem):
+    att, up, down, stem, q, pin = shards
+    copies = []
     for layer in range(LAYERS):
-        slot = outs[layer].at[at["z"], at["y"], at["x"], at["c"]]
+        own = outs[layer].at[at["z"], at["y"], at["x"], at["c"]]
         pieces = [
             (stem.at[layer, :, pl.ds(j * D, D)], j * D, D) for j in range(4)
         ] + [
@@ -524,68 +675,100 @@
             (up.at[layer], R_UP, 16), (down.at[layer], R_DOWN, 16),
         ]
         for i, (piece, row, count) in enumerate(pieces):
-            copy = pltpu.make_async_copy(piece, slot.at[pl.ds(row, count), :], local_sem.at[layer, i])
+            copies.append(
+                pltpu.make_async_copy(piece, own.at[pl.ds(row, count), :], local_sem.at[layer, i])
+            )
+    return copies
+
+
+def gather_forward_kernel(emb_ref, tok_ref, feat_ref, prop_ref, vec_ref, mb_ref, sb_ref, *rest):
+    shards, (out_ref, g0, g1), rest = rest[:6], rest[6:9], rest[9:]
+    saved, (w_ref, local_sem, send_sem, recv_sem, keep_sem) = rest[:-5], rest[-5:]
+    step = pl.program_id(0)
+    at = place()
+    move = Gather(at, (w_ref, g1), GATHER_GROUPS, send_sem, recv_sem)
+    keep = pltpu.make_async_copy(w_ref, g0, keep_sem)
+    @pl.when(step == 0)
+    def _():
+        local = place_own(at, shards, (w_ref, g1), local_sem)
+        for copy in local:
             copy.start()
-            locals_.append(copy)
-    greet(at)
-    for copy in locals_:
-        copy.wait()
-    chains = [(layer, s) for layer in range(LAYERS) for s in range(len(STREAMS))]
-    pending = {}
-    sent = []
-    for phase in range(4):
-        for chain in chains:
-            layer, s = chain
-            row, count, order = STREAMS[s]
-            order = order + ("c",)
-            for copy in pending.pop(chain, ()):
-                copy.wait_recv()
-            axis, done = order[phase], order[:phase]
-            got = []
-            for by in range(1, SIZES[axis]):
-                to = moved(at, axis, by)
-                sem = (layer * 4 + s, AXES.index(axis), by - 1)
-                mine = block(outs[layer], at, done, row, count)
-                copy = pltpu.make_async_remote_copy(
-                    mine, mine, send_sem.at[sem], recv_sem.at[sem],
-                    device_id=(number(to),), device_id_type=MESH,
-                )
-                copy.start()
-                sent.append(copy)
-                theirs = block(outs[layer], moved(at, axis, -by), done, row, count)
-                got.append(
-                    pltpu.make_async_remote_copy(
-                        theirs, theirs, send_sem.at[sem], recv_sem.at[sem],
-                        device_id=(number(to),), device_id_type=MESH,
-                    )
-                )
-            pending[chain] = got
-    for chain in chains:
-        for copy in pending.pop(chain):
-            copy.wait_recv()
-    for copy in sent:
-        copy.wait_send()
-
-
-def gather(att, up, down, stem, q, pin):
-    shape = jax.ShapeDtypeStruct((4, 2, 2, 2, ROWS, D), BF16)
+        greet(at)
+        for copy in local:
+            copy.wait()
+        move.run(GATHER_FIRST)
+        keep.start()
+
+    for i, moves in enumerate(GATHER_LATER[:-1]):
+        pl.when(step == i)(functools.partial(move.run, moves))
+
+    es = [emb_ref[step * SB + j] for j in range(SB)]
+    out, kept = forward_block(
+        es, tok_ref[...].astype(F32), feat_ref, prop_block(prop_ref, step), w_ref,
+        *layer_inputs(0, vec_ref, mb_ref, sb_ref)
+    )
+    out_ref[...] = out
+    for name, ref in zip(SAVED, saved):
+        if name in PER_SAMPLE:
+            for j in range(SB):
+                ref[j] = kept[name][j].astype(ref.dtype)
+        else:
+            ref[...] = kept[name].astype(ref.dtype)
+
+    @pl.when(step == pl.num_programs(0) - 1)
+    def _():
+        move.run(GATHER_LATER[-1])
+        keep.wait()
+        move.close()
+
+
+def gather_forward(tokens, feat, prop, emb, vecs, mbs, sbs, shards):
+    samples = emb.shape[0]
+    steps = samples // SB
+    assert steps == 4
+    rows = samples * TOK
+    shapes = saved_shapes(samples)
+    lead = (4, 2, 2, 2, ROWS, D)
     any_spec = pl.BlockSpec(memory_space=pl.ANY)
-    return pl.pallas_call(
-        gather_kernel,
-        out_shape=[shape, shape],
-        in_specs=[any_spec] * 6,
-        out_specs=[any_spec] * 2,
+    smem = pl.BlockSpec(memory_space=pltpu.SMEM)
+    saved = [(shapes[n][0], shapes[n][1], shapes[n][0][0] // steps) for n in SAVED]
+    outs = [((rows, D), F32, SB * TOK)] + saved
+    weights = jax.ShapeDtypeStruct(lead, BF16)
+    res = pl.pallas_call(
+        gather_forward_kernel,
+        grid=(steps,),
+        in_specs=[smem, blocked(tokens.shape, SB * TOK), blocked(feat.shape, SB * FR * STEPS)]
+        + [whole(a.shape) for a in (prop, vecs, mbs, sbs)] + [any_spec] * 6,
+        out_specs=[blocked(*((outs[0][0], outs[0][2]))), any_spec, any_spec]
+        + [blocked(s, n) for s, _, n in outs[1:]],
+        out_shape=[jax.ShapeDtypeStruct(*outs[0][:2]), weights, weights]
+        + [jax.ShapeDtypeStruct(s, d) for s, d, _ in outs[1:]],
         scratch_shapes=[
+            pltpu.VMEM(lead, BF16),
             pltpu.SemaphoreType.DMA((LAYERS, 9)),
-            pltpu.SemaphoreType.DMA((8, 4, 3)),
-            pltpu.SemaphoreType.DMA((8, 4, 3)),
+            pltpu.SemaphoreType.DMA((2 * len(GATHER_GROUPS), 4, 3)),
+            pltpu.SemaphoreType.DMA((2 * len(GATHER_GROUPS), 4, 3)),
+            pltpu.SemaphoreType.DMA(()),
         ],
-        compiler_params=pltpu.CompilerParams(collective_id=0, has_side_effects=True),
-    )(att, up, down, stem, q, pin)
+        compiler_params=pltpu.CompilerParams(
+            dimension_semantics=("arbitrary",), vmem_limit_bytes=VMEM_LIMIT, collective_id=0,
+            has_side_effects=True,
+        ),
+    )(emb, tokens, feat, prop, vecs, mbs, sbs, *shards)
+    hidden, w0, w1 = res[:3]
+    return hidden, res[3:], w0.reshape(STEMS, ROWS, D), w1.reshape(STEMS, ROWS, D)
+
+
+STREAMS = (
+    (0, 256, ("z", "x", "y")),
+    (256, 256, ("z", "y", "x")),
+    (512, 48, ("x", "y", "z")),
+    (560, 48, ("y", "x", "z")),
+)
 
 
 def scatter_kernel(
-    g0, g1, s0, s1, att, up, down, stem, q, pin, small,
+    g0, g1, s0, s1, mats, small,
     acc0, acc1, rc0, rc1, rx0, rx1, ry0, ry1, rz0, rz1, sm, smr, smz,
     send_sem, recv_sem, ssend, srecv,
 ):
@@ -662,26 +845,13 @@
             if phase < 3:
                 acc[keep + (rows, slice(None))] = value.astype(BF16)
             else:
-                finish_rows(layer, s, value)
+                mats[layer, rows, :] = value
             return carry
 
         if total == 1:
             one(0, 0)
         else:
             lax.fori_loop(0, total, one, 0)
-
-    def finish_rows(layer, s, value):
-        if s < 2:
-            for j in range(2):
-                col = (2 * s + j) * D
-                stem[layer, :, col : col + D] = value[j * D : (j + 1) * D]
-        elif s == 2:
-            q[layer] = value[:SQ]
-            pin[layer] = value[SQ:]
-        else:
-            att[layer] = value[0:16]
-            up[layer] = value[16:32]
-            down[layer] = value[32:48]
 
     smalls = ("c", "x", "y", "z")
 
@@ -743,12 +913,9 @@
         scratch += [pltpu.VMEM(shape + (ROWS, D), BF16)] * 2
     return pl.pallas_call(
         scatter_kernel,
-        out_shape=[
-            out(LAYERS, 16, D), out(LAYERS, 16, D), out(LAYERS, 16, D), out(LAYERS, D, 4 * D),
-            out(LAYERS, SQ, D), out(LAYERS, PROP, D), out(LAYERS, SMALL, D),
-        ],
+        out_shape=[out(LAYERS, ROWS, D), out(LAYERS, SMALL, D)],
         in_specs=[vmem] * 4,
-        out_specs=[vmem] * 7,
+        out_specs=[vmem] * 2,
         scratch_shapes=scratch
         + [
             pltpu.VMEM((4, LAYERS, SMALL, D), F32),
@@ -765,6 +932,38 @@
     )(g0.reshape(lead), g1.reshape(lead), s0, s1)
 
 
+def unpack_kernel(mats, small, att, up, down, stem, q, pin, vec, mb, sb):
+    for layer in range(LAYERS):
+        for j in range(4):
+            stem[layer, :, j * D : (j + 1) * D] = mats[layer, j * D : (j + 1) * D, :]
+        q[layer] = mats[layer, R_Q:R_PIN, :]
+        pin[layer] = mats[layer, R_PIN:R_ATT, :]
+        att[layer] = mats[layer, R_ATT:R_UP, :]
+        up[layer] = mats[layer, R_UP:R_DOWN, :]
+        down[layer] = mats[layer, R_DOWN:ROWS, :]
+        vec[layer] = small[layer, 0:8, :]
+        for i in range(4):
+            mb[layer : layer + 1, i * D : (i + 1) * D] = small[layer, 8 + i : 9 + i, :]
+        sb[layer] = small[layer, 16:SMALL, :]
+
+
+def unpack(mats, small):
+    def out(*shape):
+        return jax.ShapeDtypeStruct(shape, F32)
+
+    vmem = pl.BlockSpec(memory_space=pltpu.VMEM)
+    return pl.pallas_call(
+        unpack_kernel,
+        out_shape=[
+            out(LAYERS, 16, D), out(LAYERS, 16, D), out(LAYERS, 16, D), out(LAYERS, D, 4 * D),
+            out(LAYERS, SQ, D), out(LAYERS, PROP, D), out(LAYERS, 8, D), out(LAYERS, FF),
+            out(LAYERS, 2 * STEMS, D),
+        ],
+        in_specs=[vmem] * 2,
+        out_specs=[vmem] * 9,
+    )(mats, small)
+
+
 def pack(attn, up, down, stem, queries, pin):
     gathered = [lax.all_gather(a, "fsdp", axis=1, tiled=True) for a in (attn, up, down, stem, queries, pin)]
     attn, up, down, stem, queries, pin = gathered
@@ -786,27 +985,21 @@
 def body(n, tokens, features, proprio, embodiment, trunk_attn, feedforward_up_weight, mlp_down,
          stem_mats, stem_queries, prop_in, trunk_vectors, mlp_bias, stem_bias, cotangent):
     shards = (trunk_attn, feedforward_up_weight, mlp_down, stem_mats, stem_queries, prop_in)
-    vecs = trunk_vectors.astype(F32)
-    mbs = mlp_bias.astype(F32).reshape(LAYERS, 1, FF)
-    sbs = stem_bias.astype(F32)
+    out, gtok, gfeat, gprop, g0, g1 = compute(
+        tokens, features, proprio, embodiment, shards, trunk_vectors, mlp_bias, stem_bias,
+        cotangent, None if n == 32 else pack(*shards),
+    )
     if n == 32:
-        w0, w1 = (w.reshape(STEMS, ROWS, D) for w in gather(*shards))
-    else:
-        w0, w1 = pack(*shards)
-    out, gtok, gfeat, gprop, g0, g1 = compute(
-        tokens, features, proprio, embodiment, w0, w1, vecs, mbs, sbs, cotangent, BF16
-    )
-    if n == 32:
-        *mats, small = scatter(g0[0], g1[0], g0[1], g1[1])
-    else:
-        mats = [
-            lax.psum_scatter(a.reshape(LAYERS, -1, a.shape[-1]), "fsdp", scatter_dimension=1, tiled=True)
-            for a in unpack_blocks(jnp.stack([g0[0], g1[0]]).astype(F32))
-        ]
-        small = lax.psum(jnp.stack([g0[1], g1[1]]), "fsdp")
+        *rest, gsb = unpack(*scatter(g0[0], g1[0], g0[1], g1[1]))
+        return (out, gtok, gfeat, gprop, *rest, gsb.reshape(LAYERS, STEMS, 2, D))
+    mats = [
+        lax.psum_scatter(a.reshape(LAYERS, -1, a.shape[-1]), "fsdp", scatter_dimension=1, tiled=True)
+        for a in unpack_blocks(jnp.stack([g0[0], g1[0]]).astype(F32))
+    ]
+    small = lax.psum(jnp.stack([g0[1], g1[1]]), "fsdp")
     gvec = small[:, :8]
     gmb = small[:, 8:12].reshape(LAYERS, FF)
-    gsb = jnp.swapaxes(small[:, 16:].reshape(LAYERS, 2, STEMS, D), 1, 2)
+    gsb = small[:, 16:].reshape(LAYERS, STEMS, 2, D)
     return (out, gtok, gfeat, gprop, *mats, gvec, gmb, gsb)
 
 

time: 372 us -> 223 us (0.60)
  Pallas kernels: 348 us -> 223 us
  local copies, waits for them, and re-layouts: 20.4 us -> 0 us
    pallas_call x3 -> x2, Pallas kernels: 198 us -> 74 us  [call(): pl.pallas_call(kernel, grid_spec=pltpu.PrefetchScalarGridSpec(num_scalar_...]
    unnamed x26 -> x0, local copies, waits for them, and re-layouts: 15 us -> none
    pallas_call x2 -> x3, Pallas kernels: 150 us -> 149 us  [the longest x1 75.8 us: scatter(): pl.pallas_call(scatter_kernel, out_shape=[out(LAYERS, ROWS, D), out(LAYER...]
where the time goes in v3:
time: 223 us
  Pallas kernels  223 us (100%)
    pallas_call x1, Pallas kernels, scatter(): pl.pallas_call(scatter_kernel, out_shape=[out(LAYERS, ROWS, D), out(LAYER...  75.8 us
    pallas_call x2, Pallas kernels, call(): pl.pallas_call(kernel, grid_spec=pltpu.PrefetchScalarGridSpec(num_scalar_...  74 us
    pallas_call x1, Pallas kernels, gather_forward(): pl.pallas_call(gather_forward_kernel, grid=(steps,), in_specs=[smem, bloc...  70.8 us

profile of v3, /device:TPU:0, one launch (start us, length us, event | category | flops | bytes accessed | tf_op | source)
XLA Modules:
  0.0 223.2 jit_solution(15484957381426461836)
XLA Ops:
  0.6 70.8 %shard_map.237 = (f32[2048,128]{1,0:T(8,128)}, bf16[4,2,2,2,608,128]{5,4,3,2,1,0:T(8,128)(2,1)}, bf16[4,2,2,2,608,128]{5,4,3,2,1,0:T(8,128)(2,1)}, bf16[64,112,1...) custom-call(s32[64]{0:T(128)} %emb_ref.5, ...), custom_call_target="tpu_custom_call" | custom-call | tf_op jit(solution)/shard_map/pallas_call | solution.py:737
  71.5 42.4 %shard_map.238 = (bf16[2048,128]{1,0:T(8,128)(2,1)}, f32[2048,128]{1,0:T(8,128)}, bf16[64,112,128]{2,1,0:T(8,128)(2,1)}, f32[1024,32]{1,0:T(8,128)}, bf16[32,608,128]{2,1,0:T(8,128)(2,1)}, /*index=5*/f32[80,128]{1,0:T(8,128)}) custom-call(s32[64]{0:T(128)} %emb_ref.5, f32[2048,128]{1,0:T(8,128)} %get-tuple-element.51.hid_ref, bf16[6272,128]{1,0:T(8,128)(2,1)} %bitcast.18, ...), custom_call_target="tpu_custom_call" | custom-call | tf_op jit(solution)/shard_map/pallas_call | solution.py:502
  113.9 31.5 %shard_map.239 = (f32[2048,128]{1,0:T(8,128)}, f32[6272,128]{1,0:T(8,128)}, f32[2,32,64]{2,1,0:T(8,128)}, bf16[32,608,128]{2,1,0:T(8,128)(2,1)}, f32[80,128]{1,0:T(8,128)}) custom-call(s32[64]{0:T(128)} %emb_ref.5, f32[2048,128]{1,0:T(8,128)} %get-tuple-element.54.grad_ref, bf16[2,32,64]{2,1,0:T(8,128)(2,1)} %bitcast.27, bf16[32,608,128]{2,1,0:T(8,128)(2,1)} %bitcast.20, ...), custom_call_target="tpu_custom_call" | custom-call | tf_op jit(solution)/shard_map/pallas_call | solution.py:502
  145.4 75.8 %shard_map.240 = (f32[2,608,128]{2,1,0:T(8,128)}, f32[2,80,128]{2,1,0:T(8,128)}) custom-call(bf16[4,2,2,2,608,128]{5,4,3,2,1,0:T(8,128)(2,1)} %bitcast.21, bf16[4,2,2,2,608,128]{5,4,3,2,1,0:T(8,128)(2,1)} %bitcast.19, f32[80,128]{1,0:T(8,128)} %get-tuple-element.76.s0, f32[80,128]{1,0:T(8,128)} %get-tuple-element.77.s1), custom_call_target="tpu_custom_call" | custom-call | tf_op jit(solution)/shard_map/pallas_call | solution.py:914
  221.2 2.0 shard_map.241

commit v4 on v3

--- a/solution.py
+++ b/solution.py
@@ -141,7 +141,7 @@
     return weight * (1.0 / jnp.sum(weight, 0, keepdims=True))
 
 
-def forward_block(es, hidden, feat_ref, props, w_ref, vec, mb, sb):
+def forward_block(es, hidden, feat_ref, props, w_ref, vec, mb, sb, tick=None):
     kept = {}
     pre = [
         dot(props[j * PR : (j + 1) * PR], slot(w_ref, e, R_PIN, R_ATT))
@@ -185,6 +185,8 @@
         mixes += [contract(wide[t * D : (t + 1) * D], SQ).astype(BF16) for t in range(STEPS)]
     mix = jnp.concatenate(mixes, 0)
     kept["mix"] = mix
+    if tick is not None:
+        tick()
     outs = [
         dot(mix[j * TOK : (j + 1) * TOK], slot(w_ref, e, 2 * D, 3 * D)) for j, e in enumerate(es)
     ]
@@ -215,7 +217,7 @@
     return second + (dot(act, down) + vec[7:8]), kept
 
 
-def backward_block(es, grad, kept, props, w_ref, vec, acc):
+def backward_block(es, grad, kept, props, w_ref, vec, acc, tick=None):
     wqkv, wout, up, down = trunk_weights(w_ref)
     out_low = grad.astype(BF16)
     acc["vec"][7] += fold(out_low.astype(F32))
@@ -262,6 +264,9 @@
     mask16 = head_mask(SQ, 0.25)
     mask16_one = head_mask(SQ, 1.0)
     row16 = lax.broadcasted_iota(jnp.int32, (PR, D), 0)
+    row8 = lax.broadcasted_iota(jnp.int32, (8, D), 0)
+    if tick is not None:
+        tick()
     gs_in = [stem_grad[j * TOK : (j + 1) * TOK] for j in range(SB)]
     gmixes = [dot_nt(gs_in[j], slot(w_ref, e, 2 * D, 3 * D)).astype(BF16) for j, e in enumerate(es)]
     grad_wo = [dot_tn(kept["mix"][j * TOK : (j + 1) * TOK], gs_in[j]) for j in range(SB)]
@@ -305,26 +310,28 @@
     grad_wkv = [dot_tn(kept["ctx"][j], gkvs[j]) for j in range(SB)]
     grad_wp = [dot_tn(kept["pact"][j * PR : (j + 1) * PR], prow_low[j]) for j in range(SB)]
     grad_pin = [dot_tn(props[j * PR : (j + 1) * PR], gppres[j]) for j in range(SB)]
-    stem = acc["stem"]
     for j, e in enumerate(es):
-        stem[e, 0:D, :] += grad_wkv[j][:, :D]
-        stem[e, D : 2 * D, :] += grad_wkv[j][:, D:]
-        stem[e, 2 * D : 3 * D, :] += grad_wo[j]
-        stem[e, 3 * D : 4 * D, :] += grad_wp[j]
-        stem[e, R_Q:R_PIN, :] += grad_q[j]
-        stem[e, R_PIN:R_ATT, :] += grad_pin[j]
-        acc["sb"][pl.ds(2 * e, 1), :] += jnp.sum(gppres[j].astype(F32), 0, keepdims=True)
-        acc["sb"][pl.ds(2 * e + 1, 1), :] += jnp.sum(prows[j], 0, keepdims=True)
+        bias = jnp.where(
+            row8 == 0,
+            jnp.sum(gppres[j].astype(F32), 0, keepdims=True),
+            jnp.where(row8 == 1, jnp.sum(prows[j], 0, keepdims=True), 0.0),
+        )
+        acc["add"](
+            j, e,
+            (
+                (0, grad_wkv[j][:, :D]), (D, grad_wkv[j][:, D:]), (2 * D, grad_wo[j]),
+                (3 * D, grad_wp[j]), (R_Q, grad_q[j]), (R_PIN, grad_pin[j]), (R_ATT, bias),
+            ),
+        )
     return grad_first, grad_contexts, grad_props
 
 
-ACC = ("stem", "sb", "wqkv", "wout", "up", "down", "vec", "mb")
-
-
-def acc_shapes():
+ACC = ("stem", "wqkv", "wout", "up", "down", "vec", "mb")
+
+
+def acc_shapes(entries):
     return [
-        pltpu.VMEM((STEMS, STEM_ROWS, D), F32),
-        pltpu.VMEM((2 * STEMS, D), F32),
+        pltpu.VMEM((entries, STEM_ROWS + 8, D), F32),
         pltpu.VMEM((D, 3 * D), F32),
         pltpu.VMEM((D, D), F32),
         pltpu.VMEM((D, FF), F32),
@@ -339,26 +346,43 @@
         ref[...] = jnp.zeros(ref.shape, ref.dtype)
 
 
+def add_in_place(acc):
+    def add(j, e, pieces):
+        for row, value in pieces:
+            acc["stem"][e, row : row + value.shape[0], :] += value
+
+    return {**acc, "add": add}
+
+
+def trunk_blocks(acc):
+    wqkv = acc["wqkv"][...]
+    attn = [wqkv[:, :D], wqkv[:, D : 2 * D], wqkv[:, 2 * D :], acc["wout"][...]]
+    return (
+        jnp.concatenate(attn, 0).astype(BF16).reshape(STEMS, 16, D),
+        acc["up"][...].T.astype(BF16).reshape(STEMS, 16, D),
+        acc["down"][...].T.astype(BF16).reshape(STEMS, 16, D),
+    )
+
+
+def small_rows(acc):
+    mb = jnp.sum(acc["mb"][...], 0, keepdims=True)
+    return jnp.concatenate(
+        [jnp.sum(acc["vec"][...], 1)] + [mb[:, i * D : (i + 1) * D] for i in range(4)]
+        + [jnp.zeros((4, D), F32)], 0
+    )
+
+
 def finish(acc, grad_ref, small_ref):
     def stem_out(e, carry):
-        grad_ref[e, 0:STEM_ROWS, :] = acc["stem"][e].astype(grad_ref.dtype)
+        grad_ref[e, 0:STEM_ROWS, :] = acc["stem"][e, 0:STEM_ROWS, :].astype(grad_ref.dtype)
         return carry
 
     lax.fori_loop(0, STEMS, stem_out, 0)
-    wqkv = acc["wqkv"][...]
-    attn = [wqkv[:, :D], wqkv[:, D : 2 * D], wqkv[:, 2 * D :], acc["wout"][...]]
-    for block in range(4):
-        grad_ref[block * 8 : block * 8 + 8, R_ATT:R_UP, :] = (
-            attn[block].astype(grad_ref.dtype).reshape(8, 16, D)
-        )
-    grad_ref[:, R_UP:R_DOWN, :] = acc["up"][...].T.astype(grad_ref.dtype).reshape(STEMS, 16, D)
-    grad_ref[:, R_DOWN:ROWS, :] = acc["down"][...].T.astype(grad_ref.dtype).reshape(STEMS, 16, D)
-    small_ref[0:8, :] = jnp.sum(acc["vec"][...], 1)
-    mb = jnp.sum(acc["mb"][...], 0, keepdims=True)
-    small_ref[8:16, :] = jnp.concatenate(
-        [mb[:, i * D : (i + 1) * D] for i in range(4)] + [jnp.zeros((4, D), F32)], 0
-    )
-    small_ref[16:SMALL, :] = acc["sb"][...]
+    for i, part in enumerate(trunk_blocks(acc)):
+        grad_ref[:, R_ATT + 16 * i : R_ATT + 16 * (i + 1), :] = part
+    small_ref[0:16, :] = small_rows(acc)
+    for e in range(STEMS):
+        small_ref[16 + 2 * e : 18 + 2 * e, :] = acc["stem"][e, STEM_ROWS : STEM_ROWS + 2, :]
 
 
 SAVED = ("ctx", "kv", "prob", "mix", "first", "qkv", "sprob", "smix", "second", "act", "slope", "pact", "pslope")
@@ -421,21 +445,39 @@
             ref[...] = kept[name].astype(ref.dtype)
 
 
+def link_samples(emb_ref, before_ref, last_ref):
+    def unset(e, carry):
+        last_ref[e] = -1
+        return carry
+
+    def link(s, carry):
+        e = emb_ref[s]
+        before_ref[s] = last_ref[e]
+        last_ref[e] = s
+        return carry
+
+    lax.fori_loop(0, STEMS, unset, 0)
+    lax.fori_loop(0, before_ref.shape[0], link, 0)
+
+
 def middle_kernel(
     emb_ref, hid_ref, feat_ref, prop_ref, w_ref, vec_ref, mb_ref, sb_ref, cot_ref,
-    out_ref, ghid_ref, gfeat_ref, gprop_ref, gw_ref, gsmall_ref, *accs
+    out_ref, ghid_ref, gfeat_ref, gprop_ref, gw_ref, gsmall_ref, before_ref, last_ref, *accs
 ):
     step = pl.program_id(0)
     acc = dict(zip(ACC, accs))
 
-    pl.when(step == 0)(lambda: clear(acc))
+    @pl.when(step == 0)
+    def _():
+        clear(acc)
+        link_samples(emb_ref, before_ref, last_ref)
 
     es = [emb_ref[step * SB + j] for j in range(SB)]
     vec, mb, sb = layer_inputs(1, vec_ref, mb_ref, sb_ref)
     props = prop_block(prop_ref, step)
     out, kept = forward_block(es, hid_ref[...], feat_ref, props, w_ref, vec, mb, sb)
     out_ref[...] = out.astype(BF16)
-    ghid, gctx, gprop = backward_block(es, cot_ref[...].astype(F32), kept, props, w_ref, vec, acc)
+    ghid, gctx, gprop = backward_block(es, cot_ref[...].astype(F32), kept, props, w_ref, vec, add_in_place(acc))
     ghid_ref[...] = ghid
     for j in range(SB):
         gfeat_ref[j] = gctx[j]
@@ -456,7 +498,7 @@
     kept = {name: [ref[j] for j in range(SB)] if name in PER_SAMPLE else ref[...] for name, ref in zip(SAVED, saved)}
     props = prop_block(prop_ref, step)
     vec = vec_ref[0].astype(F32)
-    ghid, gctx, gprop = backward_block(es, grad_ref[...], kept, props, w_ref, vec, acc)
+    ghid, gctx, gprop = backward_block(es, grad_ref[...], kept, props, w_ref, vec, add_in_place(acc))
     gtok_ref[...] = ghid
     for j in range(0, SB, 4):
         totals = [gctx[i].astype(F32) + gfeat1_ref[i].astype(F32) for i in range(j, j + 4)]
@@ -505,7 +547,10 @@
             num_scalar_prefetch=1,
             grid=(steps,),
             in_specs=[blocked(a.shape, n) if n else whole(a.shape) for a, n in ins],
-            out_specs=[blocked(s, n) if n else whole(s) for s, _, n in outs],
+            out_specs=[
+                pl.BlockSpec(memory_space=pltpu.SMEM) if n is None else blocked(s, n) if n else whole(s)
+                for s, _, n in outs
+            ],
             scratch_shapes=scratch,
         ),
         out_shape=[jax.ShapeDtypeStruct(s, d) for s, d, _ in outs],
@@ -538,26 +583,37 @@
         )
         hidden, saved = res[0], res[1:]
     grad_outs = [((STEMS, ROWS, D), BF16, 0), ((SMALL, D), F32, 0)]
-    out, ghid, gfeat1, gprop1, *grads1 = call(
+    out, ghid, gfeat1, gprop1, *grads1, before, last = call(
         middle_kernel, steps, emb,
         [(hidden, rb), (feat, fb), (prop, 0), (w1, 0), (vecs, 0), (mbs, 0), (sbs, 0),
          (cot.reshape(rows, D), rb)],
         [((rows, D), BF16, rb), ((rows, D), F32, rb), ((samples, CR, D), BF16, SB),
-         ((samples * PR, PROP), F32, SB * PR)] + grad_outs,
-        acc_shapes(),
-    )
-    gtok, gfeat, gprop, *grads0 = call(
-        backward_kernel, steps, emb,
+         ((samples * PR, PROP), F32, SB * PR)] + grad_outs
+        + [((samples,), jnp.int32, None), ((STEMS,), jnp.int32, None)],
+        acc_shapes(STEMS),
+    )
+    backward_ins = (
         [(ghid, rb), (prop, 0), (w0, 0), (vecs, 0), (gfeat1, SB), (gprop1, SB * PR)]
-        + [(a, per(a.shape)) for a in saved],
-        [((rows, D), F32, rb), ((samples * FR * STEPS, D), F32, fb), ((STEPS, PROP, samples), F32, 0)]
-        + grad_outs,
-        [pltpu.VMEM((PROP, STEPS * samples), F32)] + acc_shapes(),
-    )
+        + [(a, per(a.shape)) for a in saved]
+    )
+    backward_outs = [
+        ((rows, D), F32, rb), ((samples * FR * STEPS, D), F32, fb), ((STEPS, PROP, samples), F32, 0)
+    ]
+    if weights is None:
+        gtok, gfeat, gprop, mats, small = backward_scatter(
+            steps, (emb, before, last), backward_ins, backward_outs, *grads1
+        )
+        gtok, gfeat, *mats, small = unpack(mats, small, gtok, gfeat)
+    else:
+        gtok, gfeat, gprop, *grads0 = call(
+            backward_kernel, steps, emb, backward_ins, backward_outs + grad_outs,
+            [pltpu.VMEM((PROP, STEPS * samples), F32)] + acc_shapes(STEMS),
+        )
+        mats, small = (jnp.stack(pair) for pair in zip(grads0, grads1))
     gfeat = jnp.swapaxes(gfeat.reshape(samples, FR, STEPS, D), 1, 2)
     return (
         out.reshape(tokens.shape), gtok.reshape(tokens.shape), gfeat, gprop.transpose(2, 0, 1),
-        grads0, grads1
+        mats, small
     )
 
 
@@ -652,15 +708,19 @@
 GATHER_GROUPS = chunks_of(0, BOUNDS) + chunks_of(1, BOUNDS)
 GATHER_FIRST = (
     (0, 0), (1, 0), (0, 1), (2, 0), (1, 1), (0, 2), (3, 0), (2, 1), (1, 2), (0, 3), (4, 0), (3, 1), (2, 2),
-    (1, 3), (5, 0), (0, 4), (3, 2), (2, 3), (1, 4), (6, 0), (3, 3), (7, 0), (2, 4), (3, 4),
+    (1, 3), (0, 4), (5, 0), (3, 2), (4, 1), (2, 3), (1, 4), (6, 0), (5, 1), (3, 3), (2, 4), (7, 0), (3, 4),
 )
 GATHER_LATER = (
-    ((4, 1), (5, 1), (6, 1), (7, 1)),
-    ((4, 2), (5, 2)),
-    ((6, 2), (7, 2)),
-    ((4, 3), (5, 3)),
-    ((6, 3), (7, 3), (4, 4), (5, 4), (6, 4), (7, 4)),
+    ((4, 2), (6, 1)),
+    ((7, 1),),
+    ((5, 2),),
+    ((6, 2),),
+    ((4, 3),),
+    ((7, 2),),
+    ((5, 3),),
+    ((6, 3),),
 )
+GATHER_END = ((7, 3), (4, 4), (5, 4), (6, 4), (7, 4))
 
 
 def place_own(at, shards, outs, local_sem):
@@ -699,13 +759,15 @@
         move.run(GATHER_FIRST)
         keep.start()
 
-    for i, moves in enumerate(GATHER_LATER[:-1]):
-        pl.when(step == i)(functools.partial(move.run, moves))
-
+    def moves_at(half):
+        for i in range(len(GATHER_LATER) // 2):
+            pl.when(step == i)(functools.partial(move.run, GATHER_LATER[2 * i + half]))
+
+    moves_at(0)
     es = [emb_ref[step * SB + j] for j in range(SB)]
     out, kept = forward_block(
         es, tok_ref[...].astype(F32), feat_ref, prop_block(prop_ref, step), w_ref,
-        *layer_inputs(0, vec_ref, mb_ref, sb_ref)
+        *layer_inputs(0, vec_ref, mb_ref, sb_ref), tick=lambda: moves_at(1)
     )
     out_ref[...] = out
     for name, ref in zip(SAVED, saved):
@@ -717,7 +779,7 @@
 
     @pl.when(step == pl.num_programs(0) - 1)
     def _():
-        move.run(GATHER_LATER[-1])
+        move.run(GATHER_END)
         keep.wait()
         move.close()
 
@@ -738,7 +800,7 @@
         gather_forward_kernel,
         grid=(steps,),
         in_specs=[smem, blocked(tokens.shape, SB * TOK), blocked(feat.shape, SB * FR * STEPS)]
-        + [whole(a.shape) for a in (prop, vecs, mbs, sbs)] + [any_spec] * 6,
+        + [whole(a.shape) for a in (prop, vecs, mbs, sbs) + tuple(shards)],
         out_specs=[blocked(*((outs[0][0], outs[0][2]))), any_spec, any_spec]
         + [blocked(s, n) for s, _, n in outs[1:]],
         out_shape=[jax.ShapeDtypeStruct(*outs[0][:2]), weights, weights]
@@ -759,180 +821,280 @@
     return hidden, res[3:], w0.reshape(STEMS, ROWS, D), w1.reshape(STEMS, ROWS, D)
 
 
-STREAMS = (
-    (0, 256, ("z", "x", "y")),
-    (256, 256, ("z", "y", "x")),
-    (512, 48, ("x", "y", "z")),
-    (560, 48, ("y", "x", "z")),
+class Scatter:
+    def __init__(self, at, groups, source, acc, lands, out, small, sems):
+        self.at, self.groups, self.source, self.acc, self.lands, self.out = at, groups, source, acc, lands, out
+        self.send_sem, self.recv_sem, self.small_send, self.small_recv = sems
+        self.sm, self.smr, self.smz, self.small_out = small
+
+    def order(self, chunk):
+        return ("c",) + chunk[3][::-1]
+
+    def left(self, chunk, phase):
+        return [a for a in AXES if a not in self.order(chunk)[: phase + 1]]
+
+    def copies(self, g, phase):
+        for i, chunk in enumerate(self.groups[g]):
+            _, row, count, _ = chunk
+            axis, left = self.order(chunk)[phase], self.left(chunk, phase)
+            for by in range(1, SIZES[axis]):
+                to = moved(self.at, axis, by)
+                src = []
+                for a in "zyx":
+                    spot = to if a == axis else self.at
+                    src.append(pl.ds(0, SIZES[a]) if a in left else spot[a])
+                dst = [by - 1] if axis == "z" else [pl.ds(0, SIZES[a]) for a in left]
+                source = self.source(to["c"]) if phase == 0 else self.acc
+                rows = (pl.ds(row, count), slice(None))
+                sem = (2 * g + i, AXES.index(axis), by - 1)
+                yield pltpu.make_async_remote_copy(
+                    source.at[tuple(src) + rows], self.lands[phase].at[tuple(dst) + rows],
+                    self.send_sem.at[sem], self.recv_sem.at[sem],
+                    device_id=(number(to),), device_id_type=MESH,
+                )
+
+    def add(self, g, phase):
+        for chunk in self.groups[g]:
+            _, row, count, _ = chunk
+            axis, left = self.order(chunk)[phase], self.left(chunk, phase)
+            rows = (pl.ds(row, count), slice(None))
+            total = 1
+            for a in left:
+                total *= SIZES[a]
+
+            def one(i, carry):
+                spot = dict(self.at)
+                rest = i
+                for a in left[::-1]:
+                    spot[a] = rest % SIZES[a]
+                    rest = rest // SIZES[a]
+                keep = (spot["z"], spot["y"], spot["x"])
+                value = self.acc[keep + rows].astype(F32)
+                if axis == "z":
+                    for by in range(SIZES["z"] - 1):
+                        value = value + self.lands[3][(by,) + rows].astype(F32)
+                    self.out[rows] = value
+                else:
+                    land = tuple(spot[a] for a in left)
+                    self.acc[keep + rows] = (value + self.lands[phase][land + rows].astype(F32)).astype(BF16)
+                return carry
+
+            if total == 1:
+                one(0, 0)
+            else:
+                lax.fori_loop(0, total, one, 0)
+
+    def small_copies(self, phase, arriving):
+        axis = "cxyz"[phase]
+        for by in range(1, SIZES[axis]):
+            whose = moved(self.at, axis, -by) if arriving else self.at
+            dst = self.smz.at[whose["z"]] if axis == "z" else self.smr.at[phase]
+            yield pltpu.make_async_remote_copy(
+                self.sm.at[phase], dst, self.small_send.at[phase, by - 1], self.small_recv.at[phase, by - 1],
+                device_id=(number(moved(self.at, axis, by)),), device_id_type=MESH,
+            )
+
+    def small_add(self, phase):
+        if phase < 3:
+            self.sm[phase + 1] = self.sm[phase] + self.smr[phase]
+        else:
+            self.smz[self.at["z"]] = self.sm[phase]
+            self.small_out[...] = (self.smz[0] + self.smz[1]) + (self.smz[2] + self.smz[3])
+
+    def run(self, moves):
+        for g, phase in moves:
+            if phase > 0:
+                for copy in self.small_copies(phase - 1, True) if g < 0 else self.copies(g, phase - 1):
+                    copy.wait_recv()
+                self.small_add(phase - 1) if g < 0 else self.add(g, phase - 1)
+            if phase < 4:
+                for copy in self.small_copies(phase, False) if g < 0 else self.copies(g, phase):
+                    copy.start()
+
+    def close(self):
+        for phase in range(4):
+            for g in range(len(self.groups)):
+                for copy in self.copies(g, phase):
+                    copy.wait_send()
+            for copy in self.small_copies(phase, False):
+                copy.wait_send()
+
+
+SCATTER_GROUPS = chunks_of(0, BOUNDS)
+SCATTER_BESIDE = (
+    ((0, 0), (1, 0), (2, 0), (3, 0), (-1, 0)),
+    ((0, 1), (1, 1), (-1, 1)),
+    ((2, 1), (3, 1), (-1, 2)),
+    (),
+    ((0, 2), (1, 2), (-1, 3)),
+    ((2, 2), (-1, 4)),
+    ((3, 2),),
+    ((0, 3), (1, 3)),
 )
-
-
-def scatter_kernel(
-    g0, g1, s0, s1, mats, small,
-    acc0, acc1, rc0, rc1, rx0, rx1, ry0, ry1, rz0, rz1, sm, smr, smz,
-    send_sem, recv_sem, ssend, srecv,
-):
+SCATTER_END = ((2, 3), (3, 3))
+
+
+def scatter_last():
+    n = len(SCATTER_GROUPS)
+    for t in range(n + 4):
+        for phase in range(5):
+            if 0 <= t - phase < n:
+                yield 0, t - phase, phase
+        if t < 5:
+            yield 0, -1, t
+        if 2 <= t < 2 + n:
+            yield 1, t - 2, 4
+
+
+def backward_scatter_kernel(emb_ref, before_ref, last_ref, grad_ref, prop_ref, w_ref, vec_ref, gfeat1_ref, gprop1_ref, *rest):
+    n = len(SAVED)
+    saved, (g1, s1), rest = rest[:n], rest[n : n + 2], rest[n + 2 :]
+    (gtok_ref, gfeat_ref, gprop_ref, mats_ref, small_ref, gprops), rest = rest[:6], rest[6:]
+    acc, rest = dict(zip(ACC, rest[: len(ACC)])), rest[len(ACC) :]
+    trunk, sbuf, own_sem = rest[:3]
+    per_layer = rest[3:]
+    step = pl.program_id(0)
+    samples = before_ref.shape[0]
     at = place()
-    grads = (g0, g1)
-    accs = (acc0, acc1)
-    lands = {"c": (rc0, rc1), "x": (rx0, rx1), "y": (ry0, ry1), "z": (rz0, rz1)}
-    greet(at)
-    chains = [(layer, s) for layer in (1, 0) for s in range(len(STREAMS))]
-    sent = []
-
-    def start(chain, phase):
-        layer, s = chain
-        row, count, order = STREAMS[s]
-        order = ("c",) + order[::-1]
-        axis = order[phase]
-        left = [a for a in AXES if a not in order[: phase + 1]]
-        source = grads[layer] if phase == 0 else accs[layer]
-        got = []
-        for by in range(1, SIZES[axis]):
-            to = moved(at, axis, by)
-            index = []
-            for a in AXES:
-                if a == "c" and phase > 0:
-                    continue
-                if a == axis:
-                    index.append(to[a])
-                else:
-                    index.append(pl.ds(0, SIZES[a]) if a in left else at[a])
-            src = source.at[tuple(index) + (pl.ds(row, count), slice(None))]
-            index = [] if axis != "z" else [by - 1]
-            for a in AXES:
-                if a != axis and a != "c":
-                    index.append(pl.ds(0, SIZES[a]) if a in left else 0)
-            dst = lands[axis][layer].at[tuple(index) + (pl.ds(row, count), slice(None))]
-            sem = (layer * 4 + s, AXES.index(axis), by - 1)
-            copy = pltpu.make_async_remote_copy(
-                src, dst, send_sem.at[sem], recv_sem.at[sem],
-                device_id=(number(to),), device_id_type=MESH,
-            )
-            copy.start()
-            sent.append(copy)
-            got.append(copy)
-        return got
-
-    def add(chain, phase):
-        layer, s = chain
-        row, count, order = STREAMS[s]
-        order = ("c",) + order[::-1]
-        axis = order[phase]
-        left = [a for a in AXES if a not in order[: phase + 1]]
-        source = grads[layer] if phase == 0 else accs[layer]
-        acc, land = accs[layer], lands[axis][layer]
-        rows = pl.ds(row, count)
-        total = 1
-        for a in left:
-            total *= SIZES[a]
+
+    def scatter_of(layer):
+        accum, r0, r1, r2, r3, sm, smr, smz, *sems = per_layer[12 * layer : 12 * (layer + 1)]
+        source = (lambda c: g1.at[:, :, :, c]) if layer else (lambda c: sbuf)
+        return Scatter(
+            at, SCATTER_GROUPS, source, accum, (r0, r1, r2, r3), mats_ref.at[layer],
+            (sm, smr, smz, small_ref.at[layer]), sems,
+        )
+
+    first, second = scatter_of(0), scatter_of(1)
+    own = pltpu.make_async_copy(g1.at[:, :, :, at["c"]], second.acc, own_sem)
+
+    @pl.when(step == 0)
+    def _():
+        own.start()
+        greet(at)
+        for name in ACC[1:]:
+            acc[name][...] = jnp.zeros(acc[name].shape, F32)
+        second.sm[0] = s1[...]
+        own.wait()
+        second.run(SCATTER_BESIDE[0])
+
+    def moves_at(half):
+        for i in range(len(SCATTER_BESIDE) // 2):
+            if 2 * i + half:
+                pl.when(step == i)(functools.partial(second.run, SCATTER_BESIDE[2 * i + half]))
+
+    moves_at(0)
+    es = [emb_ref[step * SB + j] for j in range(SB)]
+    befores = [before_ref[step * SB + j] for j in range(SB)]
+    stem = acc["stem"]
+
+    def add(j, e, pieces):
+        for row, value in pieces:
+            old = stem[jnp.maximum(befores[j], 0), row : row + value.shape[0], :]
+            stem[step * SB + j, row : row + value.shape[0], :] = value + jnp.where(befores[j] >= 0, old, 0.0)
+
+    kept = {
+        name: [ref[j] for j in range(SB)] if name in PER_SAMPLE else ref[...]
+        for name, ref in zip(SAVED, saved)
+    }
+    props = prop_block(prop_ref, step)
+    ghid, gctx, gprop = backward_block(
+        es, grad_ref[...], kept, props, w_ref, vec_ref[0].astype(F32), {**acc, "add": add}, lambda: moves_at(1)
+    )
+    gtok_ref[...] = ghid
+    for j in range(0, SB, 4):
+        totals = [gctx[i].astype(F32) + gfeat1_ref[i].astype(F32) for i in range(j, j + 4)]
+        gfeat_ref[j * STEPS * FR : (j + 4) * STEPS * FR, :] = jnp.concatenate(
+            [total[: STEPS * FR] for total in totals], 0
+        )
+    add_proprio(jnp.concatenate(gprop, 0) + gprop1_ref[...], gprops, step)
+
+    def gather_group(g):
+        start, stop = BOUNDS[g], BOUNDS[g + 1]
+        middle = min(stop, STEM_ROWS)
 
         def one(i, carry):
-            spot = dict(at)
-            lspot = {"z": 0, "y": 0, "x": 0}
-            rest = i
-            for a in left[::-1]:
-                spot[a] = rest % SIZES[a]
-                lspot[a] = spot[a]
-                rest = rest // SIZES[a]
-            keep = (spot["z"], spot["y"], spot["x"])
-            mine = source[keep + ((at["c"],) if phase == 0 else ()) + (rows, slice(None))]
-            value = mine.astype(F32)
-            for by in range(1, SIZES[axis]):
-                index = () if axis != "z" else (by - 1,)
-                index += tuple(lspot[a] for a in AXES if a != axis and a != "c")
-                value = value + land[index + (rows, slice(None))].astype(F32)
-            if phase < 3:
-                acc[keep + (rows, slice(None))] = value.astype(BF16)
-            else:
-                mats[layer, rows, :] = value
+            spot = (i // 4, (i // 2) % 2, i % 2)
+            for ref, c in ((first.acc, at["c"]), (sbuf, 1 - at["c"])):
+                e = 2 * i + c
+                s = last_ref[e]
+                value = stem[jnp.maximum(s, 0), start:middle, :]
+                ref[spot + (slice(start, middle), slice(None))] = jnp.where(s >= 0, value, 0.0).astype(BF16)
+                if stop > middle:
+                    ref[spot + (slice(middle, stop), slice(None))] = trunk[e]
             return carry
 
-        if total == 1:
-            one(0, 0)
-        else:
-            lax.fori_loop(0, total, one, 0)
-
-    smalls = ("c", "x", "y", "z")
-
-    def small_start(phase):
-        axis = smalls[phase]
-        for by in range(1, SIZES[axis]):
-            to = moved(at, axis, by)
-            dst = smr.at[phase] if axis != "z" else smz.at[at["z"]]
-            sem = (phase, by - 1)
-            copy = pltpu.make_async_remote_copy(
-                sm.at[phase], dst, ssend.at[sem], srecv.at[sem],
-                device_id=(number(to),), device_id_type=MESH,
-            )
-            copy.start()
-            sent.append(copy)
-
-    def small_land(phase):
-        axis = smalls[phase]
-        for by in range(1, SIZES[axis]):
-            src = moved(at, axis, -by)
-            dst = smr.at[phase] if axis != "z" else smz.at[src["z"]]
-            sem = (phase, by - 1)
-            pltpu.make_async_remote_copy(
-                sm.at[phase], dst, ssend.at[sem], srecv.at[sem],
-                device_id=(number(moved(at, axis, by)),), device_id_type=MESH,
-            ).wait_recv()
-        if axis != "z":
-            sm[phase + 1] = sm[phase] + smr[phase]
-        else:
-            smz[at["z"]] = sm[phase]
-            small[...] = (smz[0] + smz[1]) + (smz[2] + smz[3])
-
-    pending = {chain: start(chain, 0) for chain in chains}
-    sm[0, 0] = s0[...]
-    sm[0, 1] = s1[...]
-    small_start(0)
-    for phase in range(4):
-        for chain in chains:
-            for copy in pending.pop(chain):
-                copy.wait_recv()
-            add(chain, phase)
-            if phase < 3:
-                pending[chain] = start(chain, phase + 1)
-        small_land(phase)
-        if phase < 3:
-            small_start(phase + 1)
-    for copy in sent:
-        copy.wait_send()
-
-
-def scatter(g0, g1, s0, s1):
-    def out(*shape):
-        return jax.ShapeDtypeStruct(shape, F32)
-
-    vmem = pl.BlockSpec(memory_space=pltpu.VMEM)
+        lax.fori_loop(0, STEMS // 2, one, 0)
+
+    @pl.when(step == pl.num_programs(0) - 1)
+    def _():
+        for i, part in enumerate(trunk_blocks(acc)):
+            trunk[:, 16 * i : 16 * (i + 1), :] = part
+        first.sm[0, 0:16, :] = small_rows(acc)
+        for e in range(STEMS):
+            s = last_ref[e]
+            value = stem[jnp.maximum(s, 0), STEM_ROWS : STEM_ROWS + 8, :]
+            first.sm[0, 16 + 2 * e : 18 + 2 * e, :] = jnp.where(s >= 0, value, 0.0)[0:2]
+        second.run(SCATTER_END)
+        for layer, g, phase in scatter_last():
+            if phase == 0 and g >= 0:
+                gather_group(g)
+            (first, second)[layer].run(((g, phase),))
+        write_proprio(gprops, gprop_ref)
+        second.close()
+        first.close()
+
+
+def backward_scatter(steps, scalars, ins, outs, g1, s1):
     lead = (4, 2, 2, 2, ROWS, D)
-    scratch = []
-    for shape in ((4, 2, 2), (4, 2, 2), (4, 2), (4, 2), (3, 2, 2)):
-        scratch += [pltpu.VMEM(shape + (ROWS, D), BF16)] * 2
+    samples = scalars[0].shape[0]
+    smem = pl.BlockSpec(memory_space=pltpu.SMEM)
+    any_spec = pl.BlockSpec(memory_space=pl.ANY)
+    outs = outs + [((LAYERS, ROWS, D), F32, 0), ((LAYERS, SMALL, D), F32, 0)]
+    per_layer = [
+        pltpu.VMEM((4, 2, 2, ROWS, D), BF16),
+        pltpu.VMEM((4, 2, 2, ROWS, D), BF16),
+        pltpu.VMEM((4, 2, ROWS, D), BF16),
+        pltpu.VMEM((4, ROWS, D), BF16),
+        pltpu.VMEM((3, ROWS, D), BF16),
+        pltpu.VMEM((4, SMALL, D), F32),
+        pltpu.VMEM((3, SMALL, D), F32),
+        pltpu.VMEM((4, SMALL, D), F32),
+        pltpu.SemaphoreType.DMA((2 * len(SCATTER_GROUPS), 4, 3)),
+        pltpu.SemaphoreType.DMA((2 * len(SCATTER_GROUPS), 4, 3)),
+        pltpu.SemaphoreType.DMA((4, 3)),
+        pltpu.SemaphoreType.DMA((4, 3)),
+    ]
     return pl.pallas_call(
-        scatter_kernel,
-        out_shape=[out(LAYERS, ROWS, D), out(LAYERS, SMALL, D)],
-        in_specs=[vmem] * 4,
-        out_specs=[vmem] * 2,
-        scratch_shapes=scratch
+        backward_scatter_kernel,
+        grid=(steps,),
+        in_specs=[smem] * 3 + [blocked(a.shape, n) if n else whole(a.shape) for a, n in ins]
+        + [any_spec, whole(s1.shape)],
+        out_specs=[blocked(s, n) if n else whole(s) for s, _, n in outs],
+        out_shape=[jax.ShapeDtypeStruct(s, d) for s, d, _ in outs],
+        scratch_shapes=[pltpu.VMEM((PROP, STEPS * samples), F32)] + acc_shapes(samples)
         + [
-            pltpu.VMEM((4, LAYERS, SMALL, D), F32),
-            pltpu.VMEM((3, LAYERS, SMALL, D), F32),
-            pltpu.VMEM((4, LAYERS, SMALL, D), F32),
-            pltpu.SemaphoreType.DMA((8, 4, 3)),
-            pltpu.SemaphoreType.DMA((8, 4, 3)),
-            pltpu.SemaphoreType.DMA((4, 3)),
-            pltpu.SemaphoreType.DMA((4, 3)),
-        ],
+            pltpu.VMEM((STEMS, 48, D), BF16),
+            pltpu.VMEM((4, 2, 2, ROWS, D), BF16),
+            pltpu.SemaphoreType.DMA(()),
+        ]
+        + per_layer * LAYERS,
         compiler_params=pltpu.CompilerParams(
-            collective_id=1, has_side_effects=True, vmem_limit_bytes=VMEM_LIMIT
+            dimension_semantics=("arbitrary",), vmem_limit_bytes=VMEM_LIMIT, collective_id=1,
+            has_side_effects=True,
         ),
-    )(g0.reshape(lead), g1.reshape(lead), s0, s1)
-
-
-def unpack_kernel(mats, small, att, up, down, stem, q, pin, vec, mb, sb):
+    )(*scalars, *[a for a, _ in ins], g1.reshape(lead), s1)
+
+
+def unpack_kernel(mats, small, gtok_in, gfeat_in, gtok, gfeat, att, up, down, stem, q, pin, vec, mb, sb):
+    gtok[...] = gtok_in[...]
+    gfeat[...] = gfeat_in[...]
+    pl.when(pl.program_id(0) == 0)(
+        lambda: split_gradients(mats, small, att, up, down, stem, q, pin, vec, mb, sb)
+    )
+
+
+def split_gradients(mats, small, att, up, down, stem, q, pin, vec, mb, sb):
     for layer in range(LAYERS):
         for j in range(4):
             stem[layer, :, j * D : (j + 1) * D] = mats[layer, j * D : (j + 1) * D, :]
@@ -947,21 +1109,20 @@
         sb[layer] = small[layer, 16:SMALL, :]
 
 
-def unpack(mats, small):
-    def out(*shape):
-        return jax.ShapeDtypeStruct(shape, F32)
-
-    vmem = pl.BlockSpec(memory_space=pltpu.VMEM)
+def unpack(mats, small, gtok, gfeat):
+    outs = [
+        (LAYERS, 16, D), (LAYERS, 16, D), (LAYERS, 16, D), (LAYERS, D, 4 * D), (LAYERS, SQ, D),
+        (LAYERS, PROP, D), (LAYERS, 8, D), (LAYERS, FF), (LAYERS, 2 * STEMS, D),
+    ]
+    steps = 4
+    moved_through = [blocked(a.shape, a.shape[0] // steps) for a in (gtok, gfeat)]
     return pl.pallas_call(
         unpack_kernel,
-        out_shape=[
-            out(LAYERS, 16, D), out(LAYERS, 16, D), out(LAYERS, 16, D), out(LAYERS, D, 4 * D),
-            out(LAYERS, SQ, D), out(LAYERS, PROP, D), out(LAYERS, 8, D), out(LAYERS, FF),
-            out(LAYERS, 2 * STEMS, D),
-        ],
-        in_specs=[vmem] * 2,
-        out_specs=[vmem] * 9,
-    )(mats, small)
+        grid=(steps,),
+        out_shape=[jax.ShapeDtypeStruct(s, F32) for s in [gtok.shape, gfeat.shape] + outs],
+        in_specs=[whole(mats.shape), whole(small.shape)] + moved_through,
+        out_specs=moved_through + [whole(s) for s in outs],
+    )(mats, small, gtok, gfeat)
 
 
 def pack(attn, up, down, stem, queries, pin):
@@ -985,18 +1146,17 @@
 def body(n, tokens, features, proprio, embodiment, trunk_attn, feedforward_up_weight, mlp_down,
          stem_mats, stem_queries, prop_in, trunk_vectors, mlp_bias, stem_bias, cotangent):
     shards = (trunk_attn, feedforward_up_weight, mlp_down, stem_mats, stem_queries, prop_in)
-    out, gtok, gfeat, gprop, g0, g1 = compute(
+    out, gtok, gfeat, gprop, mats, small = compute(
         tokens, features, proprio, embodiment, shards, trunk_vectors, mlp_bias, stem_bias,
         cotangent, None if n == 32 else pack(*shards),
     )
     if n == 32:
-        *rest, gsb = unpack(*scatter(g0[0], g1[0], g0[1], g1[1]))
-        return (out, gtok, gfeat, gprop, *rest, gsb.reshape(LAYERS, STEMS, 2, D))
+        return (out, gtok, gfeat, gprop, *mats, small.reshape(LAYERS, STEMS, 2, D))
     mats = [
         lax.psum_scatter(a.reshape(LAYERS, -1, a.shape[-1]), "fsdp", scatter_dimension=1, tiled=True)
-        for a in unpack_blocks(jnp.stack([g0[0], g1[0]]).astype(F32))
-    ]
-    small = lax.psum(jnp.stack([g0[1], g1[1]]), "fsdp")
+        for a in unpack_blocks(mats.astype(F32))
+    ]
+    small = lax.psum(small, "fsdp")
     gvec = small[:, :8]
     gmb = small[:, 8:12].reshape(LAYERS, FF)
     gsb = small[:, 16:].reshape(LAYERS, STEMS, 2, D)

time: 223 us -> 197 us (0.88)
  Pallas kernels: 223 us -> 195 us
    pallas_call x2 -> x1, Pallas kernels: 74 us -> 43.3 us  [call(): pl.pallas_call(kernel, grid_spec=pltpu.PrefetchScalarGridSpec(num_scalar_...]
    pallas_call x2, Pallas kernels: 77.7 us -> 86.7 us  [the longest x1 81.5 us: backward_scatter(): pl.pallas_call(backward_scatter_kernel, grid=(steps,), in_specs=[smem] *...]
    pallas_call x1, Pallas kernels: 70.8 us -> 65.3 us  [gather_forward(): pl.pallas_call(gather_forward_kernel, grid=(steps,), in_specs=[smem, bloc...]
where the time goes in v4:
time: 197 us
  Pallas kernels  195 us (99%)
    pallas_call x1, Pallas kernels, backward_scatter(): pl.pallas_call(backward_scatter_kernel, grid=(steps,), in_specs=[smem] *...  81.5 us
    pallas_call x1, Pallas kernels, gather_forward(): pl.pallas_call(gather_forward_kernel, grid=(steps,), in_specs=[smem, bloc...  65.3 us
    pallas_call x1, Pallas kernels, call(): pl.pallas_call(kernel, grid_spec=pltpu.PrefetchScalarGridSpec(num_scalar_...  43.3 us
    pallas_call x1, Pallas kernels, unpack(): pl.pallas_call(unpack_kernel, grid=(steps,), out_shape=[jax.ShapeDtypeStr...  5.25 us

profile of v4, /device:TPU:0, one launch (start us, length us, event | category | flops | bytes accessed | tf_op | source)
XLA Modules:
  0.0 196.6 jit_solution(16703073990030795682)
XLA Ops:
  0.6 65.3 %shard_map.237 = (f32[2048,128]{1,0:T(8,128)}, bf16[4,2,2,2,608,128]{5,4,3,2,1,0:T(8,128)(2,1)}, bf16[4,2,2,2,608,128]{5,4,3,2,1,0:T(8,128)(2,1)}, bf16[64,112,1...) custom-call(s32[64]{0:T(128)} %emb_ref.5, ...), custom_call_target="tpu_custom_call" | custom-call | tf_op jit(solution)/shard_map/pallas_call | solution.py:799
  66.0 43.3 %shard_map.238 = (bf16[2048,128]{1,0:T(8,128)(2,1)}, f32[2048,128]{1,0:T(8,128)}, bf16[64,112,128]{2,1,0:T(8,128)(2,1)}, f32[1024,32]{1,0:T(8,128)}, bf16[32,608...) custom-call(s32[64]{0:T(128)} %emb_ref.5, f32[2048,128]{1,0:T(8,128)} %get-tuple-element.53.hid_ref, ...), custom_call_target="tpu_custom_call" | custom-call | tf_op jit(solution)/shard_map/pallas_call | solution.py:544
  109.2 81.5 %shard_map.239 = (f32[2048,128]{1,0:T(8,128)}, f32[6272,128]{1,0:T(8,128)}, f32[2,32,64]{2,1,0:T(8,128)}, f32[2,608,128]{2,1,0:T(8,128)}, f32[2,80,128]{2,1,0:T(8,128)}) custom-call(s32[64]{0:T(128)} %emb_ref.5, s32[64]{0:T(128)} %get-tuple-element.56.before_ref, s32[32]{0:T(128)} %get-tuple-element.57.last_ref, f32[2048,128]{1,0:T(8,128)} %get-tuple-element.58.grad_ref, ...), custom_call_target="tpu_custom_call" | custom-call | tf_op jit(solution)/shard_map/pallas_call | solution.py:1068
  190.7 0.0 copy-start
  190.8 5.2 %shard_map.240 = (f32[2048,128]{1,0:T(8,128)}, f32[6272,128]{1,0:T(8,128)}, f32[2,16,128]{2,1,0:T(8,128)}, f32[2,16,128]{2,1,0:T(8,128)}, f32[2,16,128]{2,1,0:T(...) custom-call(f32[2,608,128]{2,1,0:T(8,128)} %get-tuple-element.77.mat, ...), custom_call_target="tpu_custom_call" | custom-call | tf_op jit(solution)/shard_map/pallas_call | solution.py:1119
  196.0 0.0 copy-done
  196.0 0.6 copy.28
Async XLA Ops:
  190.7 5.3 %copy-start = (f32[2,32,64]{2,1,0:T(8,128)S(1)}, f32[2,32,64]{2,1,0:T(8,128)}, u32[]{:S(2)}) copy-start(f32[2,32,64]{2,1,0:T(8,128)} %get-tuple-element.83) | copy-start | bytes 49156

commit v5 on v4

--- a/solution.py
+++ b/solution.py
@@ -16,21 +16,23 @@
 FR = 49
 CR = 112
 PROP = 32
-PR = 16
 STEMS = 32
 STEPS = 2
 LAYERS = 2
 TOK = 32
 SB = 16
 
-R_Q = 4 * D
-R_PIN = R_Q + SQ
+R_Q = 3 * D
+R_WP = R_Q + SQ
+R_PIN = R_WP + D
 R_ATT = R_PIN + PROP
 R_UP = R_ATT + 16
 R_DOWN = R_UP + 16
 ROWS = R_DOWN + 16
-STEM_ROWS = R_ATT
+STEM_ROWS = R_WP
 SMALL = 16 + 2 * STEMS
+
+MAT_ROWS = (0, D, 2 * D, R_WP)
 
 F32 = jnp.float32
 BF16 = jnp.bfloat16
@@ -141,33 +143,91 @@
     return weight * (1.0 / jnp.sum(weight, 0, keepdims=True))
 
 
-def forward_block(es, hidden, feat_ref, props, w_ref, vec, mb, sb, tick=None):
+def stem_ids(emb_ref, rows, down=False):
+    samples = emb_ref.shape[1]
+    row = lax.broadcasted_iota(jnp.int32, (rows, samples), 0) // STEPS
+    pick = (row == lax.broadcasted_iota(jnp.int32, (rows, samples), 1)).astype(BF16)
+    stems = jnp.broadcast_to(emb_ref[...].astype(F32).astype(BF16), (D, samples))
+    return dot_nt(stems, pick) if down else dot_nt(pick, stems)
+
+
+def spread(values, ids):
+    values = values.astype(F32)
+    return jnp.concatenate([jnp.where(ids == e, values, 0.0).astype(BF16) for e in range(STEMS)], 1)
+
+
+def sample_rows(samples):
+    shape = (samples * STEPS, samples * STEPS)
+    row = lax.broadcasted_iota(jnp.int32, shape, 0)
+    column = (row % STEPS) * samples + row // STEPS
+    return (lax.broadcasted_iota(jnp.int32, shape, 1) == column).astype(BF16)
+
+
+def spread_down(values, ids):
+    values = values.astype(F32)
+    return jnp.concatenate([jnp.where(ids == e, values, 0.0).astype(BF16) for e in range(STEMS)], 0)
+
+
+def spread_proprio(prop_ref, ids, down=False):
+    both = jnp.concatenate([prop_ref[t] for t in range(STEPS)], 1)
+    group = D // PROP
+    tiled = jnp.concatenate([both] * group, 0)
+    place_ = sample_rows(prop_ref.shape[2])
+    rows = dot_nt(tiled, place_) if down else dot_nt(place_, tiled)
+    entry = (lax.broadcasted_iota(jnp.int32, rows.shape, 0 if down else 1) // PROP).astype(F32)
+    return jnp.concatenate(
+        [jnp.where(ids == entry + float(group * b), rows, 0.0).astype(BF16) for b in range(STEMS // group)],
+        0 if down else 1,
+    )
+
+
+def bias_picks(ids):
+    lane = lax.broadcasted_iota(jnp.int32, (ids.shape[0], 2 * STEMS), 1).astype(F32)
+    twice = 2.0 * ids[:, : 2 * STEMS]
+    return (lane == twice).astype(BF16), (lane == twice + 1.0).astype(BF16)
+
+
+def proprio_forward(emb_ref, prop_ref, w_ref, biases):
+    ids = stem_ids(emb_ref, STEPS * emb_ref.shape[1])
+    first, second = bias_picks(ids)
+    pre = dot(spread_proprio(prop_ref, ids), all_slots(w_ref, R_PIN, R_ATT)) + dot(first, biases)
+    act, slope = gelu_parts(pre)
+    act = act.astype(BF16)
+    return act, slope, dot(spread(act, ids), all_slots(w_ref, R_WP, R_PIN)) + dot(second, biases)
+
+
+def proprio_backward(emb_ref, prop_ref, w_ref, act, slope, grad_rows):
+    ids = stem_ids(emb_ref, STEPS * emb_ref.shape[1])
+    first, second = bias_picks(ids)
+    low = grad_rows.astype(BF16)
+    wp = jnp.concatenate([slot(w_ref, e, R_WP, R_PIN) for e in range(STEMS)], 1)
+    pin = jnp.concatenate([slot(w_ref, e, R_PIN, R_ATT) for e in range(STEMS)], 1)
+    grad_pre = (dot_nt(spread(low, ids), wp) * slope).astype(BF16)
+    down = stem_ids(emb_ref, STEPS * emb_ref.shape[1], True)
+    return (
+        dot(spread_down(act.astype(F32).T, down), low), dot(spread_proprio(prop_ref, down, True), grad_pre),
+        dot_tn(first, grad_pre) + dot_tn(second, low), dot_nt(spread(grad_pre, ids), pin),
+    )
+
+
+def forward_block(es, hidden, feat_ref, prows, w_ref, vec, mb, tick=None):
     kept = {}
-    pre = [
-        dot(props[j * PR : (j + 1) * PR], slot(w_ref, e, R_PIN, R_ATT))
-        + sb(e)[0:1, :]
-        for j, e in enumerate(es)
-    ]
-    pact, pslope = gelu_parts(jnp.concatenate(pre, 0))
-    pact = pact.astype(BF16)
-    kept["pact"], kept["pslope"] = pact, pslope
-    row16 = lax.broadcasted_iota(jnp.int32, (PR, D), 0)
-    prows = [
-        dot(pact[j * PR : (j + 1) * PR], slot(w_ref, e, 3 * D, 4 * D)) + sb(e)[1:2, :]
-        for j, e in enumerate(es)
-    ]
+    row8 = lax.broadcasted_iota(jnp.int32, (8, D), 0)
     contexts = []
     for j in range(SB):
         rows = feat_ref[j * STEPS * FR : (j + 1) * STEPS * FR, :]
-        last = jnp.concatenate([rows[96:98], jnp.zeros((14, D), BF16)], 0).astype(F32)
-        tail = jnp.where(row16 < 2, last, jnp.where(row16 < 4, prows[j], 0.0))
-        contexts.append(jnp.concatenate([rows[:96], tail.astype(BF16)], 0))
+        last = jnp.concatenate([rows[96:98], jnp.zeros((14, D), BF16)], 0).astype(F32)[:8]
+        k = j // 4 * 8
+        mine = pltpu.roll(prows[k : k + 8], (2 - 2 * (j % 4)) % 8, 0)
+        tail = jnp.where(row8 < 2, last, jnp.where(row8 < 4, mine, 0.0))
+        tail = jnp.concatenate([tail, jnp.zeros((8, D), F32)], 0).astype(BF16)
+        contexts.append(jnp.concatenate([rows[:96], tail], 0))
     kept["ctx"] = contexts
     kvs = [dot(contexts[j], stem_kv_weight(w_ref, e)).astype(BF16) for j, e in enumerate(es)]
     kept["kv"] = kvs
     mask16 = head_mask(SQ, 0.25)
     scores = [
-        dot_nt(kvs[j][:, :D], expand(slot(w_ref, e, R_Q, R_PIN), mask16)) for j, e in enumerate(es)
+        dot_nt(kvs[j][:, :D], expand(slot(w_ref, e, R_Q, R_WP), mask16)) for j, e in enumerate(es)
     ]
     valid = lax.broadcasted_iota(jnp.int32, (104, D), 0) < STEPS * (FR + 1)
     pad = jnp.zeros((8, D), F32)
@@ -217,7 +277,7 @@
     return second + (dot(act, down) + vec[7:8]), kept
 
 
-def backward_block(es, grad, kept, props, w_ref, vec, acc, tick=None):
+def backward_block(es, grad, kept, w_ref, vec, acc, tick=None):
     wqkv, wout, up, down = trunk_weights(w_ref)
     out_low = grad.astype(BF16)
     acc["vec"][7] += fold(out_low.astype(F32))
@@ -263,7 +323,6 @@
     stem_grad = grad_first.astype(BF16)
     mask16 = head_mask(SQ, 0.25)
     mask16_one = head_mask(SQ, 1.0)
-    row16 = lax.broadcasted_iota(jnp.int32, (PR, D), 0)
     row8 = lax.broadcasted_iota(jnp.int32, (8, D), 0)
     if tick is not None:
         tick()
@@ -289,41 +348,28 @@
         gp = jnp.where(even, grad_ps[j][:104, :D], grad_ps[j][:104, D:])
         gs = p * step_apply(gp, step_reduce(gp * p, jnp.add), jnp.subtract)
         gss.append(jnp.concatenate([gs, pad], 0).astype(BF16))
-    gks = [dot(gss[j], expand(slot(w_ref, e, R_Q, R_PIN), mask16)) for j, e in enumerate(es)]
+    gks = [dot(gss[j], expand(slot(w_ref, e, R_Q, R_WP), mask16)) for j, e in enumerate(es)]
     gkvs = [
         jnp.concatenate([gks[j], gvs[j]], 1).astype(BF16) for j in range(SB)
     ]
     grad_contexts = [
         dot_nt(gkvs[j], stem_kv_weight(w_ref, e)).astype(BF16) for j, e in enumerate(es)
     ]
-    prows = [
-        jnp.where((row16 == 2) | (row16 == 3), grad_contexts[j][96:112].astype(F32), 0.0)
-        for j in range(SB)
-    ]
-    prow_low = [p.astype(BF16) for p in prows]
-    gpacts = [dot_nt(prow_low[j], slot(w_ref, e, 3 * D, 4 * D)) for j, e in enumerate(es)]
-    gppres = [
-        (gpacts[j] * kept["pslope"][j * PR : (j + 1) * PR]).astype(BF16) for j in range(SB)
-    ]
-    grad_props = [dot_nt(gppres[j], slot(w_ref, e, R_PIN, R_ATT)) for j, e in enumerate(es)]
+    grad_prows = []
+    for k in range(0, SB, 4):
+        rows = jnp.zeros((8, D), F32)
+        for j in range(k, k + 4):
+            tail = pltpu.roll(grad_contexts[j][96:112].astype(F32)[:8], (2 * (j % 4) - 2) % 8, 0)
+            rows = jnp.where(row8 // 2 == j % 4, tail, rows)
+        grad_prows.append(rows)
     grad_q = [contract(dot_tn(gss[j], kvs[j][:, :D]), SQ) * 0.25 for j in range(SB)]
     grad_wkv = [dot_tn(kept["ctx"][j], gkvs[j]) for j in range(SB)]
-    grad_wp = [dot_tn(kept["pact"][j * PR : (j + 1) * PR], prow_low[j]) for j in range(SB)]
-    grad_pin = [dot_tn(props[j * PR : (j + 1) * PR], gppres[j]) for j in range(SB)]
     for j, e in enumerate(es):
-        bias = jnp.where(
-            row8 == 0,
-            jnp.sum(gppres[j].astype(F32), 0, keepdims=True),
-            jnp.where(row8 == 1, jnp.sum(prows[j], 0, keepdims=True), 0.0),
-        )
         acc["add"](
             j, e,
-            (
-                (0, grad_wkv[j][:, :D]), (D, grad_wkv[j][:, D:]), (2 * D, grad_wo[j]),
-                (3 * D, grad_wp[j]), (R_Q, grad_q[j]), (R_PIN, grad_pin[j]), (R_ATT, bias),
-            ),
+            ((0, grad_wkv[j][:, :D]), (D, grad_wkv[j][:, D:]), (2 * D, grad_wo[j]), (R_Q, grad_q[j])),
         )
-    return grad_first, grad_contexts, grad_props
+    return grad_first, grad_contexts, jnp.concatenate(grad_prows, 0)
 
 
 ACC = ("stem", "wqkv", "wout", "up", "down", "vec", "mb")
@@ -331,7 +377,7 @@
 
 def acc_shapes(entries):
     return [
-        pltpu.VMEM((entries, STEM_ROWS + 8, D), F32),
+        pltpu.VMEM((entries, STEM_ROWS, D), F32),
         pltpu.VMEM((D, 3 * D), F32),
         pltpu.VMEM((D, D), F32),
         pltpu.VMEM((D, FF), F32),
@@ -372,20 +418,27 @@
     )
 
 
-def finish(acc, grad_ref, small_ref):
+def other_blocks(acc, grads):
+    grad_wp, grad_pin = grads
+    return (
+        (R_WP, grad_wp.astype(BF16).reshape(STEMS, D, D)),
+        (R_PIN, grad_pin.astype(BF16).reshape(STEMS, PROP, D)),
+    ) + tuple((R_ATT + 16 * i, part) for i, part in enumerate(trunk_blocks(acc)))
+
+
+def finish(acc, grads, bias, grad_ref, small_ref):
     def stem_out(e, carry):
-        grad_ref[e, 0:STEM_ROWS, :] = acc["stem"][e, 0:STEM_ROWS, :].astype(grad_ref.dtype)
+        grad_ref[e, 0:STEM_ROWS, :] = acc["stem"][e].astype(grad_ref.dtype)
         return carry
 
     lax.fori_loop(0, STEMS, stem_out, 0)
-    for i, part in enumerate(trunk_blocks(acc)):
-        grad_ref[:, R_ATT + 16 * i : R_ATT + 16 * (i + 1), :] = part
+    for start, part in other_blocks(acc, grads):
+        grad_ref[:, start : start + part.shape[1], :] = part
     small_ref[0:16, :] = small_rows(acc)
-    for e in range(STEMS):
-        small_ref[16 + 2 * e : 18 + 2 * e, :] = acc["stem"][e, STEM_ROWS : STEM_ROWS + 2, :]
-
-
-SAVED = ("ctx", "kv", "prob", "mix", "first", "qkv", "sprob", "smix", "second", "act", "slope", "pact", "pslope")
+    small_ref[16:SMALL, :] = bias
+
+
+SAVED = ("ctx", "kv", "prob", "mix", "first", "qkv", "sprob", "smix", "second", "act", "slope")
 PER_SAMPLE = ("ctx", "kv", "prob", "sprob")
 
 
@@ -403,40 +456,22 @@
         second=((rows, D), F32),
         act=((rows, FF), BF16),
         slope=((rows, FF), BF16),
-        pact=((samples * PR, D), BF16),
-        pslope=((samples * PR, D), F32),
-    )
-
-
-def step_rows(step, samples):
-    shape = (SB * PR, STEPS * samples)
-    row = lax.broadcasted_iota(jnp.int32, shape, 0)
-    column = (row % PR - 2) * samples + step * SB + row // PR
-    held = (row % PR == 2) | (row % PR == 3)
-    return jnp.where(held & (lax.broadcasted_iota(jnp.int32, shape, 1) == column), 1.0, 0.0).astype(BF16)
-
-
-def prop_block(prop_ref, step):
-    both = jnp.concatenate([prop_ref[t] for t in range(STEPS)], 1)
-    return dot_nt(step_rows(step, prop_ref.shape[2]), both).astype(BF16)
-
-
-def layer_inputs(layer, vec_ref, mb_ref, sb_ref):
-    return (
-        vec_ref[layer].astype(F32), mb_ref[layer : layer + 1, :].astype(F32),
-        lambda e: sb_ref[layer, e].astype(F32),
-    )
-
-
-def forward_kernel(emb_ref, tok_ref, feat_ref, prop_ref, w_ref, vec_ref, mb_ref, sb_ref, out_ref, *rest):
-    saved = rest
-    step = pl.program_id(0)
-    es = [emb_ref[step * SB + j] for j in range(SB)]
-    out, kept = forward_block(
-        es, tok_ref[...].astype(F32), feat_ref, prop_block(prop_ref, step), w_ref,
-        *layer_inputs(0, vec_ref, mb_ref, sb_ref)
-    )
-    out_ref[...] = out
+    )
+
+
+def layer_inputs(layer, vec_ref, mb_ref):
+    return vec_ref[layer].astype(F32), mb_ref[layer : layer + 1, :].astype(F32)
+
+
+def start_forward(layer, emb_ref, prop_ref, w_ref, sb_ref, act_ref, slope_ref, rows_ref):
+    act_ref[...], slope_ref[...], rows_ref[...] = proprio_forward(emb_ref, prop_ref, w_ref, sb_ref[layer])
+
+
+def block_rows(step):
+    return pl.ds(pl.multiple_of(step * SB * STEPS, SB * STEPS), SB * STEPS)
+
+
+def save(kept, saved):
     for name, ref in zip(SAVED, saved):
         if name in PER_SAMPLE:
             for j in range(SB):
@@ -445,6 +480,30 @@
             ref[...] = kept[name].astype(ref.dtype)
 
 
+def load(saved):
+    return {
+        name: [ref[j] for j in range(SB)] if name in PER_SAMPLE else ref[...]
+        for name, ref in zip(SAVED, saved)
+    }
+
+
+def forward_kernel(
+    emb_ref, ids_ref, tok_ref, feat_ref, prop_ref, w_ref, vec_ref, mb_ref, sb_ref, out_ref, act_ref, slope_ref, *rest
+):
+    saved, rows_ref = rest[:-1], rest[-1]
+    step = pl.program_id(0)
+    pl.when(step == 0)(
+        lambda: start_forward(0, ids_ref, prop_ref, w_ref, sb_ref, act_ref, slope_ref, rows_ref)
+    )
+    es = [emb_ref[step * SB + j] for j in range(SB)]
+    out, kept = forward_block(
+        es, tok_ref[...].astype(F32), feat_ref, rows_ref[block_rows(step), :], w_ref,
+        *layer_inputs(0, vec_ref, mb_ref)
+    )
+    out_ref[...] = out
+    save(kept, saved)
+
+
 def link_samples(emb_ref, before_ref, last_ref):
     def unset(e, carry):
         last_ref[e] = -1
@@ -461,8 +520,9 @@
 
 
 def middle_kernel(
-    emb_ref, hid_ref, feat_ref, prop_ref, w_ref, vec_ref, mb_ref, sb_ref, cot_ref,
-    out_ref, ghid_ref, gfeat_ref, gprop_ref, gw_ref, gsmall_ref, before_ref, last_ref, *accs
+    emb_ref, ids_ref, hid_ref, feat_ref, prop_ref, w_ref, vec_ref, mb_ref, sb_ref, cot_ref,
+    out_ref, ghid_ref, gfeat_ref, gprop_ref, gw_ref, gsmall_ref, before_ref, last_ref,
+    act_ref, slope_ref, rows_ref, grows_ref, *accs
 ):
     step = pl.program_id(0)
     acc = dict(zip(ACC, accs))
@@ -471,62 +531,73 @@
     def _():
         clear(acc)
         link_samples(emb_ref, before_ref, last_ref)
+        start_forward(1, ids_ref, prop_ref, w_ref, sb_ref, act_ref, slope_ref, rows_ref)
 
     es = [emb_ref[step * SB + j] for j in range(SB)]
-    vec, mb, sb = layer_inputs(1, vec_ref, mb_ref, sb_ref)
-    props = prop_block(prop_ref, step)
-    out, kept = forward_block(es, hid_ref[...], feat_ref, props, w_ref, vec, mb, sb)
+    vec, mb = layer_inputs(1, vec_ref, mb_ref)
+    out, kept = forward_block(
+        es, hid_ref[...], feat_ref, rows_ref[block_rows(step), :], w_ref, vec, mb
+    )
     out_ref[...] = out.astype(BF16)
-    ghid, gctx, gprop = backward_block(es, cot_ref[...].astype(F32), kept, props, w_ref, vec, add_in_place(acc))
+    ghid, gctx, grows = backward_block(
+        es, cot_ref[...].astype(F32), kept, w_ref, vec, add_in_place(acc)
+    )
     ghid_ref[...] = ghid
+    grows_ref[block_rows(step), :] = grows
     for j in range(SB):
         gfeat_ref[j] = gctx[j]
-        gprop_ref[j * PR : (j + 1) * PR, :] = gprop[j]
-    pl.when(step == pl.num_programs(0) - 1)(lambda: finish(acc, gw_ref, gsmall_ref))
-
-
-def backward_kernel(emb_ref, grad_ref, prop_ref, w_ref, vec_ref, gfeat1_ref, gprop1_ref, *rest):
-    n = len(SAVED)
-    saved = rest[:n]
-    gtok_ref, gfeat_ref, gprop_ref, gw_ref, gsmall_ref, gprops = rest[n : n + 6]
-    acc = dict(zip(ACC, rest[n + 6 :]))
-    step = pl.program_id(0)
-
-    pl.when(step == 0)(lambda: clear(acc))
-
-    es = [emb_ref[step * SB + j] for j in range(SB)]
-    kept = {name: [ref[j] for j in range(SB)] if name in PER_SAMPLE else ref[...] for name, ref in zip(SAVED, saved)}
-    props = prop_block(prop_ref, step)
-    vec = vec_ref[0].astype(F32)
-    ghid, gctx, gprop = backward_block(es, grad_ref[...], kept, props, w_ref, vec, add_in_place(acc))
-    gtok_ref[...] = ghid
+
+    @pl.when(step == pl.num_programs(0) - 1)
+    def _():
+        *grads, bias, gprop_ref[...] = proprio_backward(
+            ids_ref, prop_ref, w_ref, act_ref[...], slope_ref[...], grows_ref[...]
+        )
+        finish(acc, grads, bias, gw_ref, gsmall_ref)
+
+
+def write_features(gctx, gfeat1_ref, gfeat_ref):
     for j in range(0, SB, 4):
         totals = [gctx[i].astype(F32) + gfeat1_ref[i].astype(F32) for i in range(j, j + 4)]
         gfeat_ref[j * STEPS * FR : (j + 4) * STEPS * FR, :] = jnp.concatenate(
             [total[: STEPS * FR] for total in totals], 0
         )
-    add_proprio(jnp.concatenate(gprop, 0) + gprop1_ref[...], gprops, step)
-
-    @pl.when(step == pl.num_programs(0) - 1)
-    def _():
-        finish(acc, gw_ref, gsmall_ref)
-        write_proprio(gprops, gprop_ref)
-
-
-def add_proprio(rows, gprops, step):
-    place_ = step_rows(step, gprops.shape[1] // STEPS)
+
+
+def write_proprio(rows, gprop_ref):
+    samples = gprop_ref.shape[2]
+    place_ = sample_rows(samples)
     high = rows.astype(BF16)
     rest = rows - high.astype(F32)
     middle = rest.astype(BF16)
     low = (rest - middle.astype(F32)).astype(BF16)
-    part = dot_tn(high, place_) + (dot_tn(middle, place_) + dot_tn(low, place_))
-    gprops[...] = jnp.where(step == 0, part, gprops[...] + part)
-
-
-def write_proprio(gprops, gprop_ref):
-    samples = gprop_ref.shape[2]
+    out = dot_tn(high, place_) + (dot_tn(middle, place_) + dot_tn(low, place_))
     for t in range(STEPS):
-        gprop_ref[t] = gprops[:, t * samples : (t + 1) * samples]
+        gprop_ref[t] = out[:, t * samples : (t + 1) * samples]
+
+
+def backward_kernel(
+    emb_ref, ids_ref, grad_ref, prop_ref, w_ref, vec_ref, gfeat1_ref, gprop1_ref, act_ref, slope_ref, *rest
+):
+    n = len(SAVED)
+    saved = rest[:n]
+    gtok_ref, gfeat_ref, gprop_ref, gw_ref, gsmall_ref, grows_ref = rest[n : n + 6]
+    acc = dict(zip(ACC, rest[n + 6 :]))
+    step = pl.program_id(0)
+    pl.when(step == 0)(lambda: clear(acc))
+    es = [emb_ref[step * SB + j] for j in range(SB)]
+    vec = vec_ref[0].astype(F32)
+    ghid, gctx, grows = backward_block(es, grad_ref[...], load(saved), w_ref, vec, add_in_place(acc))
+    gtok_ref[...] = ghid
+    grows_ref[block_rows(step), :] = grows
+    write_features(gctx, gfeat1_ref, gfeat_ref)
+
+    @pl.when(step == pl.num_programs(0) - 1)
+    def _():
+        *grads, bias, gprop = proprio_backward(
+            ids_ref, prop_ref, w_ref, act_ref[...], slope_ref[...], grows_ref[...]
+        )
+        finish(acc, grads, bias, gw_ref, gsmall_ref)
+        write_proprio(gprop + gprop1_ref[...], gprop_ref)
 
 
 def blocked(shape, per_step):
@@ -568,32 +639,36 @@
     tok = tokens.reshape(rows, D)
     feat = jnp.swapaxes(features, 1, 2).reshape(samples * FR * STEPS, D)
     prop = proprio.transpose(1, 2, 0)
+    ids = emb.reshape(1, samples)
+    sbs = sbs.reshape(LAYERS, 2 * STEMS, D)
     fb = SB * FR * STEPS
+    prows = (STEPS * samples, D)
     shapes = saved_shapes(samples)
     per = lambda s: s[0] // steps
+    forward_ins = [(ids, 0), (tok, rb), (feat, fb), (prop, 0), (vecs, 0), (mbs, 0), (sbs, 0)]
+    forward_outs = [((rows, D), F32, rb), (prows, BF16, 0), (prows, F32, 0)] + [
+        (shapes[n][0], shapes[n][1], per(shapes[n][0])) for n in SAVED
+    ]
     if weights is None:
-        hidden, saved, w0, w1 = gather_forward(tok, feat, prop, emb, vecs, mbs, sbs, shards)
+        hidden, act, slope, w0, w1, *saved = gather_forward(steps, emb, forward_ins, forward_outs, shards)
     else:
         w0, w1 = weights
-        saved_outs = [(shapes[n][0], shapes[n][1], per(shapes[n][0])) for n in SAVED]
-        res = call(
-            forward_kernel, steps, emb,
-            [(tok, rb), (feat, fb), (prop, 0), (w0, 0), (vecs, 0), (mbs, 0), (sbs, 0)],
-            [((rows, D), F32, rb)] + saved_outs, [],
+        forward_ins = forward_ins[:4] + [(w0, 0)] + forward_ins[4:]
+        hidden, act, slope, *saved = call(
+            forward_kernel, steps, emb, forward_ins, forward_outs, [pltpu.VMEM(prows, F32)]
         )
-        hidden, saved = res[0], res[1:]
     grad_outs = [((STEMS, ROWS, D), BF16, 0), ((SMALL, D), F32, 0)]
     out, ghid, gfeat1, gprop1, *grads1, before, last = call(
         middle_kernel, steps, emb,
-        [(hidden, rb), (feat, fb), (prop, 0), (w1, 0), (vecs, 0), (mbs, 0), (sbs, 0),
+        [(ids, 0), (hidden, rb), (feat, fb), (prop, 0), (w1, 0), (vecs, 0), (mbs, 0), (sbs, 0),
          (cot.reshape(rows, D), rb)],
         [((rows, D), BF16, rb), ((rows, D), F32, rb), ((samples, CR, D), BF16, SB),
-         ((samples * PR, PROP), F32, SB * PR)] + grad_outs
+         ((STEPS * samples, PROP), F32, 0)] + grad_outs
         + [((samples,), jnp.int32, None), ((STEMS,), jnp.int32, None)],
-        acc_shapes(STEMS),
+        [pltpu.VMEM(prows, BF16)] + [pltpu.VMEM(prows, F32)] * 3 + acc_shapes(STEMS),
     )
     backward_ins = (
-        [(ghid, rb), (prop, 0), (w0, 0), (vecs, 0), (gfeat1, SB), (gprop1, SB * PR)]
+        [(ids, 0), (ghid, rb), (prop, 0), (w0, 0), (vecs, 0), (gfeat1, SB), (gprop1, 0), (act, 0), (slope, 0)]
         + [(a, per(a.shape)) for a in saved]
     )
     backward_outs = [
@@ -607,7 +682,7 @@
     else:
         gtok, gfeat, gprop, *grads0 = call(
             backward_kernel, steps, emb, backward_ins, backward_outs + grad_outs,
-            [pltpu.VMEM((PROP, STEPS * samples), F32)] + acc_shapes(STEMS),
+            [pltpu.VMEM(prows, F32)] + acc_shapes(STEMS),
         )
         mats, small = (jnp.stack(pair) for pair in zip(grads0, grads1))
     gfeat = jnp.swapaxes(gfeat.reshape(samples, FR, STEPS, D), 1, 2)
@@ -705,22 +780,14 @@
 
 
 BOUNDS = (0, 160, 320, 480, ROWS)
-GATHER_GROUPS = chunks_of(0, BOUNDS) + chunks_of(1, BOUNDS)
+HALVES = (0, 320, ROWS)
+GATHER_GROUPS = chunks_of(0, BOUNDS) + chunks_of(1, HALVES)
 GATHER_FIRST = (
     (0, 0), (1, 0), (0, 1), (2, 0), (1, 1), (0, 2), (3, 0), (2, 1), (1, 2), (0, 3), (4, 0), (3, 1), (2, 2),
-    (1, 3), (0, 4), (5, 0), (3, 2), (4, 1), (2, 3), (1, 4), (6, 0), (5, 1), (3, 3), (2, 4), (7, 0), (3, 4),
+    (5, 0), (1, 3), (0, 4), (3, 2), (2, 3), (1, 4), (4, 1), (3, 3), (2, 4), (5, 1), (3, 4),
 )
-GATHER_LATER = (
-    ((4, 2), (6, 1)),
-    ((7, 1),),
-    ((5, 2),),
-    ((6, 2),),
-    ((4, 3),),
-    ((7, 2),),
-    ((5, 3),),
-    ((6, 3),),
-)
-GATHER_END = ((7, 3), (4, 4), (5, 4), (6, 4), (7, 4))
+GATHER_LATER = ((), ((4, 2),), (), ((5, 2),), (), (), ((4, 3),), ())
+GATHER_END = ((5, 3), (4, 4), (5, 4))
 
 
 def place_own(at, shards, outs, local_sem):
@@ -729,7 +796,7 @@
     for layer in range(LAYERS):
         own = outs[layer].at[at["z"], at["y"], at["x"], at["c"]]
         pieces = [
-            (stem.at[layer, :, pl.ds(j * D, D)], j * D, D) for j in range(4)
+            (stem.at[layer, :, pl.ds(j * D, D)], row, D) for j, row in enumerate(MAT_ROWS)
         ] + [
             (q.at[layer], R_Q, SQ), (pin.at[layer], R_PIN, PROP), (att.at[layer], R_ATT, 16),
             (up.at[layer], R_UP, 16), (down.at[layer], R_DOWN, 16),
@@ -741,13 +808,14 @@
     return copies
 
 
-def gather_forward_kernel(emb_ref, tok_ref, feat_ref, prop_ref, vec_ref, mb_ref, sb_ref, *rest):
-    shards, (out_ref, g0, g1), rest = rest[:6], rest[6:9], rest[9:]
-    saved, (w_ref, local_sem, send_sem, recv_sem, keep_sem) = rest[:-5], rest[-5:]
+def gather_forward_kernel(emb_ref, ids_ref, tok_ref, feat_ref, prop_ref, vec_ref, mb_ref, sb_ref, *rest):
+    shards, (out_ref, act_ref, slope_ref, g0, g1), rest = rest[:6], rest[6:11], rest[11:]
+    saved, (rows_ref, w_ref, local_sem, send_sem, recv_sem, keep_sem) = rest[:-6], rest[-6:]
     step = pl.program_id(0)
     at = place()
     move = Gather(at, (w_ref, g1), GATHER_GROUPS, send_sem, recv_sem)
     keep = pltpu.make_async_copy(w_ref, g0, keep_sem)
+
     @pl.when(step == 0)
     def _():
         local = place_own(at, shards, (w_ref, g1), local_sem)
@@ -758,6 +826,7 @@
             copy.wait()
         move.run(GATHER_FIRST)
         keep.start()
+        start_forward(0, ids_ref, prop_ref, w_ref, sb_ref, act_ref, slope_ref, rows_ref)
 
     def moves_at(half):
         for i in range(len(GATHER_LATER) // 2):
@@ -766,16 +835,11 @@
     moves_at(0)
     es = [emb_ref[step * SB + j] for j in range(SB)]
     out, kept = forward_block(
-        es, tok_ref[...].astype(F32), feat_ref, prop_block(prop_ref, step), w_ref,
-        *layer_inputs(0, vec_ref, mb_ref, sb_ref), tick=lambda: moves_at(1)
+        es, tok_ref[...].astype(F32), feat_ref, rows_ref[block_rows(step), :], w_ref,
+        *layer_inputs(0, vec_ref, mb_ref), tick=lambda: moves_at(1)
     )
     out_ref[...] = out
-    for name, ref in zip(SAVED, saved):
-        if name in PER_SAMPLE:
-            for j in range(SB):
-                ref[j] = kept[name][j].astype(ref.dtype)
-        else:
-            ref[...] = kept[name].astype(ref.dtype)
+    save(kept, saved)
 
     @pl.when(step == pl.num_programs(0) - 1)
     def _():
@@ -784,41 +848,37 @@
         move.close()
 
 
-def gather_forward(tokens, feat, prop, emb, vecs, mbs, sbs, shards):
-    samples = emb.shape[0]
-    steps = samples // SB
-    assert steps == 4
-    rows = samples * TOK
-    shapes = saved_shapes(samples)
+def gather_forward(steps, emb, ins, outs, shards):
+    assert 2 * steps == len(GATHER_LATER)
     lead = (4, 2, 2, 2, ROWS, D)
     any_spec = pl.BlockSpec(memory_space=pl.ANY)
     smem = pl.BlockSpec(memory_space=pltpu.SMEM)
-    saved = [(shapes[n][0], shapes[n][1], shapes[n][0][0] // steps) for n in SAVED]
-    outs = [((rows, D), F32, SB * TOK)] + saved
     weights = jax.ShapeDtypeStruct(lead, BF16)
+    ins = ins + [(a, 0) for a in shards]
+    specs = [blocked(s, n) if n else whole(s) for s, _, n in outs]
+    shapes = [jax.ShapeDtypeStruct(s, d) for s, d, _ in outs]
+    groups = 2 * len(GATHER_GROUPS)
     res = pl.pallas_call(
         gather_forward_kernel,
         grid=(steps,),
-        in_specs=[smem, blocked(tokens.shape, SB * TOK), blocked(feat.shape, SB * FR * STEPS)]
-        + [whole(a.shape) for a in (prop, vecs, mbs, sbs) + tuple(shards)],
-        out_specs=[blocked(*((outs[0][0], outs[0][2]))), any_spec, any_spec]
-        + [blocked(s, n) for s, _, n in outs[1:]],
-        out_shape=[jax.ShapeDtypeStruct(*outs[0][:2]), weights, weights]
-        + [jax.ShapeDtypeStruct(s, d) for s, d, _ in outs[1:]],
+        in_specs=[smem] + [blocked(a.shape, n) if n else whole(a.shape) for a, n in ins],
+        out_specs=specs[:3] + [any_spec, any_spec] + specs[3:],
+        out_shape=shapes[:3] + [weights, weights] + shapes[3:],
         scratch_shapes=[
+            pltpu.VMEM(outs[2][0], F32),
             pltpu.VMEM(lead, BF16),
             pltpu.SemaphoreType.DMA((LAYERS, 9)),
-            pltpu.SemaphoreType.DMA((2 * len(GATHER_GROUPS), 4, 3)),
-            pltpu.SemaphoreType.DMA((2 * len(GATHER_GROUPS), 4, 3)),
+            pltpu.SemaphoreType.DMA((groups, 4, 3)),
+            pltpu.SemaphoreType.DMA((groups, 4, 3)),
             pltpu.SemaphoreType.DMA(()),
         ],
         compiler_params=pltpu.CompilerParams(
             dimension_semantics=("arbitrary",), vmem_limit_bytes=VMEM_LIMIT, collective_id=0,
             has_side_effects=True,
         ),
-    )(emb, tokens, feat, prop, vecs, mbs, sbs, *shards)
-    hidden, w0, w1 = res[:3]
-    return hidden, res[3:], w0.reshape(STEMS, ROWS, D), w1.reshape(STEMS, ROWS, D)
+    )(emb, *[a for a, _ in ins])
+    hidden, act, slope, w0, w1, *saved = res
+    return (hidden, act, slope, w0.reshape(STEMS, ROWS, D), w1.reshape(STEMS, ROWS, D), *saved)
 
 
 class Scatter:
@@ -858,31 +918,15 @@
             _, row, count, _ = chunk
             axis, left = self.order(chunk)[phase], self.left(chunk, phase)
             rows = (pl.ds(row, count), slice(None))
-            total = 1
-            for a in left:
-                total *= SIZES[a]
-
-            def one(i, carry):
-                spot = dict(self.at)
-                rest = i
-                for a in left[::-1]:
-                    spot[a] = rest % SIZES[a]
-                    rest = rest // SIZES[a]
-                keep = (spot["z"], spot["y"], spot["x"])
-                value = self.acc[keep + rows].astype(F32)
-                if axis == "z":
-                    for by in range(SIZES["z"] - 1):
-                        value = value + self.lands[3][(by,) + rows].astype(F32)
-                    self.out[rows] = value
-                else:
-                    land = tuple(spot[a] for a in left)
-                    self.acc[keep + rows] = (value + self.lands[phase][land + rows].astype(F32)).astype(BF16)
-                return carry
-
-            if total == 1:
-                one(0, 0)
+            keep = tuple(slice(None) if a in left else self.at[a] for a in "zyx") + rows
+            value = self.acc[keep].astype(F32)
+            if axis == "z":
+                for by in range(SIZES["z"] - 1):
+                    value = value + self.lands[3][(by,) + rows].astype(F32)
+                self.out[rows] = value
             else:
-                lax.fori_loop(0, total, one, 0)
+                land = (slice(None),) * len(left) + rows
+                self.acc[keep] = (value + self.lands[phase][land].astype(F32)).astype(BF16)
 
     def small_copies(self, phase, arriving):
         axis = "cxyz"[phase]
@@ -920,38 +964,33 @@
                 copy.wait_send()
 
 
-SCATTER_GROUPS = chunks_of(0, BOUNDS)
+SCATTER_GROUPS = (chunks_of(0, BOUNDS), chunks_of(1, HALVES))
 SCATTER_BESIDE = (
-    ((0, 0), (1, 0), (2, 0), (3, 0), (-1, 0)),
-    ((0, 1), (1, 1), (-1, 1)),
-    ((2, 1), (3, 1), (-1, 2)),
+    ((1, 0), (0, 0), (-1, 0)),
+    ((-1, 1),),
+    ((0, 1), (-1, 2)),
+    ((1, 1), (-1, 3)),
+    ((-1, 4),),
+    ((0, 2),),
+    ((1, 2),),
     (),
-    ((0, 2), (1, 2), (-1, 3)),
-    ((2, 2), (-1, 4)),
-    ((3, 2),),
-    ((0, 3), (1, 3)),
 )
-SCATTER_END = ((2, 3), (3, 3))
-
-
-def scatter_last():
-    n = len(SCATTER_GROUPS)
-    for t in range(n + 4):
-        for phase in range(5):
-            if 0 <= t - phase < n:
-                yield 0, t - phase, phase
-        if t < 5:
-            yield 0, -1, t
-        if 2 <= t < 2 + n:
-            yield 1, t - 2, 4
-
-
-def backward_scatter_kernel(emb_ref, before_ref, last_ref, grad_ref, prop_ref, w_ref, vec_ref, gfeat1_ref, gprop1_ref, *rest):
+SCATTER_END = (
+    (0, 0, 0), (0, -1, 0), (1, 0, 3), (0, 1, 0), (0, 0, 1), (0, -1, 1), (0, 2, 0), (1, 1, 3), (0, 1, 1), (0, 0, 2),
+    (0, -1, 2), (0, 3, 0), (0, 2, 1), (1, 0, 4), (0, 1, 2), (1, 1, 4), (0, 0, 3), (0, -1, 3), (0, 3, 1), (0, 2, 2),
+    (0, 1, 3), (0, 0, 4), (0, -1, 4), (0, 3, 2), (0, 2, 3), (0, 1, 4), (0, 3, 3), (0, 2, 4), (0, 3, 4),
+)
+
+
+def backward_scatter_kernel(
+    emb_ref, before_ref, last_ref, ids_ref, grad_ref, prop_ref, w_ref, vec_ref, gfeat1_ref, gprop1_ref,
+    act_ref, slope_ref, *rest
+):
     n = len(SAVED)
     saved, (g1, s1), rest = rest[:n], rest[n : n + 2], rest[n + 2 :]
-    (gtok_ref, gfeat_ref, gprop_ref, mats_ref, small_ref, gprops), rest = rest[:6], rest[6:]
+    (gtok_ref, gfeat_ref, gprop_ref, mats_ref, small_ref, grows_ref), rest = rest[:6], rest[6:]
     acc, rest = dict(zip(ACC, rest[: len(ACC)])), rest[len(ACC) :]
-    trunk, sbuf, own_sem = rest[:3]
+    others, sbuf, own_sem = rest[:3]
     per_layer = rest[3:]
     step = pl.program_id(0)
     samples = before_ref.shape[0]
@@ -961,7 +1000,7 @@
         accum, r0, r1, r2, r3, sm, smr, smz, *sems = per_layer[12 * layer : 12 * (layer + 1)]
         source = (lambda c: g1.at[:, :, :, c]) if layer else (lambda c: sbuf)
         return Scatter(
-            at, SCATTER_GROUPS, source, accum, (r0, r1, r2, r3), mats_ref.at[layer],
+            at, SCATTER_GROUPS[layer], source, accum, (r0, r1, r2, r3), mats_ref.at[layer],
             (sm, smr, smz, small_ref.at[layer]), sems,
         )
 
@@ -993,54 +1032,51 @@
             old = stem[jnp.maximum(befores[j], 0), row : row + value.shape[0], :]
             stem[step * SB + j, row : row + value.shape[0], :] = value + jnp.where(befores[j] >= 0, old, 0.0)
 
-    kept = {
-        name: [ref[j] for j in range(SB)] if name in PER_SAMPLE else ref[...]
-        for name, ref in zip(SAVED, saved)
-    }
-    props = prop_block(prop_ref, step)
-    ghid, gctx, gprop = backward_block(
-        es, grad_ref[...], kept, props, w_ref, vec_ref[0].astype(F32), {**acc, "add": add}, lambda: moves_at(1)
+    ghid, gctx, grows = backward_block(
+        es, grad_ref[...], load(saved), w_ref, vec_ref[0].astype(F32), {**acc, "add": add},
+        lambda: moves_at(1)
     )
     gtok_ref[...] = ghid
-    for j in range(0, SB, 4):
-        totals = [gctx[i].astype(F32) + gfeat1_ref[i].astype(F32) for i in range(j, j + 4)]
-        gfeat_ref[j * STEPS * FR : (j + 4) * STEPS * FR, :] = jnp.concatenate(
-            [total[: STEPS * FR] for total in totals], 0
-        )
-    add_proprio(jnp.concatenate(gprop, 0) + gprop1_ref[...], gprops, step)
+    grows_ref[block_rows(step), :] = grows
+    write_features(gctx, gfeat1_ref, gfeat_ref)
 
     def gather_group(g):
         start, stop = BOUNDS[g], BOUNDS[g + 1]
-        middle = min(stop, STEM_ROWS)
-
-        def one(i, carry):
-            spot = (i // 4, (i // 2) % 2, i % 2)
-            for ref, c in ((first.acc, at["c"]), (sbuf, 1 - at["c"])):
-                e = 2 * i + c
-                s = last_ref[e]
-                value = stem[jnp.maximum(s, 0), start:middle, :]
-                ref[spot + (slice(start, middle), slice(None))] = jnp.where(s >= 0, value, 0.0).astype(BF16)
-                if stop > middle:
-                    ref[spot + (slice(middle, stop), slice(None))] = trunk[e]
+
+        def line(z, carry):
+            for i in range(4):
+                spot = (z, i // 2, i % 2)
+                for ref, c in ((first.acc, at["c"]), (sbuf, 1 - at["c"])):
+                    e = 8 * z + 2 * i + c
+                    s = last_ref[e]
+                    if start < STEM_ROWS:
+                        end = min(stop, STEM_ROWS)
+                        value = stem[jnp.maximum(s, 0), start:end, :]
+                        ref[spot + (slice(start, end), slice(None))] = jnp.where(s >= 0, value, 0.0).astype(BF16)
+                    if stop > STEM_ROWS:
+                        begin = max(start, STEM_ROWS)
+                        ref[spot + (slice(begin, stop), slice(None))] = others[
+                            e, begin - STEM_ROWS : stop - STEM_ROWS, :
+                        ]
             return carry
 
-        lax.fori_loop(0, STEMS // 2, one, 0)
+        lax.fori_loop(0, SIZES["z"], line, 0)
 
     @pl.when(step == pl.num_programs(0) - 1)
     def _():
-        for i, part in enumerate(trunk_blocks(acc)):
-            trunk[:, 16 * i : 16 * (i + 1), :] = part
+        *grads, bias, gprop = proprio_backward(
+            ids_ref, prop_ref, w_ref, act_ref[...], slope_ref[...], grows_ref[...]
+        )
+        for row, part in other_blocks(acc, grads):
+            row -= STEM_ROWS
+            others[:, row : row + part.shape[1], :] = part
         first.sm[0, 0:16, :] = small_rows(acc)
-        for e in range(STEMS):
-            s = last_ref[e]
-            value = stem[jnp.maximum(s, 0), STEM_ROWS : STEM_ROWS + 8, :]
-            first.sm[0, 16 + 2 * e : 18 + 2 * e, :] = jnp.where(s >= 0, value, 0.0)[0:2]
-        second.run(SCATTER_END)
-        for layer, g, phase in scatter_last():
+        first.sm[0, 16:SMALL, :] = bias
+        for layer, g, phase in SCATTER_END:
             if phase == 0 and g >= 0:
                 gather_group(g)
             (first, second)[layer].run(((g, phase),))
-        write_proprio(gprops, gprop_ref)
+        write_proprio(gprop + gprop1_ref[...], gprop_ref)
         second.close()
         first.close()
 
@@ -1060,8 +1096,8 @@
         pltpu.VMEM((4, SMALL, D), F32),
         pltpu.VMEM((3, SMALL, D), F32),
         pltpu.VMEM((4, SMALL, D), F32),
-        pltpu.SemaphoreType.DMA((2 * len(SCATTER_GROUPS), 4, 3)),
-        pltpu.SemaphoreType.DMA((2 * len(SCATTER_GROUPS), 4, 3)),
+        pltpu.SemaphoreType.DMA((2 * len(BOUNDS), 4, 3)),
+        pltpu.SemaphoreType.DMA((2 * len(BOUNDS), 4, 3)),
         pltpu.SemaphoreType.DMA((4, 3)),
         pltpu.SemaphoreType.DMA((4, 3)),
     ]
@@ -1072,9 +1108,9 @@
         + [any_spec, whole(s1.shape)],
         out_specs=[blocked(s, n) if n else whole(s) for s, _, n in outs],
         out_shape=[jax.ShapeDtypeStruct(s, d) for s, d, _ in outs],
-        scratch_shapes=[pltpu.VMEM((PROP, STEPS * samples), F32)] + acc_shapes(samples)
+        scratch_shapes=[pltpu.VMEM((STEPS * samples, D), F32)] + acc_shapes(samples)
         + [
-            pltpu.VMEM((STEMS, 48, D), BF16),
+            pltpu.VMEM((STEMS, ROWS - STEM_ROWS, D), BF16),
             pltpu.VMEM((4, 2, 2, ROWS, D), BF16),
             pltpu.SemaphoreType.DMA(()),
         ]
@@ -1096,9 +1132,9 @@
 
 def split_gradients(mats, small, att, up, down, stem, q, pin, vec, mb, sb):
     for layer in range(LAYERS):
-        for j in range(4):
-            stem[layer, :, j * D : (j + 1) * D] = mats[layer, j * D : (j + 1) * D, :]
-        q[layer] = mats[layer, R_Q:R_PIN, :]
+        for j, row in enumerate(MAT_ROWS):
+            stem[layer, :, j * D : (j + 1) * D] = mats[layer, row : row + D, :]
+        q[layer] = mats[layer, R_Q:R_WP, :]
         pin[layer] = mats[layer, R_PIN:R_ATT, :]
         att[layer] = mats[layer, R_ATT:R_UP, :]
         up[layer] = mats[layer, R_UP:R_DOWN, :]
@@ -1129,17 +1165,15 @@
     gathered = [lax.all_gather(a, "fsdp", axis=1, tiled=True) for a in (attn, up, down, stem, queries, pin)]
     attn, up, down, stem, queries, pin = gathered
     stem = stem.reshape(LAYERS, STEMS, D, 4, D).transpose(0, 1, 3, 2, 4).reshape(LAYERS, STEMS, 4 * D, D)
-    parts = [stem] + [a.reshape(LAYERS, STEMS, -1, D) for a in (queries, pin, attn, up, down)]
-    return jnp.concatenate(parts, 2)
+    queries, *parts = [a.reshape(LAYERS, STEMS, -1, D) for a in (queries, pin, attn, up, down)]
+    return jnp.concatenate([stem[:, :, : 3 * D], queries, stem[:, :, 3 * D :], *parts], 2)
 
 
 def unpack_blocks(grad):
-    lead = grad.shape[:-2]
-    stem = grad[..., : 4 * D, :].reshape(lead + (4, D, D))
-    stem = jnp.swapaxes(stem, -3, -2).reshape(lead + (D, 4 * D))
+    stem = jnp.concatenate([grad[..., row : row + D, :] for row in MAT_ROWS], -1)
     return (
         grad[..., R_ATT:R_UP, :], grad[..., R_UP:R_DOWN, :], grad[..., R_DOWN:ROWS, :],
-        stem, grad[..., R_Q:R_PIN, :], grad[..., R_PIN:R_ATT, :],
+        stem, grad[..., R_Q:R_WP, :], grad[..., R_PIN:R_ATT, :],
     )
 
 

time: 197 us -> 192 us (0.975)
  Pallas kernels: 195 us -> 190 us
    pallas_call x1, Pallas kernels: 43.3 us -> 39.7 us  [call(): pl.pallas_call(kernel, grid_spec=pltpu.PrefetchScalarGridSpec(num_scalar_...]
where the time goes in v5:
time: 192 us; the launch traced here: 191 us
  Pallas kernels  190 us (99%)
    pallas_call x1, Pallas kernels, backward_scatter(): pl.pallas_call(backward_scatter_kernel, grid=(steps,), in_specs=[smem] *...  80.2 us
    pallas_call x1, Pallas kernels, gather_forward(): pl.pallas_call(gather_forward_kernel, grid=(steps,), in_specs=[smem] + [b...  64.8 us
    pallas_call x1, Pallas kernels, call(): pl.pallas_call(kernel, grid_spec=pltpu.PrefetchScalarGridSpec(num_scalar_...  39.7 us
    pallas_call x1, Pallas kernels, unpack(): pl.pallas_call(unpack_kernel, grid=(steps,), out_shape=[jax.ShapeDtypeStr...  5.25 us

profile of v5, /device:TPU:0, one launch (start us, length us, event | category | flops | bytes accessed | tf_op | source)
XLA Modules:
  0.0 191.3 jit_solution(72796684249048229)
XLA Ops:
  0.6 64.8 %shard_map.237 = (f32[2048,128]{1,0:T(8,128)}, bf16[128,128]{1,0:T(8,128)(2,1)}, f32[128,128]{1,0:T(8,128)}, bf16[4,2,2,2,608,128]{5,4,3,2,1,0:T(8,128)(2,1)}, b...) custom-call(s32[64]{0:T(128)} %emb_ref.5, ...), custom_call_target="tpu_custom_call" | custom-call | tf_op jit(solution)/shard_map/pallas_call | solution.py:861
  65.4 39.7 %shard_map.238 = (bf16[2048,128]{1,0:T(8,128)(2,1)}, f32[2048,128]{1,0:T(8,128)}, bf16[64,112,128]{2,1,0:T(8,128)(2,1)}, f32[128,32]{1,0:T(8,128)}, bf16[32,608,...) custom-call(s32[64]{0:T(128)} %emb_ref.5, s32[1,64]{1,0:T(1,128)} %bitcast.32, ...), custom_call_target="tpu_custom_call" | custom-call | tf_op jit(solution)/shard_map/pallas_call | solution.py:615
  105.1 80.2 %shard_map.239 = (f32[2048,128]{1,0:T(8,128)}, f32[6272,128]{1,0:T(8,128)}, f32[2,32,64]{2,1,0:T(8,128)}, f32[2,608,128]{2,1,0:T(8,128)}, f32[2,80,128]{2,1,0:T(8,128)}) custom-call(s32[64]{0:T(128)} %emb_ref.5, s32[64]{0:T(128)} %get-tuple-element.56.before_ref, s32[32]{0:T(128)} %get-tuple-element.57.last_ref, s32[1,64]{1,0:T(1,128)} %bitcast.33, ...), custom_call_target="tpu_custom_call" | custom-call | tf_op jit(solution)/shard_map/pallas_call | solution.py:1104
  185.4 0.0 copy-start
  185.4 5.2 %shard_map.240 = (f32[2048,128]{1,0:T(8,128)}, f32[6272,128]{1,0:T(8,128)}, f32[2,16,128]{2,1,0:T(8,128)}, f32[2,16,128]{2,1,0:T(8,128)}, f32[2,16,128]{2,1,0:T(...) custom-call(f32[2,608,128]{2,1,0:T(8,128)} %get-tuple-element.77.mat, ...), custom_call_target="tpu_custom_call" | custom-call | tf_op jit(solution)/shard_map/pallas_call | solution.py:1155
  190.6 0.0 copy-done
  190.7 0.6 copy.28
Async XLA Ops:
  185.4 5.3 %copy-start = (f32[2,32,64]{2,1,0:T(8,128)S(1)}, f32[2,32,64]{2,1,0:T(8,128)}, u32[]{:S(2)}) copy-start(f32[2,32,64]{2,1,0:T(8,128)} %get-tuple-element.83) | copy-start | bytes 49156

commit v6 on v5

--- a/solution.py
+++ b/solution.py
@@ -781,13 +781,14 @@
 
 BOUNDS = (0, 160, 320, 480, ROWS)
 HALVES = (0, 320, ROWS)
-GATHER_GROUPS = chunks_of(0, BOUNDS) + chunks_of(1, HALVES)
+THIRDS = (0, 256, 448, ROWS)
+GATHER_GROUPS = chunks_of(0, BOUNDS) + chunks_of(1, THIRDS)
 GATHER_FIRST = (
     (0, 0), (1, 0), (0, 1), (2, 0), (1, 1), (0, 2), (3, 0), (2, 1), (1, 2), (0, 3), (4, 0), (3, 1), (2, 2),
-    (5, 0), (1, 3), (0, 4), (3, 2), (2, 3), (1, 4), (4, 1), (3, 3), (2, 4), (5, 1), (3, 4),
+    (5, 0), (1, 3), (0, 4), (3, 2), (2, 3), (1, 4), (6, 0), (4, 1), (3, 3), (2, 4), (5, 1), (3, 4),
 )
-GATHER_LATER = ((), ((4, 2),), (), ((5, 2),), (), (), ((4, 3),), ())
-GATHER_END = ((5, 3), (4, 4), (5, 4))
+GATHER_LATER = ((), ((4, 2), (6, 1)), (), ((5, 2),), ((6, 2),), ((4, 3),), (), ((5, 3),))
+GATHER_END = ((6, 3), (4, 4), (5, 4), (6, 4))
 
 
 def place_own(at, shards, outs, local_sem):
@@ -966,19 +967,20 @@
 
 SCATTER_GROUPS = (chunks_of(0, BOUNDS), chunks_of(1, HALVES))
 SCATTER_BESIDE = (
-    ((1, 0), (0, 0), (-1, 0)),
+    ((-1, 0), (0, 0), (1, 0)),
     ((-1, 1),),
-    ((0, 1), (-1, 2)),
-    ((1, 1), (-1, 3)),
+    ((-1, 2), (0, 1), (1, 1)),
+    ((-1, 3),),
     ((-1, 4),),
     ((0, 2),),
+    (),
     ((1, 2),),
-    (),
 )
+PROPRIO = None
 SCATTER_END = (
-    (0, 0, 0), (0, -1, 0), (1, 0, 3), (0, 1, 0), (0, 0, 1), (0, -1, 1), (0, 2, 0), (1, 1, 3), (0, 1, 1), (0, 0, 2),
-    (0, -1, 2), (0, 3, 0), (0, 2, 1), (1, 0, 4), (0, 1, 2), (1, 1, 4), (0, 0, 3), (0, -1, 3), (0, 3, 1), (0, 2, 2),
-    (0, 1, 3), (0, 0, 4), (0, -1, 4), (0, 3, 2), (0, 2, 3), (0, 1, 4), (0, 3, 3), (0, 2, 4), (0, 3, 4),
+    (0, 0, 0), (1, 0, 3), (0, 1, 0), (0, 0, 1), PROPRIO, (0, -1, 0), (0, 2, 0), (0, 1, 1), (0, -1, 1), (1, 1, 3),
+    (0, 0, 2), (0, 3, 0), (0, 2, 1), (0, -1, 2), (0, 1, 2), (0, 0, 3), (0, 3, 1), (0, 2, 2), (0, -1, 3), (1, 0, 4),
+    (0, 1, 3), (0, 0, 4), (0, 3, 2), (1, 1, 4), (0, 2, 3), (0, 1, 4), (0, 3, 3), (0, 2, 4), (0, -1, 4), (0, 3, 4),
 )
 
 
@@ -1064,19 +1066,22 @@
 
     @pl.when(step == pl.num_programs(0) - 1)
     def _():
-        *grads, bias, gprop = proprio_backward(
-            ids_ref, prop_ref, w_ref, act_ref[...], slope_ref[...], grows_ref[...]
-        )
-        for row, part in other_blocks(acc, grads):
-            row -= STEM_ROWS
-            others[:, row : row + part.shape[1], :] = part
-        first.sm[0, 0:16, :] = small_rows(acc)
-        first.sm[0, 16:SMALL, :] = bias
-        for layer, g, phase in SCATTER_END:
-            if phase == 0 and g >= 0:
+        for move in SCATTER_END:
+            if move is PROPRIO:
+                *grads, bias, gprop = proprio_backward(
+                    ids_ref, prop_ref, w_ref, act_ref[...], slope_ref[...], grows_ref[...]
+                )
+                for row, part in other_blocks(acc, grads):
+                    row -= STEM_ROWS
+                    others[:, row : row + part.shape[1], :] = part
+                first.sm[0, 0:16, :] = small_rows(acc)
+                first.sm[0, 16:SMALL, :] = bias
+                write_proprio(gprop + gprop1_ref[...], gprop_ref)
+                continue
+            layer, g, phase = move
+            if layer == 0 and phase == 0 and g >= 0:
                 gather_group(g)
             (first, second)[layer].run(((g, phase),))
-        write_proprio(gprop + gprop1_ref[...], gprop_ref)
         second.close()
         first.close()
 

time: 192 us -> 182 us (0.948)
  Pallas kernels: 190 us -> 180 us
    pallas_call x1, Pallas kernels: 80.2 us -> 69.9 us  [backward_scatter(): pl.pallas_call(backward_scatter_kernel, grid=(steps,), in_specs=[smem] *...]
where the time goes in v6:
time: 182 us
  Pallas kernels  180 us (99%)
    pallas_call x1, Pallas kernels, backward_scatter(): pl.pallas_call(backward_scatter_kernel, grid=(steps,), in_specs=[smem] *...  69.9 us
    pallas_call x1, Pallas kernels, gather_forward(): pl.pallas_call(gather_forward_kernel, grid=(steps,), in_specs=[smem] + [b...  65.3 us
    pallas_call x1, Pallas kernels, call(): pl.pallas_call(kernel, grid_spec=pltpu.PrefetchScalarGridSpec(num_scalar_...  39.7 us
    pallas_call x1, Pallas kernels, unpack(): pl.pallas_call(unpack_kernel, grid=(steps,), out_shape=[jax.ShapeDtypeStr...  5.25 us

profile of v6, /device:TPU:0, one launch (start us, length us, event | category | flops | bytes accessed | tf_op | source)
XLA Modules:
  0.0 181.5 jit_solution(12756735603935699999)
XLA Ops:
  0.6 65.3 %shard_map.237 = (f32[2048,128]{1,0:T(8,128)}, bf16[128,128]{1,0:T(8,128)(2,1)}, f32[128,128]{1,0:T(8,128)}, bf16[4,2,2,2,608,128]{5,4,3,2,1,0:T(8,128)(2,1)}, b...) custom-call(s32[64]{0:T(128)} %emb_ref.5, ...), custom_call_target="tpu_custom_call" | custom-call | tf_op jit(solution)/shard_map/pallas_call | solution.py:862
  66.0 39.7 %shard_map.238 = (bf16[2048,128]{1,0:T(8,128)(2,1)}, f32[2048,128]{1,0:T(8,128)}, bf16[64,112,128]{2,1,0:T(8,128)(2,1)}, f32[128,32]{1,0:T(8,128)}, bf16[32,608,...) custom-call(s32[64]{0:T(128)} %emb_ref.5, s32[1,64]{1,0:T(1,128)} %bitcast.32, ...), custom_call_target="tpu_custom_call" | custom-call | tf_op jit(solution)/shard_map/pallas_call | solution.py:615
  105.7 69.9 %shard_map.239 = (f32[2048,128]{1,0:T(8,128)}, f32[6272,128]{1,0:T(8,128)}, f32[2,32,64]{2,1,0:T(8,128)}, f32[2,608,128]{2,1,0:T(8,128)}, f32[2,80,128]{2,1,0:T(8,128)}) custom-call(s32[64]{0:T(128)} %emb_ref.5, s32[64]{0:T(128)} %get-tuple-element.56.before_ref, s32[32]{0:T(128)} %get-tuple-element.57.last_ref, s32[1,64]{1,0:T(1,128)} %bitcast.33, ...), custom_call_target="tpu_custom_call" | custom-call | tf_op jit(solution)/shard_map/pallas_call | solution.py:1109
  175.6 0.0 copy-start
  175.7 5.2 %shard_map.240 = (f32[2048,128]{1,0:T(8,128)}, f32[6272,128]{1,0:T(8,128)}, f32[2,16,128]{2,1,0:T(8,128)}, f32[2,16,128]{2,1,0:T(8,128)}, f32[2,16,128]{2,1,0:T(...) custom-call(f32[2,608,128]{2,1,0:T(8,128)} %get-tuple-element.77.mat, ...), custom_call_target="tpu_custom_call" | custom-call | tf_op jit(solution)/shard_map/pallas_call | solution.py:1160
  180.9 0.0 copy-done
  180.9 0.6 copy.28
Async XLA Ops:
  175.6 5.3 %copy-start = (f32[2,32,64]{2,1,0:T(8,128)S(1)}, f32[2,32,64]{2,1,0:T(8,128)}, u32[]{:S(2)}) copy-start(f32[2,32,64]{2,1,0:T(8,128)} %get-tuple-element.83) | copy-start | bytes 49156

commit v7 on v6

--- a/solution.py
+++ b/solution.py
@@ -781,11 +781,12 @@
 
 BOUNDS = (0, 160, 320, 480, ROWS)
 HALVES = (0, 320, ROWS)
+PROPRIO = None
 THIRDS = (0, 256, 448, ROWS)
-GATHER_GROUPS = chunks_of(0, BOUNDS) + chunks_of(1, THIRDS)
+GATHER_GROUPS = chunks_of(0, BOUNDS)[::-1] + chunks_of(1, THIRDS)
 GATHER_FIRST = (
     (0, 0), (1, 0), (0, 1), (2, 0), (1, 1), (0, 2), (3, 0), (2, 1), (1, 2), (0, 3), (4, 0), (3, 1), (2, 2),
-    (5, 0), (1, 3), (0, 4), (3, 2), (2, 3), (1, 4), (6, 0), (4, 1), (3, 3), (2, 4), (5, 1), (3, 4),
+    (5, 0), (1, 3), (0, 4), (3, 2), (2, 3), (1, 4), (6, 0), (4, 1), PROPRIO, (3, 3), (2, 4), (5, 1), (3, 4),
 )
 GATHER_LATER = ((), ((4, 2), (6, 1)), (), ((5, 2),), ((6, 2),), ((4, 3),), (), ((5, 3),))
 GATHER_END = ((6, 3), (4, 4), (5, 4), (6, 4))
@@ -825,9 +826,12 @@
         greet(at)
         for copy in local:
             copy.wait()
-        move.run(GATHER_FIRST)
+        for step_ in GATHER_FIRST:
+            if step_ is PROPRIO:
+                start_forward(0, ids_ref, prop_ref, w_ref, sb_ref, act_ref, slope_ref, rows_ref)
+            else:
+                move.run((step_,))
         keep.start()
-        start_forward(0, ids_ref, prop_ref, w_ref, sb_ref, act_ref, slope_ref, rows_ref)
 
     def moves_at(half):
         for i in range(len(GATHER_LATER) // 2):
@@ -976,7 +980,6 @@
     (),
     ((1, 2),),
 )
-PROPRIO = None
 SCATTER_END = (
     (0, 0, 0), (1, 0, 3), (0, 1, 0), (0, 0, 1), PROPRIO, (0, -1, 0), (0, 2, 0), (0, 1, 1), (0, -1, 1), (1, 1, 3),
     (0, 0, 2), (0, 3, 0), (0, 2, 1), (0, -1, 2), (0, 1, 2), (0, 0, 3), (0, 3, 1), (0, 2, 2), (0, -1, 3), (1, 0, 4),
@@ -1016,8 +1019,9 @@
         for name in ACC[1:]:
             acc[name][...] = jnp.zeros(acc[name].shape, F32)
         second.sm[0] = s1[...]
-        own.wait()
         second.run(SCATTER_BESIDE[0])
+
+    pl.when(step == 1)(own.wait)
 
     def moves_at(half):
         for i in range(len(SCATTER_BESIDE) // 2):
@@ -1155,7 +1159,7 @@
         (LAYERS, 16, D), (LAYERS, 16, D), (LAYERS, 16, D), (LAYERS, D, 4 * D), (LAYERS, SQ, D),
         (LAYERS, PROP, D), (LAYERS, 8, D), (LAYERS, FF), (LAYERS, 2 * STEMS, D),
     ]
-    steps = 4
+    steps = 2
     moved_through = [blocked(a.shape, a.shape[0] // steps) for a in (gtok, gfeat)]
     return pl.pallas_call(
         unpack_kernel,
@@ -1163,6 +1167,9 @@
         out_shape=[jax.ShapeDtypeStruct(s, F32) for s in [gtok.shape, gfeat.shape] + outs],
         in_specs=[whole(mats.shape), whole(small.shape)] + moved_through,
         out_specs=moved_through + [whole(s) for s in outs],
+        compiler_params=pltpu.CompilerParams(
+            dimension_semantics=("arbitrary",), vmem_limit_bytes=VMEM_LIMIT
+        ),
     )(mats, small, gtok, gfeat)
 
 

time: 182 us -> 180 us (0.989)
  Pallas kernels: 180 us -> 178 us
where the time goes in v7:
time: 180 us
  Pallas kernels  178 us (99%)
    pallas_call x1, Pallas kernels, backward_scatter(): pl.pallas_call(backward_scatter_kernel, grid=(steps,), in_specs=[smem] *...  70.2 us
    pallas_call x1, Pallas kernels, gather_forward(): pl.pallas_call(gather_forward_kernel, grid=(steps,), in_specs=[smem] + [b...  64.2 us
    pallas_call x1, Pallas kernels, call(): pl.pallas_call(kernel, grid_spec=pltpu.PrefetchScalarGridSpec(num_scalar_...  39.7 us
    pallas_call x1, Pallas kernels, unpack(): pl.pallas_call(unpack_kernel, grid=(steps,), out_shape=[jax.ShapeDtypeStr...  4.22 us

profile of v7, /device:TPU:0, one launch (start us, length us, event | category | flops | bytes accessed | tf_op | source)
XLA Modules:
  0.0 179.7 jit_solution(6146698087636597277)
XLA Ops:
  0.6 64.2 %shard_map.237 = (f32[2048,128]{1,0:T(8,128)}, bf16[128,128]{1,0:T(8,128)(2,1)}, f32[128,128]{1,0:T(8,128)}, bf16[4,2,2,2,608,128]{5,4,3,2,1,0:T(8,128)(2,1)}, b...) custom-call(s32[64]{0:T(128)} %emb_ref.5, ...), custom_call_target="tpu_custom_call" | custom-call | tf_op jit(solution)/shard_map/pallas_call | solution.py:866
  64.9 39.7 %shard_map.238 = (bf16[2048,128]{1,0:T(8,128)(2,1)}, f32[2048,128]{1,0:T(8,128)}, bf16[64,112,128]{2,1,0:T(8,128)(2,1)}, f32[128,32]{1,0:T(8,128)}, bf16[32,608,...) custom-call(s32[64]{0:T(128)} %emb_ref.5, s32[1,64]{1,0:T(1,128)} %bitcast.32, ...), custom_call_target="tpu_custom_call" | custom-call | tf_op jit(solution)/shard_map/pallas_call | solution.py:615
  104.6 70.2 %shard_map.239 = (f32[2048,128]{1,0:T(8,128)}, f32[6272,128]{1,0:T(8,128)}, f32[2,32,64]{2,1,0:T(8,128)}, f32[2,608,128]{2,1,0:T(8,128)}, f32[2,80,128]{2,1,0:T(8,128)}) custom-call(s32[64]{0:T(128)} %emb_ref.5, s32[64]{0:T(128)} %get-tuple-element.56.before_ref, s32[32]{0:T(128)} %get-tuple-element.57.last_ref, s32[1,64]{1,0:T(1,128)} %bitcast.33, ...), custom_call_target="tpu_custom_call" | custom-call | tf_op jit(solution)/shard_map/pallas_call | solution.py:1113
  174.8 0.0 copy-start
  174.8 4.2 %shard_map.240 = (f32[2048,128]{1,0:T(8,128)}, f32[6272,128]{1,0:T(8,128)}, f32[2,16,128]{2,1,0:T(8,128)}, f32[2,16,128]{2,1,0:T(8,128)}, f32[2,16,128]{2,1,0:T(...) custom-call(f32[2,608,128]{2,1,0:T(8,128)} %get-tuple-element.77.mat, ...), custom_call_target="tpu_custom_call" | custom-call | tf_op jit(solution)/shard_map/pallas_call | solution.py:1164
  179.1 0.0 copy-done
  179.1 0.6 copy.28
Async XLA Ops:
  174.8 4.2 %copy-start = (f32[2,32,64]{2,1,0:T(8,128)S(1)}, f32[2,32,64]{2,1,0:T(8,128)}, u32[]{:S(2)}) copy-start(f32[2,32,64]{2,1,0:T(8,128)} %get-tuple-element.83) | copy-start | bytes 49156

commit v8 on v7

--- a/solution.py
+++ b/solution.py
@@ -783,7 +783,7 @@
 HALVES = (0, 320, ROWS)
 PROPRIO = None
 THIRDS = (0, 256, 448, ROWS)
-GATHER_GROUPS = chunks_of(0, BOUNDS)[::-1] + chunks_of(1, THIRDS)
+GATHER_GROUPS = chunks_of(0, (0, 160, 352, 512, ROWS))[::-1] + chunks_of(1, THIRDS)
 GATHER_FIRST = (
     (0, 0), (1, 0), (0, 1), (2, 0), (1, 1), (0, 2), (3, 0), (2, 1), (1, 2), (0, 3), (4, 0), (3, 1), (2, 2),
     (5, 0), (1, 3), (0, 4), (3, 2), (2, 3), (1, 4), (6, 0), (4, 1), PROPRIO, (3, 3), (2, 4), (5, 1), (3, 4),

time: 180 us -> 181 us (level)
  no operation moved by 1% of the time
where the time goes in v8:
time: 181 us
  Pallas kernels  179 us (99%)
    pallas_call x1, Pallas kernels, backward_scatter(): pl.pallas_call(backward_scatter_kernel, grid=(steps,), in_specs=[smem] *...  71.7 us
    pallas_call x1, Pallas kernels, gather_forward(): pl.pallas_call(gather_forward_kernel, grid=(steps,), in_specs=[smem] + [b...  63.8 us
    pallas_call x1, Pallas kernels, call(): pl.pallas_call(kernel, grid_spec=pltpu.PrefetchScalarGridSpec(num_scalar_...  39.6 us
    pallas_call x1, Pallas kernels, unpack(): pl.pallas_call(unpack_kernel, grid=(steps,), out_shape=[jax.ShapeDtypeStr...  4.22 us

profile of v8, /device:TPU:0, one launch (start us, length us, event | category | flops | bytes accessed | tf_op | source)
XLA Modules:
  0.0 180.6 jit_solution(11652717942181037913)
XLA Ops:
  0.6 63.8 %shard_map.237 = (f32[2048,128]{1,0:T(8,128)}, bf16[128,128]{1,0:T(8,128)(2,1)}, f32[128,128]{1,0:T(8,128)}, bf16[4,2,2,2,608,128]{5,4,3,2,1,0:T(8,128)(2,1)}, b...) custom-call(s32[64]{0:T(128)} %emb_ref.5, ...), custom_call_target="tpu_custom_call" | custom-call | tf_op jit(solution)/shard_map/pallas_call | solution.py:866
  64.4 39.6 %shard_map.238 = (bf16[2048,128]{1,0:T(8,128)(2,1)}, f32[2048,128]{1,0:T(8,128)}, bf16[64,112,128]{2,1,0:T(8,128)(2,1)}, f32[128,32]{1,0:T(8,128)}, bf16[32,608,...) custom-call(s32[64]{0:T(128)} %emb_ref.5, s32[1,64]{1,0:T(1,128)} %bitcast.32, ...), custom_call_target="tpu_custom_call" | custom-call | tf_op jit(solution)/shard_map/pallas_call | solution.py:615
  104.0 71.7 %shard_map.239 = (f32[2048,128]{1,0:T(8,128)}, f32[6272,128]{1,0:T(8,128)}, f32[2,32,64]{2,1,0:T(8,128)}, f32[2,608,128]{2,1,0:T(8,128)}, f32[2,80,128]{2,1,0:T(8,128)}) custom-call(s32[64]{0:T(128)} %emb_ref.5, s32[64]{0:T(128)} %get-tuple-element.56.before_ref, s32[32]{0:T(128)} %get-tuple-element.57.last_ref, s32[1,64]{1,0:T(1,128)} %bitcast.33, ...), custom_call_target="tpu_custom_call" | custom-call | tf_op jit(solution)/shard_map/pallas_call | solution.py:1113
  175.7 0.0 copy-start
  175.7 4.2 %shard_map.240 = (f32[2048,128]{1,0:T(8,128)}, f32[6272,128]{1,0:T(8,128)}, f32[2,16,128]{2,1,0:T(8,128)}, f32[2,16,128]{2,1,0:T(8,128)}, f32[2,16,128]{2,1,0:T(...) custom-call(f32[2,608,128]{2,1,0:T(8,128)} %get-tuple-element.77.mat, ...), custom_call_target="tpu_custom_call" | custom-call | tf_op jit(solution)/shard_map/pallas_call | solution.py:1164
  179.9 0.0 copy-done
  179.9 0.6 copy.28
Async XLA Ops:
  175.7 4.2 %copy-start = (f32[2,32,64]{2,1,0:T(8,128)S(1)}, f32[2,32,64]{2,1,0:T(8,128)}, u32[]{:S(2)}) copy-start(f32[2,32,64]{2,1,0:T(8,128)} %get-tuple-element.83) | copy-start | bytes 49156
